TPU v7x, 32 devices: a whole 2x2x4 slice. The times are simulated.
32 devices in a mesh: fsdp: 4 (over z), seq: 8 (over y, x, core).
Axes of the slice: x: 2, y: 2, z: 4, core: 2. Of those that a mesh axis runs over, the one named last changes fastest.
Arguments:
- tokens: bfloat16 [4096, 2048], P(('fsdp', 'seq')), may hold values from -6 to 6
- segments: int32 [4096], P(('fsdp', 'seq')), may hold values from 0 to 2, as said below
- routes: int32 [4096, 8], P(('fsdp', 'seq')), may hold values from 0 to 15, all different within a row; in each aligned block of 128 rows (0 to 127, 128 to 255, ...) at most 96 rows name the same one
- out_grad: bfloat16 [4096, 2048], P(('fsdp', 'seq')), may hold values from -6 to 6
- w_query: float32 [2048, 2048], P(('fsdp', 'seq')), may hold values from -0.125 to 0.125
- w_key: float32 [2048, 2048], P(('fsdp', 'seq')), may hold values from -0.125 to 0.125
- w_value: float32 [2048, 2048], P(('fsdp', 'seq')), may hold values from -0.125 to 0.125
- w_out: float32 [2048, 2048], P(('fsdp', 'seq')), may hold values from -3 to 3
- router: float32 [2048, 16], P(('fsdp', 'seq')), may hold values from -0.0625 to 0.0625
- attn_gain: float32 [2048], P(('fsdp', 'seq')), may hold values from 0.25 to 1.75
- q_gain: float32 [2048], P(('fsdp', 'seq')), may hold values from 0.25 to 1.75
- k_gain: float32 [2048], P(('fsdp', 'seq')), may hold values from 0.25 to 1.75
- ffn_gain: float32 [2048], P(('fsdp', 'seq')), may hold values from 0.25 to 1.75
- expert_gate_up: float32 [32, 2048, 2, 512], P(('fsdp', 'seq')), may hold values from -0.125 to 0.125
- expert_down: float32 [32, 512, 2048], P(('fsdp', 'seq')), may hold values from -6 to 6
Outputs:
- output: bfloat16 [4096, 2048], P(('fsdp', 'seq'))
- input_grad: bfloat16 [4096, 2048], P(('fsdp', 'seq'))
- w_query_grad: float32 [2048, 2048], P(('fsdp', 'seq'))
- w_key_grad: float32 [2048, 2048], P(('fsdp', 'seq'))
- w_value_grad: float32 [2048, 2048], P(('fsdp', 'seq'))
- w_out_grad: float32 [2048, 2048], P(('fsdp', 'seq'))
- router_grad: float32 [2048, 16], P(('fsdp', 'seq'))
- attn_gain_grad: float32 [2048], P(('fsdp', 'seq'))
- q_gain_grad: float32 [2048], P(('fsdp', 'seq'))
- k_gain_grad: float32 [2048], P(('fsdp', 'seq'))
- ffn_gain_grad: float32 [2048], P(('fsdp', 'seq'))
- expert_gate_up_grad: float32 [32, 2048, 2, 512], P(('fsdp', 'seq'))
- expert_down_grad: float32 [32, 512, 2048], P(('fsdp', 'seq'))
Inputs may be any that keep to these rules, and one draw needn't show every extreme that they name: `segments`: segment numbers restart in each sequence of 1024 tokens: three documents 0, 1, 2 in order, the first and the last each 1 to 64 tokens long. `routes`: each row names 8 different experts. Within the 128 rows of one device no expert is named by more than 96 rows, and in some device one is named by exactly 96.
All inputs are finite; a program needn't handle non-finite values.
Results may differ from a plain program's by a relative error of at most 0.02.
The roundings to bfloat16 on the way count: a program that leaves them out, or rounds other values in their place, can miss the bound.
Values may be sent and summed in bfloat16 or wider, within the bound.
No kernel may reach another device: no remote copies, remote signals or barrier semaphores. Data moves between devices by JAX's collectives and lax.ppermute only.
A program may use at most 448 MiB of HBM per device.

v0:
```python
import jax
import jax.numpy as jnp
from jax import lax
from jax.sharding import PartitionSpec as P

HEADS = 16
SPLIT = 2


EPSILON = 1e-05
THETA = 10000.0


def rms_scale(values, gain):
    inverse = lax.rsqrt(jnp.mean(values * values, axis=-1, keepdims=True) + EPSILON)
    return values * inverse * gain


def rotate(values, positions, head_count):
    row_count = values.shape[0]
    head_width = values.shape[1] // head_count
    half_width = head_width // 2
    frequency = THETA ** (-jnp.arange(half_width, dtype=jnp.float32) * 2.0 / head_width)
    angles = positions.astype(jnp.float32)[:, None] * frequency[None, :]
    cosine_table = jnp.cos(angles)[:, None, :]
    sine_table = jnp.sin(angles)[:, None, :]
    shaped = values.reshape(row_count, head_count, head_width)
    first_half = shaped[..., :half_width]
    second_half = shaped[..., half_width:]
    turned = jnp.concatenate(
        [
            first_half * cosine_table - second_half * sine_table,
            second_half * cosine_table + first_half * sine_table,
        ],
        axis=-1,
    )
    return turned.reshape(row_count, head_count * head_width)


def softmax_rows(values):
    return jax.nn.softmax(values, axis=-1)


def contract_rows(left, right):
    return lax.dot_general(
        left, right, (((0,), (0,)), ((), ())), preferred_element_type=jnp.float32
    )


def times_transposed(left, right):
    return lax.dot_general(
        left, right, (((1,), (1,)), ((), ())), preferred_element_type=jnp.float32
    )


def gather_dense(w_query, w_key, w_value, w_out, router, attn_gain, q_gain, k_gain, ffn_gain):
    return (
        lax.all_gather(w_query.astype(jnp.bfloat16), ("fsdp", "seq"), axis=0, tiled=True),
        lax.all_gather(w_key.astype(jnp.bfloat16), ("fsdp", "seq"), axis=0, tiled=True),
        lax.all_gather(w_value.astype(jnp.bfloat16), ("fsdp", "seq"), axis=0, tiled=True),
        lax.all_gather(w_out.astype(jnp.bfloat16), ("fsdp", "seq"), axis=0, tiled=True),
        lax.all_gather(router.astype(jnp.bfloat16), ("fsdp", "seq"), axis=0, tiled=True),
        lax.all_gather(attn_gain.astype(jnp.bfloat16), ("fsdp", "seq"), axis=0, tiled=True),
        lax.all_gather(q_gain.astype(jnp.bfloat16), ("fsdp", "seq"), axis=0, tiled=True),
        lax.all_gather(k_gain.astype(jnp.bfloat16), ("fsdp", "seq"), axis=0, tiled=True),
        lax.all_gather(ffn_gain.astype(jnp.bfloat16), ("fsdp", "seq"), axis=0, tiled=True),
    )


def slot_table(routes, expert_count):
    expert_ids = routes.reshape(-1)
    onehot = (expert_ids[:, None] == jnp.arange(expert_count, dtype=jnp.int32)[None, :]).astype(
        jnp.int32
    )
    slot_ids = jnp.sum((jnp.cumsum(onehot, axis=0) - 1) * onehot, axis=1)
    return (expert_ids, slot_ids)


def pack_rows(rows_in, expert_ids, slot_ids, expert_count, capacity):
    model_width = rows_in.shape[1]
    buffer = (
        jnp.zeros((expert_count, capacity, model_width), rows_in.dtype)
        .at[expert_ids, slot_ids]
        .set(rows_in)
    )
    doubled = jnp.broadcast_to(buffer[:, None], (expert_count, SPLIT, capacity, model_width))
    return doubled.reshape(expert_count * SPLIT, capacity, model_width)


def send_out(buffer):
    return lax.all_to_all(buffer, ("fsdp", "seq"), split_axis=0, concat_axis=0, tiled=True)


def sum_parts(returned, expert_ids, slot_ids, expert_count, capacity):
    model_width = returned.shape[-1]
    table = returned.reshape(expert_count, SPLIT, capacity, model_width)
    picked = table[expert_ids, :, slot_ids].astype(jnp.float32)
    return jnp.sum(picked, axis=1)


def per_device(
    tokens,
    segments,
    routes,
    out_grad,
    w_query,
    w_key,
    w_value,
    w_out,
    router,
    attn_gain,
    q_gain,
    k_gain,
    ffn_gain,
    expert_gate_up,
    expert_down,
):
    devices = lax.axis_size(("fsdp", "seq"))
    expert_count = devices // SPLIT
    tok_rows = tokens.shape[0]
    top_count = routes.shape[1]
    model_width = tokens.shape[1]
    head_width = model_width // HEADS
    capacity = max(2, 3 * tok_rows * top_count // (2 * expert_count))
    score_scale = head_width ** (-0.5)
    gathered = gather_dense(
        w_query, w_key, w_value, w_out, router, attn_gain, q_gain, k_gain, ffn_gain
    )
    attn_scale = gathered[5].astype(jnp.float32)
    query_scale = gathered[6].astype(jnp.float32)
    key_scale = gathered[7].astype(jnp.float32)
    ffn_scale = gathered[8].astype(jnp.float32)
    inputs = tokens.astype(jnp.float32)
    normed, attn_back = jax.vjp(rms_scale, inputs, attn_scale)
    normed_low = normed.astype(jnp.bfloat16)
    query_proj = jnp.dot(normed_low, gathered[0], preferred_element_type=jnp.float32)
    key_proj = jnp.dot(normed_low, gathered[1], preferred_element_type=jnp.float32)
    value_low = jnp.dot(normed_low, gathered[2], preferred_element_type=jnp.float32).astype(
        jnp.bfloat16
    )
    positions = lax.axis_index("seq") * tok_rows + jnp.arange(tok_rows, dtype=jnp.int32)

    def norm_rotate(projected, gain):
        return rotate(rms_scale(projected, gain), positions, HEADS)

    query_rot, query_back = jax.vjp(norm_rotate, query_proj, query_scale)
    key_rot, key_back = jax.vjp(norm_rotate, key_proj, key_scale)
    query_low = query_rot.astype(jnp.bfloat16)
    key_low = key_rot.astype(jnp.bfloat16)
    segment_low = segments.astype(jnp.bfloat16)
    key_all, value_all, segment_all = (
        lax.all_gather(key_low, "seq", axis=0, tiled=True),
        lax.all_gather(value_low, "seq", axis=0, tiled=True),
        lax.all_gather(segment_low, "seq", axis=0, tiled=True),
    )
    seq_len = key_all.shape[0]
    query_heads = query_low.reshape(tok_rows, HEADS, head_width)
    key_heads = key_all.reshape(seq_len, HEADS, head_width)
    value_heads = value_all.reshape(seq_len, HEADS, head_width)
    key_places = jnp.arange(seq_len, dtype=jnp.int32)
    allowed = (key_places[None, :] <= positions[:, None]) & (
        segment_all.astype(jnp.float32)[None, :] == segments.astype(jnp.float32)[:, None]
    )
    allowed = allowed[None]

    def raw_scores():
        product = jnp.einsum(
            "thd,khd->htk", query_heads, key_heads, preferred_element_type=jnp.float32
        )
        return jnp.where(allowed, product * score_scale, -1e30)

    masked = raw_scores()
    row_max = jnp.max(masked, axis=-1, keepdims=True)
    exp_terms = jnp.where(allowed, jnp.exp(masked - row_max), 0.0)
    row_total = jnp.sum(exp_terms, axis=-1, keepdims=True)
    attn_probs = exp_terms / row_total
    log_total = row_max + jnp.log(row_total)
    attended = jnp.einsum(
        "htk,khd->thd",
        attn_probs.astype(jnp.bfloat16),
        value_heads,
        preferred_element_type=jnp.float32,
    )
    attended_low = attended.reshape(tok_rows, model_width).astype(jnp.bfloat16)
    middle = inputs + jnp.dot(attended_low, gathered[3], preferred_element_type=jnp.float32)
    mixed, ffn_back = jax.vjp(rms_scale, middle, ffn_scale)
    mixed_low = mixed.astype(jnp.bfloat16)
    logits = jnp.dot(mixed_low, gathered[4], preferred_element_type=jnp.float32)
    expert_probs, soft_back = jax.vjp(softmax_rows, logits)
    gates = jnp.take_along_axis(expert_probs, routes, axis=1)
    expert_ids, slot_ids = slot_table(routes, expert_count)
    repeated = jnp.repeat(mixed_low, top_count, axis=0)
    received = send_out(pack_rows(repeated, expert_ids, slot_ids, expert_count, capacity)).reshape(
        devices * capacity, model_width
    )
    gate_up_low = expert_gate_up[0].astype(jnp.bfloat16)
    down_low = expert_down[0].astype(jnp.bfloat16)
    gate_up = jnp.einsum("rd,dkf->rkf", received, gate_up_low, preferred_element_type=jnp.float32)
    gate_part = gate_up[:, 0]
    up_part = gate_up[:, 1]
    hidden = (jax.nn.silu(gate_part) * up_part).astype(jnp.bfloat16)
    result = jnp.dot(hidden, down_low, preferred_element_type=jnp.float32).astype(jnp.bfloat16)
    returned = lax.all_to_all(
        result.reshape(devices, capacity, model_width),
        ("fsdp", "seq"),
        split_axis=0,
        concat_axis=0,
        tiled=True,
    )
    expert_out = sum_parts(returned, expert_ids, slot_ids, expert_count, capacity).reshape(
        tok_rows, top_count, model_width
    )
    mixture = jnp.sum(gates[:, :, None] * expert_out, axis=1)
    output = (middle + mixture).astype(jnp.bfloat16)
    reused = gather_dense(
        w_query, w_key, w_value, w_out, router, attn_gain, q_gain, k_gain, ffn_gain
    )
    grad_output = out_grad.astype(jnp.float32)
    grad_gates = jnp.sum(expert_out * grad_output[:, None, :], axis=-1)
    grad_rows = (
        (gates[:, :, None] * grad_output[:, None, :])
        .astype(jnp.bfloat16)
        .reshape(tok_rows * top_count, model_width)
    )
    grad_received = send_out(
        pack_rows(grad_rows, expert_ids, slot_ids, expert_count, capacity)
    ).reshape(devices * capacity, model_width)
    grad_hidden = times_transposed(grad_received, down_low)
    sigmoid_gate = jax.nn.sigmoid(gate_part)
    grad_gate_part = (
        grad_hidden * up_part * (sigmoid_gate * (1.0 + gate_part * (1.0 - sigmoid_gate)))
    )
    grad_up_part = grad_hidden * jax.nn.silu(gate_part)
    grad_gate_up = jnp.stack([grad_gate_part, grad_up_part], axis=1).astype(jnp.bfloat16)
    expert_down_grad = contract_rows(hidden, grad_received)[None]
    expert_gate_up_grad = jnp.einsum(
        "rd,rkf->dkf", received, grad_gate_up, preferred_element_type=jnp.float32
    )[None]
    grad_sent = jnp.einsum(
        "rkf,dkf->rd", grad_gate_up, gate_up_low, preferred_element_type=jnp.float32
    )
    grad_returned = lax.all_to_all(
        grad_sent.reshape(devices, capacity, model_width).astype(jnp.bfloat16),
        ("fsdp", "seq"),
        split_axis=0,
        concat_axis=0,
        tiled=True,
    ).astype(jnp.float32)
    grad_mixed = jnp.sum(
        sum_parts(grad_returned, expert_ids, slot_ids, expert_count, capacity).reshape(
            tok_rows, top_count, model_width
        ),
        axis=1,
    )
    chosen = (
        routes[:, :, None] == jnp.arange(expert_count, dtype=jnp.int32)[None, None, :]
    ).astype(jnp.float32)
    grad_probs = jnp.sum(grad_gates[:, :, None] * chosen, axis=1)
    grad_logits = soft_back(grad_probs)[0].astype(jnp.bfloat16)
    router_part = contract_rows(mixed_low, grad_logits)
    grad_mixed = grad_mixed + times_transposed(grad_logits, reused[4])
    grad_middle, ffn_part = ffn_back(grad_mixed)
    grad_middle = grad_middle + grad_output
    grad_proj = grad_middle.astype(jnp.bfloat16)
    out_part = contract_rows(attended_low, grad_proj)
    grad_attended = times_transposed(grad_proj, reused[3]).astype(jnp.bfloat16)
    grad_heads = grad_attended.reshape(tok_rows, HEADS, head_width)
    again_masked = raw_scores()
    again_probs = jnp.where(allowed, jnp.exp(again_masked - log_total), 0.0)
    grad_probs_attn = jnp.einsum(
        "thd,khd->htk", grad_heads, value_heads, preferred_element_type=jnp.float32
    )
    row_delta = jnp.sum(again_probs * grad_probs_attn, axis=-1, keepdims=True)
    grad_scores = (again_probs * (grad_probs_attn - row_delta)).astype(jnp.bfloat16)
    grad_query = (
        jnp.einsum(
            "htk,khd->thd", grad_scores, key_heads, preferred_element_type=jnp.float32
        ).reshape(tok_rows, model_width)
        * score_scale
    )
    again_low = again_probs.astype(jnp.bfloat16)
    grad_key_all = (
        jnp.einsum(
            "htk,thd->khd", grad_scores, query_heads, preferred_element_type=jnp.float32
        ).reshape(seq_len, model_width)
        * score_scale
    )
    grad_value_all = jnp.einsum(
        "htk,thd->khd", again_low, grad_heads, preferred_element_type=jnp.float32
    ).reshape(seq_len, model_width)
    grad_key, grad_value = (
        lax.psum_scatter(
            grad_key_all.astype(jnp.bfloat16), "seq", scatter_dimension=0, tiled=True
        ).astype(jnp.float32),
        lax.psum_scatter(
            grad_value_all.astype(jnp.bfloat16), "seq", scatter_dimension=0, tiled=True
        ).astype(jnp.float32),
    )
    grad_query_proj, query_part = query_back(grad_query)
    grad_key_proj, key_part = key_back(grad_key)
    query_grad_low = grad_query_proj.astype(jnp.bfloat16)
    key_grad_low = grad_key_proj.astype(jnp.bfloat16)
    value_grad_low = grad_value.astype(jnp.bfloat16)
    query_weight_part = contract_rows(normed_low, query_grad_low)
    key_weight_part = contract_rows(normed_low, key_grad_low)
    value_weight_part = contract_rows(normed_low, value_grad_low)
    grad_normed = (
        times_transposed(query_grad_low, reused[0])
        + times_transposed(key_grad_low, reused[1])
        + times_transposed(value_grad_low, reused[2])
    )
    grad_inputs, attn_part = attn_back(grad_normed)
    input_grad = (grad_inputs + grad_middle).astype(jnp.bfloat16)
    reduced = (
        lax.psum_scatter(query_weight_part, ("fsdp", "seq"), scatter_dimension=0, tiled=True),
        lax.psum_scatter(key_weight_part, ("fsdp", "seq"), scatter_dimension=0, tiled=True),
        lax.psum_scatter(value_weight_part, ("fsdp", "seq"), scatter_dimension=0, tiled=True),
        lax.psum_scatter(out_part, ("fsdp", "seq"), scatter_dimension=0, tiled=True),
        lax.psum_scatter(router_part, ("fsdp", "seq"), scatter_dimension=0, tiled=True),
        lax.psum_scatter(attn_part, ("fsdp", "seq"), scatter_dimension=0, tiled=True),
        lax.psum_scatter(query_part, ("fsdp", "seq"), scatter_dimension=0, tiled=True),
        lax.psum_scatter(key_part, ("fsdp", "seq"), scatter_dimension=0, tiled=True),
        lax.psum_scatter(ffn_part, ("fsdp", "seq"), scatter_dimension=0, tiled=True),
    )
    return (
        output,
        input_grad,
        reduced[0],
        reduced[1],
        reduced[2],
        reduced[3],
        reduced[4],
        reduced[5],
        reduced[6],
        reduced[7],
        reduced[8],
        expert_gate_up_grad,
        expert_down_grad,
    )


def solution(mesh):
    return jax.shard_map(
        per_device,
        mesh=mesh,
        in_specs=(
            P(("fsdp", "seq"), None),
            P(("fsdp", "seq")),
            P(("fsdp", "seq"), None),
            P(("fsdp", "seq"), None),
            P(("fsdp", "seq"), None),
            P(("fsdp", "seq"), None),
            P(("fsdp", "seq"), None),
            P(("fsdp", "seq"), None),
            P(("fsdp", "seq"), None),
            P(("fsdp", "seq")),
            P(("fsdp", "seq")),
            P(("fsdp", "seq")),
            P(("fsdp", "seq")),
            P(("fsdp", "seq"), None, None, None),
            P(("fsdp", "seq"), None, None),
        ),
        out_specs=(
            P(("fsdp", "seq"), None),
            P(("fsdp", "seq"), None),
            P(("fsdp", "seq"), None),
            P(("fsdp", "seq"), None),
            P(("fsdp", "seq"), None),
            P(("fsdp", "seq"), None),
            P(("fsdp", "seq"), None),
            P(("fsdp", "seq")),
            P(("fsdp", "seq")),
            P(("fsdp", "seq")),
            P(("fsdp", "seq")),
            P(("fsdp", "seq"), None, None, None),
            P(("fsdp", "seq"), None, None),
        ),
        check_vma=False,
    )
```

profile of v0, /device:TPU:0, one launch (start us, length us, event | category | flops | bytes accessed | tf_op | source)
XLA Modules:
  0.0 2726.1 jit_solution(9082213106107599529)
XLA Ops:
  16.3 42.6 %all-reduce.13 = (bf16[2048]{0:T(1024)(128)(2,1)S(1)}, bf16[2048]{0:T(1024)(128)(2,1)S(1)}, bf16[2048]{0:T(1024)(128)(2,1)S(1)}, bf16[2048]{0:T(1024)(128)(2,1)S(1)}) all-reduce(bf16[2048]{0:T(1024)(128)(2,1)S(1)} %dynamic-update-slice, bf16[2048]{0:T(1024)(128)(2,1)S(1)} %dynamic-update-slice.2, ...), channel_id=1, replica_groups=mesh['fsdp'=4,'seq'=8] {'fsdp','seq'}, use_global_device_ids=true, to_apply=%add.4 | all-reduce | flops 8192 | bytes 32768
  61.0 30.7 %all-gather.15.cloned.1.call-done = bf16[2048,2048]{1,0:T(8,128)(2,1)} async-done(((bf16[64,2048]{1,0:T(8,128)(2,1)}), bf16[2048,2048]{1,0:T(8,128)(2,1)}) %all-gather.15.cloned.1.call-update) | async-done | bytes 8388624 | tf_op jit(solution)/shard_map/all_gather | solution.py:59
  98.0 73.2 %all-gather.13.cloned.1.call-done = bf16[2048,2048]{1,0:T(8,128)(2,1)} async-done(((bf16[64,2048]{1,0:T(8,128)(2,1)}), bf16[2048,2048]{1,0:T(8,128)(2,1)}) %all-gather.13.cloned.1.call-update) | async-done | bytes 8388624 | tf_op jit(solution)/shard_map/all_gather | solution.py:58
  180.9 69.8 %all-gather.9.cloned.1.call-done = bf16[2048,2048]{1,0:T(8,128)(2,1)} async-done(((bf16[64,2048]{1,0:T(8,128)(2,1)}), bf16[2048,2048]{1,0:T(8,128)(2,1)}) %all-gather.9.cloned.1.call-update) | async-done | bytes 8388624 | tf_op jit(solution)/shard_map/all_gather | solution.py:60
  272.4 16.7 all-gather.17.cloned.1.call-done
  299.7 28.5 %all-gather.11.cloned.1.call-done = bf16[1024,2048]{1,0:T(8,128)(2,1)} async-done(((bf16[128,2048]{1,0:T(8,128)(2,1)}), bf16[1024,2048]{1,0:T(8,128)(2,1)}) %all-gather.11.cloned.1.call-update) | async-done | bytes 4194320 | tf_op jit(solution)/shard_map/all_gather | solution.py:153
  336.4 72.6 %all-gather.19.cloned.1.call-done = bf16[2048,2048]{1,0:T(8,128)(2,1)} async-done(((bf16[64,2048]{1,0:T(8,128)(2,1)}), bf16[2048,2048]{1,0:T(8,128)(2,1)}) %all-gather.19.cloned.1.call-update) | async-done | bytes 8388624 | tf_op jit(solution)/shard_map/all_gather | solution.py:61
  438.2 242.0 %all-gather.1 = bf16[32,64,16]{1,2,0:T(8,128)(2,1)S(1)} all-gather(bf16[1,64,16]{1,2,0:T(8,128)(2,1)S(1)} %convert_bitcast_fusion.2), channel_id=1, replica_groups=mesh['fsdp'=4,'seq'=8] {'fsdp','seq'}, dimensions={0}, use_global_device_ids=true | all-gather | bytes 67584 | tf_op jit(solution)/shard_map/all_gather | solution.py:62
  699.0 18.0 all-to-all-done
  725.6 46.5 %all-to-all-start.2 = ((bf16[32,96,2048]{2,1,0:T(8,128)(2,1)}), bf16[32,96,2048]{2,1,0:T(8,128)(2,1)}, u32[]{:S(2)}, u32[]{:S(2)}) async-start(bf16[32,96,2048]{2,1,0:T(8,128)(2,1)} %bitcast.230), calls=%async_computation.2 | async-start | bytes 25165824 | tf_op jit(solution)/shard_map/all_to_all | solution.py:91
  779.3 15.7 fusion.23
  813.2 238.2 %all-to-all-done.2 = bf16[32,96,2048]{2,1,0:T(8,128)(2,1)} async-done(((bf16[32,96,2048]{2,1,0:T(8,128)(2,1)}), bf16[32,96,2048]{2,1,0:T(8,128)(2,1)}, u32[]{:S(2)}, u32[]{:S(2)}) %all-to-all-start.2) | async-done | bytes 12582944 | tf_op jit(solution)/shard_map/all_to_all | solution.py:91
  1055.4 18.9 fusion.37
  1077.7 17.7 bitcast_convert_fusion
  1095.4 238.8 %all-to-all-done.1 = bf16[32,96,2048]{2,1,0:T(8,128)(2,1)} async-done(((bf16[32,96,2048]{2,1,0:T(8,128)(2,1)}), bf16[32,96,2048]{2,1,0:T(8,128)(2,1)}, u32[]{:S(2)}, u32[]{:S(2)}) %all-to-all-start.1) | async-done | bytes 12582944 | tf_op jit(solution)/shard_map/all_to_all | solution.py:203
  1338.5 23.8 copy.236
  1362.3 30.9 %gather_fusion = bf16[1024,2,2048]{2,1,0:T(2,128)(2,1)} fusion(bf16[16,2,96,2048]{3,1,2,0:T(2,128)(2,1)} %copy.236, s32[1024]{0:T(1024)S(1)} %bitcast.225), kind=kCustom, calls=%fused_computation | custom fusion | bytes 16785408 | tf_op jit(solution)/shard_map/gather | solution.py:97
  1393.2 27.6 %convert_reduce_fusion = f32[1024,2048]{1,0:T(8,128)} fusion(bf16[1024,2,2048]{2,1,0:T(2,128)(2,1)} %gather_fusion), kind=kLoop, calls=%fused_computation.6 | loop fusion | flops 6291456 | bytes 16777216 | tf_op jit(solution)/shard_map/reduce_sum | solution.py:98
  1426.4 190.4 %all-to-all-done.3 = bf16[32,96,2048]{2,1,0:T(8,128)(2,1)} async-done(((bf16[32,96,2048]{2,1,0:T(8,128)(2,1)}), bf16[32,96,2048]{2,1,0:T(8,128)(2,1)}, u32[]{:S(2)}, u32[]{:S(2)}) %all-to-all-start.3) | async-done | bytes 12582944 | tf_op jit(solution)/shard_map/all_to_all | solution.py:242
  1616.8 25.6 copy.239
  1642.4 37.7 %gather_fusion.1 = f32[1024,2,2048]{2,1,0:T(2,128)} fusion(f32[16,2,96,2048]{3,1,2,0:T(2,128)} %copy.239, s32[1024]{0:T(1024)S(1)} %bitcast.226), kind=kCustom, calls=%fused_computation.1 | custom fusion | bytes 33562624 | tf_op jit(solution)/shard_map/gather | solution.py:97
  1680.1 24.9 reduce_sum.223
  1769.3 12.1 reduce-scatter.24.cloned.1.call-done
  1797.1 40.0 %reduce-scatter.22.cloned.1.call-done = bf16[128,2048]{1,0:T(8,128)(2,1)} async-done(((bf16[1024,2048]{1,0:T(8,128)(2,1)}), bf16[128,2048]{1,0:T(8,128)(2,1)}) %reduce-scatter.22.cloned.1.call-update) | async-done | bytes 524304
  1871.8 17.2 convolution_bitcast_fusion
  1889.0 16.5 copy.251
  1916.7 57.5 %reduce-scatter.26.cloned.1.call-done = f32[64,16]{1,0:T(8,128)} async-done(((f32[2048,16]{1,0:T(8,128)}), f32[64,16]{1,0:T(8,128)}) %reduce-scatter.26.cloned.1.call-update) | async-done | bytes 4112
  1991.7 41.1 %all-reduce.12 = (f32[2048]{0:T(1024)S(1)}, f32[2048]{0:T(1024)S(1)}, f32[2048]{0:T(1024)S(1)}, f32[2048]{0:T(1024)S(1)}) all-reduce(f32[2048]{0:T(1024)S(1)} %get-tuple-element.112, f32[2048]{0:T(1024)S(1)} %get-tuple-element.110, f32[2048]{0:T(1024)S(1)} %get-tuple-element.108, ...), channel_id=9, replica_groups=mesh['fsdp'=4,'seq'=8] {'fsdp','seq'}, use_global_device_ids=true, to_apply=%region_33.34.clone | all-reduce | flops 8192 | bytes 65536
  2036.3 120.8 %reduce-scatter.20.cloned.1.call-done = f32[64,2048]{1,0:T(8,128)} async-done(((f32[2048,2048]{1,0:T(8,128)}), f32[64,2048]{1,0:T(8,128)}) %reduce-scatter.20.cloned.1.call-update) | async-done | bytes 524304 | tf_op jit(solution)/shard_map/reduce_scatter | solution.py:318
  2157.1 187.4 %reduce-scatter.18.cloned.1.call-done = f32[64,2048]{1,0:T(8,128)} async-done(((f32[2048,2048]{1,0:T(8,128)}), f32[64,2048]{1,0:T(8,128)}) %reduce-scatter.18.cloned.1.call-update) | async-done | bytes 524304 | tf_op jit(solution)/shard_map/reduce_scatter | solution.py:317
  2344.5 187.3 %reduce-scatter.16.cloned.1.call-done = f32[64,2048]{1,0:T(8,128)} async-done(((f32[2048,2048]{1,0:T(8,128)}), f32[64,2048]{1,0:T(8,128)}) %reduce-scatter.16.cloned.1.call-update) | async-done | bytes 524304 | tf_op jit(solution)/shard_map/reduce_scatter | solution.py:316
  2531.9 187.5 %reduce-scatter.14.cloned.1.call-done = f32[64,2048]{1,0:T(8,128)} async-done(((f32[2048,2048]{1,0:T(8,128)}), f32[64,2048]{1,0:T(8,128)}) %reduce-scatter.14.cloned.1.call-update) | async-done | bytes 524304 | tf_op jit(solution)/shard_map/reduce_scatter | solution.py:315
  (326 shorter events, 312.4 us)
Async XLA Ops:
  7.2 84.5 %all-gather.15.cloned.1.call-start = ((), (), s32[]{:S(2)}) async-start(), calls=%async_computation.14 | async-start | bytes 8650752 | tf_op jit(solution)/shard_map/all_gather | solution.py:59
  9.0 162.2 %all-gather.13.cloned.1.call-start = ((), (), s32[]{:S(2)}) async-start(), calls=%async_computation.13 | async-start | bytes 8650752 | tf_op jit(solution)/shard_map/all_gather | solution.py:58
  10.9 239.9 %all-gather.9.cloned.1.call-start = ((), (), s32[]{:S(2)}) async-start(), calls=%async_computation.11 | async-start | bytes 8650752 | tf_op jit(solution)/shard_map/all_gather | solution.py:60
  12.7 276.5 %all-gather.17.cloned.1.call-start = ((), (), s32[]{:S(2)}) async-start(), calls=%async_computation.15 | async-start | bytes 4718592 | tf_op jit(solution)/shard_map/all_gather | solution.py:152
  58.9 191.9 %copy-start.24 = (f32[2048]{0:T(1024)}, f32[2048]{0:T(1024)S(1)}, u32[]{:S(2)}) copy-start(f32[2048]{0:T(1024)S(1)} %convert_element_type.186) | copy-start | bytes 24580
  58.9 117.1 %copy-start.40 = (f32[2048]{0:T(1024)}, f32[2048]{0:T(1024)S(1)}, u32[]{:S(2)}) copy-start(f32[2048]{0:T(1024)S(1)} %convert_element_type.195) | copy-start | bytes 24580
  60.7 190.1 %copy-start.46 = (f32[128]{0:T(128)}, f32[128]{0:T(128)S(1)}, u32[]{:S(2)}) copy-start(f32[128]{0:T(128)S(1)} %fusion.74) | copy-start | bytes 1540
  61.0 117.1 %copy-start.31 = (f32[128,64]{1,0:T(8,128)}, f32[128,64]{1,0:T(8,128)S(1)}, u32[]{:S(2)}) copy-start(f32[128,64]{1,0:T(8,128)S(1)} %get-tuple-element.149) | copy-start | bytes 98308
  61.0 117.1 %copy-start.33 = (f32[128,64]{1,0:T(8,128)}, f32[128,64]{1,0:T(8,128)S(1)}, u32[]{:S(2)}) copy-start(f32[128,64]{1,0:T(8,128)S(1)} %get-tuple-element.150) | copy-start | bytes 98308
  61.0 110.2 %copy-start.1 = (bf16[128,2048]{1,0:T(8,128)(2,1)S(1)}, bf16[128,2048]{1,0:T(8,128)(2,1)}, u32[]{:S(2)}) copy-start(bf16[128,2048]{1,0:T(8,128)(2,1)} %param.15) | copy-start | bytes 1572868
  179.5 109.7 %copy-start.14 = (bf16[128,16,64]{2,0,1:T(8,128)(2,1)}, bf16[128,16,64]{2,0,1:T(8,128)(2,1)S(1)}, u32[]{:S(2)}) copy-start(bf16[128,16,64]{2,0,1:T(8,128)(2,1)S(1)} %get-tuple-element.128) | copy-start | bytes 786436
  179.5 109.7 %copy-start.16 = (bf16[128,16,64]{2,0,1:T(8,128)(2,1)}, bf16[128,16,64]{2,0,1:T(8,128)(2,1)S(1)}, u32[]{:S(2)}) copy-start(bf16[128,16,64]{2,0,1:T(8,128)(2,1)S(1)} %get-tuple-element.129) | copy-start | bytes 786436
  180.9 91.2 %copy-start.73 = (s32[2]{0:T(128)S(1)}, s32[2]{0:T(128)}, u32[]{:S(2)}) copy-start(s32[2]{0:T(128)} %constant.88) | copy-start | bytes 28
  180.9 147.3 %all-gather.11.cloned.1.call-start = ((), (), s32[]{:S(2)}) async-start(), calls=%async_computation.12 | async-start | bytes 4718592 | tf_op jit(solution)/shard_map/all_gather | solution.py:153
  256.3 152.8 %all-gather.19.cloned.1.call-start = ((), (), s32[]{:S(2)}) async-start(), calls=%async_computation.16 | async-start | bytes 8650752 | tf_op jit(solution)/shard_map/all_gather | solution.py:61
  266.4 147.4 %copy-start.44 = (f32[2048]{0:T(1024)}, f32[2048]{0:T(1024)S(1)}, u32[]{:S(2)}) copy-start(f32[2048]{0:T(1024)S(1)} %convert_element_type.207) | copy-start | bytes 24580
  415.0 265.6 %copy-start.12 = (bf16[128,2048]{1,0:T(8,128)(2,1)}, bf16[128,2048]{1,0:T(8,128)(2,1)S(1)}, u32[]{:S(2)}) copy-start(bf16[128,2048]{1,0:T(8,128)(2,1)S(1)} %multiply_convert_fusion.3) | copy-start | bytes 1572868
  434.1 246.4 %copy-start.28 = (bf16[128,2048]{1,0:T(8,128)(2,1)S(1)}, bf16[128,2048]{1,0:T(8,128)(2,1)}, u32[]{:S(2)}) copy-start(bf16[128,2048]{1,0:T(8,128)(2,1)} %param.18) | copy-start | bytes 1572868
  434.1 283.0 %all-to-all-start = ((bf16[32,96,2048]{2,1,0:T(8,128)(2,1)}), bf16[32,96,2048]{2,1,0:T(8,128)(2,1)}, u32[]{:S(2)}, u32[]{:S(2)}) async-start(bf16[32,96,2048]{2,1,0:T(8,128)(2,1)} %bitcast.229), calls=%async_computation | async-start | bytes 25165824 | tf_op jit(solution)/shard_map/all_to_all | solution.py:91
  725.6 325.8 %all-to-all-start.2 = ((bf16[32,96,2048]{2,1,0:T(8,128)(2,1)}), bf16[32,96,2048]{2,1,0:T(8,128)(2,1)}, u32[]{:S(2)}, u32[]{:S(2)}) async-start(bf16[32,96,2048]{2,1,0:T(8,128)(2,1)} %bitcast.230), calls=%async_computation.2 | async-start | bytes 25165824 | tf_op jit(solution)/shard_map/all_to_all | solution.py:91
  1051.4 282.8 %all-to-all-start.1 = ((bf16[32,96,2048]{2,1,0:T(8,128)(2,1)}), bf16[32,96,2048]{2,1,0:T(8,128)(2,1)}, u32[]{:S(2)}, u32[]{:S(2)}) async-start(bf16[32,96,2048]{2,1,0:T(8,128)(2,1)} %bitcast.236), calls=%async_computation.1 | async-start | bytes 25165824 | tf_op jit(solution)/shard_map/all_to_all | solution.py:203
  1095.4 243.0 %copy-start.64 = (f32[128]{0:T(128)S(1)}, f32[128]{0:T(128)}, u32[]{:S(2)}) copy-start(f32[128]{0:T(128)} %copy-done.63) | copy-start | bytes 1540
  1095.4 243.1 %copy-start.49 = (f32[16,128]{1,0:T(8,128)S(1)}, f32[16,128]{1,0:T(8,128)}, u32[]{:S(2)}) copy-start(f32[16,128]{1,0:T(8,128)} %copy-done.48) | copy-start | bytes 24580
  1095.4 243.1 %copy-start.53 = (f32[16,128]{1,0:T(8,128)S(1)}, f32[16,128]{1,0:T(8,128)}, u32[]{:S(2)}) copy-start(f32[16,128]{1,0:T(8,128)} %copy-done.52) | copy-start | bytes 24580
  1334.2 282.7 %all-to-all-start.3 = ((bf16[32,96,2048]{2,1,0:T(8,128)(2,1)}), bf16[32,96,2048]{2,1,0:T(8,128)(2,1)}, u32[]{:S(2)}, u32[]{:S(2)}) async-start(bf16[32,96,2048]{2,1,0:T(8,128)(2,1)} %bitcast_convert_fusion), calls=%async_computation.3 | async-start | bytes 25165824 | tf_op jit(solution)/shard_map/all_to_all | solution.py:242
  1338.0 443.4 %reduce-scatter.24.cloned.1.call-start = ((), (), s32[]{:S(2)}) async-start(), calls=%async_computation.22 | async-start | bytes 4718592
  1734.1 103.0 %reduce-scatter.22.cloned.1.call-start = ((), (), s32[]{:S(2)}) async-start(), calls=%async_computation.21 | async-start | bytes 4718592
  1759.6 214.5 %reduce-scatter.26.cloned.1.call-start = ((), (), s32[]{:S(2)}) async-start(), calls=%async_computation.23 | async-start | bytes 1081344
  1761.0 396.1 %reduce-scatter.20.cloned.1.call-start = ((), (), s32[]{:S(2)}) async-start(), calls=%async_computation.20 | async-start | bytes 17301504 | tf_op jit(solution)/shard_map/reduce_scatter | solution.py:318
  1769.2 575.3 %reduce-scatter.18.cloned.1.call-start = ((), (), s32[]{:S(2)}) async-start(), calls=%async_computation.19 | async-start | bytes 17301504 | tf_op jit(solution)/shard_map/reduce_scatter | solution.py:317
  1790.8 741.1 %reduce-scatter.16.cloned.1.call-start = ((), (), s32[]{:S(2)}) async-start(), calls=%async_computation.18 | async-start | bytes 17301504 | tf_op jit(solution)/shard_map/reduce_scatter | solution.py:316
  1858.3 861.0 %reduce-scatter.14.cloned.1.call-start = ((), (), s32[]{:S(2)}) async-start(), calls=%async_computation.17 | async-start | bytes 17301504 | tf_op jit(solution)/shard_map/reduce_scatter | solution.py:315
  (64 other events, 1339.0 us)
Sparse Core Ops, SparseCore 0:
  11.4 80.2 all-gather.14
  95.1 76.0 all-gather.12
  174.7 76.0 all-gather.8
  253.0 36.0 all-gather.16
  291.5 36.7 all-gather.10
  331.5 77.4 all-gather.18
  1734.2 47.1 reduce-scatter.23
  1785.7 51.3 reduce-scatter.21
  1839.4 134.7 reduce-scatter.25
  1977.0 180.1 reduce-scatter.19
  2160.1 184.3 reduce-scatter.17
  2347.3 184.4 reduce-scatter.15
  2534.8 184.4 reduce-scatter.13
where the time goes:
time: 2740 us; the launch traced here: 2730 us
  waiting for transfers between devices  1770 us (65%)
  blocking collectives  335 us (12%)
  local copies, waits for them, and re-layouts  215 us (8%)
  matrix products  208 us (8%)
  other arithmetic  124 us (5%)
  starting transfers between devices  59.3 us (2%)
    all_to_all x2, waiting for transfers between devices, send_out(): lax.all_to_all(buffer, ('fsdp', 'seq'), split_axis=0, concat_axis=0, tile...  256 us
    all_gather x1, blocking collectives, gather_dense(): lax.all_gather(router.astype(jnp.bfloat16), ('fsdp', 'seq'), axis=0, tile...  242 us
    all_to_all x1, waiting for transfers between devices, per_device(): lax.all_to_all(result.reshape(devices, capacity, model_width), ('fsdp', '...  239 us
    all_to_all x1, waiting for transfers between devices, per_device(): lax.all_to_all(grad_sent.reshape(devices, capacity, model_width).astype(j...  190 us
    reduce_scatter x1, waiting for transfers between devices, per_device(): lax.psum_scatter(query_weight_part, ('fsdp', 'seq'), scatter_dimension=0,...  187 us
    reduce_scatter x1, waiting for transfers between devices, per_device(): lax.psum_scatter(value_weight_part, ('fsdp', 'seq'), scatter_dimension=0,...  187 us
    reduce_scatter x1, waiting for transfers between devices, per_device(): lax.psum_scatter(key_weight_part, ('fsdp', 'seq'), scatter_dimension=0, t...  187 us
    reduce_scatter x1, waiting for transfers between devices, per_device(): lax.psum_scatter(out_part, ('fsdp', 'seq'), scatter_dimension=0, tiled=True)  121 us
  transfers between devices with their start and end apart: 17, of which 17 were waited for; matrix products, arithmetic and copies ran while one was open for 14% of the time, Pallas kernels for 0%

commit v1 on v0

v1 whole, which is shorter than its diff:
```python
import jax
import jax.numpy as jnp
from jax import lax
from jax.experimental import pallas as pl
from jax.experimental.pallas import tpu as pltpu
from jax.sharding import PartitionSpec as P

HEADS = 16
SPLIT = 2
EPSILON = 1e-05
THETA = 10000.0
BOTH = ("fsdp", "seq")
BF16 = jnp.bfloat16
F32 = jnp.float32


def rows_by_rows(left, right):
    return lax.dot_general(left, right, (((0,), (0,)), ((), ())), preferred_element_type=F32)


def times_transposed(left, right):
    return lax.dot_general(left, right, (((1,), (1,)), ((), ())), preferred_element_type=F32)


def times(left, right):
    return jnp.dot(left, right, preferred_element_type=F32)


def inverse_rms(values):
    return lax.rsqrt(jnp.mean(values * values, axis=-1, keepdims=True) + EPSILON)


def rope_tables(positions, head_width):
    half_width = head_width // 2
    frequency = THETA ** (-jnp.arange(half_width, dtype=F32) * 2.0 / head_width)
    angles = positions.astype(F32)[:, None] * frequency[None, :]
    return jnp.cos(angles)[:, None, :], jnp.sin(angles)[:, None, :]


def rope(values, tables, heads):
    rows, width = values.shape
    cosine, sine = tables
    shaped = values.reshape(rows, heads, width // heads)
    half = width // heads // 2
    a, b = shaped[..., :half], shaped[..., half:]
    turned = jnp.concatenate([a * cosine - b * sine, b * cosine + a * sine], axis=-1)
    return turned.reshape(rows, width)


def rope_back(values, tables, heads):
    cosine, sine = tables
    return rope(values, (cosine, -sine), heads)


def exchange(x, mask, size):
    return lax.ppermute(x, "seq", [(i, i ^ mask) for i in range(size)])


def link_bits(size):
    bits, b = [], 2
    while b < size:
        bits.append(b)
        b *= 2
    return bits


def mask_order(size):
    masks = [0]
    for b in link_bits(size):
        masks = masks + [m | b for m in masks]
    return masks


def set_bits(mask):
    return [1 << i for i in range(mask.bit_length()) if mask >> i & 1]


def by_count(size):
    return sorted(mask_order(size), key=lambda m: (len(set_bits(m)), m))


def half_of(pieces, i):
    if len(pieces) == 2:
        return pieces[i]
    rows = pieces[0].shape[0] // 2
    return pieces[0][i * rows : (i + 1) * rows]


def gather_first(x, size):
    return {m: [x if m == 0 else exchange(x, m, size)] for m in [0] + link_bits(size)}


def gather_rest(pieces, size):
    pieces = dict(pieces)
    for m in by_count(size):
        bits = set_bits(m)
        if len(bits) > 1:
            low, high = bits[0], bits[-1]
            pieces[m] = [
                exchange(half_of(pieces[m ^ high], 0), high, size),
                exchange(half_of(pieces[m ^ low], 1), low, size),
            ]
    return pieces


def gather_one_way(pieces, size, high):
    pieces = dict(pieces)
    for m in by_count(size):
        bits = set_bits(m)
        if len(bits) > 1:
            b = bits[-1] if high else bits[0]
            pieces[m] = [exchange(pieces[m ^ b][0], b, size)]
    return pieces


def gather_pieces(x, size):
    return gather_rest(gather_first(x, size), size)


def flat(pieces):
    return [a for p in pieces.values() for a in p]


def other_core(pieces, size):
    return {m: [exchange(a, 1, size) for a in p] for m, p in pieces.items()}


def add_blocks(outputs, dtypes, unit):
    arrays, specs, index = [], [], {}
    for out in outputs:
        for terms in out:
            for array, block in terms:
                width = array.shape[1]
                index[(id(array), block)] = len(arrays)
                arrays.append(array)
                specs.append(pl.BlockSpec((unit, width), lambda i, block=block: (block, 0)))

    where = [[[index[(id(a), k)] for a, k in terms] for terms in out] for out in outputs]
    count = len(arrays)

    def kernel(*refs):
        for out_ref, blocks in zip(refs[count:], where):
            for i, terms in enumerate(blocks):
                total = refs[terms[0]][...].astype(F32)
                for t in terms[1:]:
                    total = total + refs[t][...].astype(F32)
                out_ref[i * unit : (i + 1) * unit, :] = total.astype(out_ref.dtype)

    shapes = [
        jax.ShapeDtypeStruct((len(out) * unit, width), dtype) for out, dtype in zip(outputs, dtypes)
    ]
    bytes_moved = sum(unit * width * 2 for _ in arrays) * 2
    return pl.pallas_call(
        kernel,
        grid=(1,),
        out_shape=shapes,
        in_specs=specs,
        out_specs=[pl.BlockSpec(s.shape, lambda i: (0, 0)) for s in shapes],
        compiler_params=pltpu.CompilerParams(vmem_limit_bytes=48 << 20),
        cost_estimate=pl.CostEstimate(flops=0, bytes_accessed=bytes_moved, transcendentals=0),
    )(*arrays)


def wait_first(outs, arrays):
    if arrays is None:
        return outs
    array, block = outs[0][0][-1]
    outs[0][0][-1] = (after(array, *arrays()), block)
    return outs


def scatter_sum(groups, size, unit, dtypes, hold=None, ties=None):
    ties = ties or {}
    order = by_count(size)
    at = {m: i for i, m in enumerate(mask_order(size))}
    extra = {(m, k): [] for m in order for k in range(len(groups))}

    def terms(m, k):
        keep, got, stride, offset, _ = groups[k]
        block = at[m] * stride + offset
        return [(keep, block), (got, block)] + extra[(m, k)]

    level = max(len(set_bits(m)) for m in order)
    while level > 0:
        routes = {}
        for m in order:
            bits = set_bits(m)
            if len(bits) == level:
                for k, g in enumerate(groups):
                    routes.setdefault((m, bits[-1] if g[4] else bits[0]), []).append(k)
        outs = [[terms(m, k) for k in members] for (m, _), members in routes.items()]
        outs = wait_first(outs, ties.get(level))
        sums = add_blocks(outs, [BF16] * len(outs), unit)
        if hold is not None:
            sums = hold(level, sums)
        for ((m, b), members), x in zip(routes.items(), sums):
            arrived = exchange(x, b, size)
            for i, k in enumerate(members):
                extra[(m ^ b, k)].append((arrived, i))
        level -= 1
    outs = wait_first([[terms(0, k)] for k in range(len(groups))], ties.get(0))
    sums = add_blocks(outs, dtypes, unit)
    return sums if hold is None else hold(0, sums)


def expert_rows(m_parts, c_all, c_rows, gates, row, gu, down):
    width = gu.shape[0]
    hidden = down.shape[0]
    rows = sum(n for _, _, n in m_parts)

    def inputs(parts):
        arrays = []
        for a, _, _ in parts:
            if not any(a is b for b in arrays):
                arrays.append(a)
        places, at = [], 0
        for a, first, n in parts:
            places.append(([i for i, b in enumerate(arrays) if b is a][0], first, n, at))
            at += n
        return arrays, places

    m_arrays, m_places = inputs(m_parts)
    nc = c_rows.shape[0]
    nm, each = len(m_arrays), rows // nc
    step = 256
    steps = rows // step
    small = 16

    def kernel(*refs):
        m_in = refs[:nm]
        c_in, table, gate_in, gu_in, dn_in = refs[nm : nm + 5]
        mix_out, dmx_out, dots_ref, m_out, c_out, hid_out, dgu_out = refs[nm + 5 : nm + 12]
        (m_s, c_s, gu_w, dn_w, hid_s, mix_s, dmx_s, dgu_s, g_s, q_s, gate_ref,
         m_sem, c_sem, w_sem, o_sem) = refs[nm + 12 :]

        copies_m = [
            pltpu.make_async_copy(
                m_in[k].at[pl.ds(first, n)], m_s.at[pl.ds(at, n)], m_sem.at[i]
            )
            for i, (k, first, n, at) in enumerate(m_places)
        ]
        copies_c = [
            pltpu.make_async_copy(
                c_in.at[pl.ds(pl.multiple_of(table[i], each), each)],
                c_s.at[pl.ds(i * each, each)],
                c_sem.at[i],
            )
            for i in range(nc)
        ]
        c_places = [(0, 0, each, i * each) for i in range(nc)]
        g_copy = pltpu.make_async_copy(gate_in.at[pl.ds(row, rows)], gate_ref, w_sem.at[2])
        w_gu = pltpu.make_async_copy(gu_in, gu_w, w_sem.at[0])
        w_dn = pltpu.make_async_copy(dn_in, dn_w, w_sem.at[1])
        def of_block(copies, places, b):
            return [c for c, p in zip(copies, places) if b * step <= p[3] < (b + 1) * step]

        for c in of_block(copies_m, m_places, 0):
            c.start()
        w_gu.start()
        g_copy.start()

        def sends(b):
            here = pl.ds(b * step, step)
            return [
                pltpu.make_async_copy(dmx_s.at[here], dmx_out.at[here], o_sem.at[2 * b]),
                pltpu.make_async_copy(mix_s.at[here], mix_out.at[here], o_sem.at[2 * b + 1]),
            ]

        n = 2 * steps
        whole = [
            pltpu.make_async_copy(m_s, m_out, o_sem.at[n]),
            pltpu.make_async_copy(c_s, c_out, o_sem.at[n + 1]),
            pltpu.make_async_copy(hid_s, hid_out, o_sem.at[n + 2]),
            pltpu.make_async_copy(dgu_s, dgu_out, o_sem.at[n + 3]),
        ]

        def block(b, carry):
            r = pl.ds(pl.multiple_of(b * step, step), step)
            for k in range(steps):

                @pl.when(b == k)
                def _():
                    for c in of_block(copies_m, m_places, k):
                        c.wait()
                    if k == 0:
                        w_gu.wait()
                        g_copy.wait()
                        w_dn.start()
                        for c in of_block(copies_c, c_places, 0):
                            c.start()
                    if k + 1 < steps:
                        for c in of_block(copies_m, m_places, k + 1):
                            c.start()

            g_s[...] = times(m_s[r, :], gu_w[...])
            for k in range(steps):

                @pl.when(b == k)
                def _():
                    for c in of_block(copies_c, c_places, k):
                        c.wait()
                    if k == 0:
                        w_dn.wait()
                    if k + 1 < steps:
                        for c in of_block(copies_c, c_places, k + 1):
                            c.start()
                    else:
                        whole[0].start()
                        whole[1].start()

            q_s[...] = times_transposed(c_s[r, :], dn_w[...])
            for s in range(step // small):
                here = slice(s * small, (s + 1) * small)
                out = pl.ds(pl.multiple_of(b * step + s * small, small), small)
                scale = gate_ref[out, :]
                g = g_s[here, :hidden]
                u = g_s[here, hidden:]
                q = q_s[here, :]
                sig = jax.nn.sigmoid(g)
                act = g * sig
                hid = act * u
                dots_ref[out, :] = jnp.sum(hid * q, axis=1, keepdims=True)
                hid_s[out, :] = (hid * scale).astype(BF16)
                dh = q * scale
                dgu_s[out, :hidden] = (dh * u * (sig + act * (1.0 - sig))).astype(BF16)
                dgu_s[out, hidden:] = (dh * act).astype(BF16)
            dmx_s[r, :] = times_transposed(dgu_s[r, :], gu_w[...]).astype(BF16)
            mix_s[r, :] = times(hid_s[r, :], dn_w[...]).astype(BF16)
            for k in range(steps):

                @pl.when(b == k)
                def _():
                    for c in sends(k):
                        c.start()

            return carry

        lax.fori_loop(0, steps, block, 0)
        whole[2].start()
        whole[3].start()
        for c in whole + [c for k in range(steps) for c in sends(k)]:
            c.wait()

    anywhere = pl.BlockSpec(memory_space=pl.ANY)
    vmem = pl.BlockSpec(memory_space=pltpu.VMEM)
    sds = jax.ShapeDtypeStruct
    return pl.pallas_call(
        kernel,
        out_shape=[
            sds((rows, width), BF16),
            sds((rows, width), BF16),
            sds((rows, 1), F32),
            sds((rows, width), BF16),
            sds((rows, width), BF16),
            sds((rows, hidden), BF16),
            sds((rows, 2 * hidden), BF16),
        ],
        in_specs=[anywhere] * (nm + 1)
        + [pl.BlockSpec(memory_space=pltpu.SMEM)]
        + [anywhere] * 3,
        out_specs=[anywhere] * 2 + [vmem] + [anywhere] * 4,
        scratch_shapes=[
            pltpu.VMEM((rows, width), BF16),
            pltpu.VMEM((rows, width), BF16),
            pltpu.VMEM((width, 2 * hidden), BF16),
            pltpu.VMEM((hidden, width), BF16),
            pltpu.VMEM((rows, hidden), BF16),
            pltpu.VMEM((rows, width), BF16),
            pltpu.VMEM((rows, width), BF16),
            pltpu.VMEM((rows, 2 * hidden), BF16),
            pltpu.VMEM((step, 2 * hidden), F32),
            pltpu.VMEM((step, hidden), F32),
            pltpu.VMEM((rows, 1), F32),
            pltpu.SemaphoreType.DMA((len(m_places),)),
            pltpu.SemaphoreType.DMA((nc,)),
            pltpu.SemaphoreType.DMA((3,)),
            pltpu.SemaphoreType.DMA((2 * steps + 4,)),
        ],
        compiler_params=pltpu.CompilerParams(vmem_limit_bytes=60 << 20),
        cost_estimate=pl.CostEstimate(
            flops=2 * rows * width * hidden * 6, bytes_accessed=24 << 20, transcendentals=0
        ),
    )(*m_arrays, c_all, c_rows, gates, gu, down)


def gate_up_weights(lefts, rights, before=None, rest=None):
    rows, width = lefts[0].shape
    cols = rights[0].shape[1]
    n, tile = len(lefts), 512
    steps = width // tile // 2
    skip = 0 if rest is None else steps

    def kernel(*refs):
        total = rows_by_rows(refs[0][...], refs[n][...])
        for i in range(1, n):
            total = total + rows_by_rows(refs[i][...], refs[n + i][...])
        out = refs[-1]
        for k in range(2):
            part = total[:, k * (cols // 2) : (k + 1) * (cols // 2)]
            out[:, k, :] = part if before is None else part + refs[2 * n][:, k, :]

    block = pl.BlockSpec((tile, 2, cols // 2), lambda i: (i + skip, 0, 0))
    extra = [] if before is None else [before]
    old = [] if rest is None else [rest]
    return pl.pallas_call(
        kernel,
        grid=(steps,),
        out_shape=jax.ShapeDtypeStruct((width, 2, cols // 2), F32),
        in_specs=[pl.BlockSpec((rows, tile), lambda i: (0, i + skip))] * n
        + [pl.BlockSpec((rows, cols), lambda i: (0, 0))] * n
        + [block] * len(extra)
        + [pl.BlockSpec(memory_space=pl.ANY)] * len(old),
        out_specs=block,
        input_output_aliases={2 * n + len(extra): 0} if old else {},
        compiler_params=pltpu.CompilerParams(vmem_limit_bytes=58 << 20),
        cost_estimate=pl.CostEstimate(
            flops=n * rows * width * cols, bytes_accessed=16 << 20, transcendentals=0
        ),
    )(*lefts, *rights, *extra, *old)


def down_weights(lefts, rights, before=None):
    rows, hidden = lefts[0].shape
    width = rights[0].shape[1]
    n, tile = len(lefts), 512

    def kernel(*refs):
        total = rows_by_rows(refs[0][...], refs[n][...])
        for i in range(1, n):
            total = total + rows_by_rows(refs[i][...], refs[n + i][...])
        refs[-1][...] = total if before is None else total + refs[2 * n][...]

    block = pl.BlockSpec((hidden, tile), lambda i: (0, i))
    extra = [] if before is None else [before]
    return pl.pallas_call(
        kernel,
        grid=(width // tile,),
        out_shape=jax.ShapeDtypeStruct((hidden, width), F32),
        in_specs=[pl.BlockSpec((rows, hidden), lambda i: (0, 0))] * n
        + [pl.BlockSpec((rows, tile), lambda i: (0, i))] * n
        + [block] * len(extra),
        out_specs=block,
        compiler_params=pltpu.CompilerParams(vmem_limit_bytes=58 << 20),
        cost_estimate=pl.CostEstimate(
            flops=2 * n * rows * width * hidden, bytes_accessed=24 << 20, transcendentals=0
        ),
    )(*lefts, *rights, *extra)


def after(x, *others):
    return lax.optimization_barrier((x, *others))[0]


def flip_slots(x, size, me):
    n = len(link_bits(size)) + 1
    for axis, b in enumerate([1] + link_bits(size)[::-1]):
        x = jnp.where((me & b) != 0, jnp.flip(x, axis), x)
    return x, n


def to_slots(x, size, me):
    n = len(link_bits(size)) + 1
    y = jnp.moveaxis(x.reshape((2,) * n + x.shape[1:]), n - 1, 0)
    return flip_slots(y, size, me)[0].reshape(x.shape)


def from_slots(x, size, me):
    n = len(link_bits(size)) + 1
    y = flip_slots(x.reshape((2,) * n + x.shape[1:]), size, me)[0]
    return jnp.moveaxis(y, 0, n - 1).reshape(x.shape)


def per_device(
    tokens,
    segments,
    routes,
    out_grad,
    w_query,
    w_key,
    w_value,
    w_out,
    router,
    attn_gain,
    q_gain,
    k_gain,
    ffn_gain,
    expert_gate_up,
    expert_down,
):
    F, S = lax.axis_size("fsdp"), lax.axis_size("seq")
    N = F * S
    experts = N // SPLIT
    R, D = tokens.shape
    HW = D // HEADS
    HL = HEADS // S
    CW = HL * HW
    RW = w_query.shape[0]
    L = S * R
    scale = HW ** (-0.5)
    me_f, me_s = lax.axis_index("fsdp"), lax.axis_index("seq")
    me = me_f * S + me_s
    order = mask_order(S)
    slots = jnp.stack([me_s ^ m for m in order + [m | 1 for m in order]])

    def shift_in(x, j):
        return lax.ppermute(x, "fsdp", [((i + j) % F, i) for i in range(F)])

    def shift_back(x, j):
        return lax.ppermute(x, "fsdp", [(i, (i + j) % F) for i in range(F)])

    def in_order(pieces):
        return [a for m in order for a in pieces[m]]

    def sequence_rows(x):
        mine = gather_pieces(x, S)
        return jnp.concatenate(in_order(mine) + in_order(other_core(mine, S)))

    w_low = jnp.stack([w.astype(BF16) for w in (w_query, w_key, w_value)], axis=1)
    w_send = w_low.reshape(RW, 3, S, CW).transpose(2, 0, 1, 3).reshape(S, RW, 3 * CW)
    w_mine = lax.all_to_all(w_send, "seq", split_axis=0, concat_axis=0, tiled=True)
    w_mine = w_mine.reshape(S * RW, 3 * CW)
    gains = jnp.stack([attn_gain, q_gain, k_gain, ffn_gain])
    small = [gains.astype(BF16), router.T.astype(BF16), segments.astype(BF16)]
    sizes = [4 * RW, experts * RW, R]
    pad = jnp.zeros((-sum(sizes) % 128,), BF16)
    small = jnp.concatenate([a.reshape(-1) for a in small] + [pad]).reshape(1, -1, 128)
    small = after(small, w_mine)
    small = jnp.broadcast_to(small, (N,) + small.shape[1:])
    small = lax.all_to_all(small, BOTH, split_axis=0, concat_axis=0, tiled=True).reshape(N, -1)
    parts, at = [], 0
    for n in sizes:
        parts.append(small[:, at : at + n])
        at += n
    gains_all = parts[0].reshape(N, 4, RW).transpose(1, 0, 2).reshape(4, D).astype(F32)
    ga, gq, gk, gf = [gains_all[i] for i in range(4)]
    router_t = parts[1].reshape(N, experts, RW).transpose(1, 0, 2).reshape(experts, D)
    segment_all = lax.dynamic_slice(parts[2].astype(F32), (me_f * S, 0), (S, R))

    wo_all = lax.all_gather(w_out.astype(BF16), BOTH, axis=0, tiled=True)
    c_all = lax.all_gather(after(out_grad, w_mine), BOTH, axis=0, tiled=True)
    expert = me // SPLIT
    unit = R // 2
    z_order = sorted(range(1, F), key=lambda j: (-min(j, F - j), j))
    hidden_width = expert_down.shape[1]
    gu_low = after(expert_gate_up, w_mine)[0].astype(BF16).reshape(D, 2 * hidden_width)
    down_low = after(expert_down, w_mine)[0].astype(BF16)

    up = down = w_mine
    ups, downs = [], []
    x_first = gather_first(after(tokens, w_mine), S)
    x_both = []
    for k in range(F - 1):
        up = lax.ppermute(up, "fsdp", [(i, i + 1) for i in range(F - 1)])
        down = lax.ppermute(down, "fsdp", [(i + 1, i) for i in range(F - 1)])
        ups.append(up)
        downs.append(down)
        if k == 0:
            keys = list(x_first)
            up, down, small, *got = lax.optimization_barrier(
                (up, down, small, *[x_first[m][0] for m in keys])
            )
            x_first = {m: [a] for m, a in zip(keys, got)}
            x_mine = gather_rest(x_first, S)
            x_other = other_core(x_first, S)
        elif k == 1:
            near = flat(x_other)
            far_keys = [m for m in x_mine if m not in x_first]
            far = [a for m in far_keys for a in x_mine[m]]
            up, down, *got = lax.optimization_barrier((up, down, *far, *near))
            far, near = got[: len(far)], got[len(far) :]
            x_other = {m: [a] for m, a in zip(keys, near)}
            for i, m in enumerate(far_keys):
                x_mine[m] = far[2 * i : 2 * i + 2]
                x_other[m] = [exchange(a, 1, S) for a in x_mine[m]]
        else:
            up, down = lax.optimization_barrier((up, down))
    x_seq = jnp.concatenate(in_order(x_mine) + in_order(x_other)).astype(F32)
    x_inverse = inverse_rms(x_seq)
    a_seq = after((x_seq * x_inverse * ga).astype(BF16), gu_low, down_low)
    cols = 3 * CW
    w_cols = jnp.concatenate(ups[::-1] + [w_mine] + downs)
    w_cols = lax.dynamic_slice(w_cols, ((F - 1 - me_f) * S * RW, 0), (D, cols))
    qkv = times(a_seq, w_cols)
    q_proj, k_proj = qkv[:, :CW], qkv[:, CW : 2 * CW]
    value = qkv[:, 2 * CW :].astype(BF16)

    def seq_sum(stats):
        stats = stats.reshape(-1, 2, S // 2, R)
        total = stats + exchange(stats, 1, S)[:, ::-1]
        for b in link_bits(S):
            other = exchange(total, b, S)
            total = total + jnp.stack([other[:, :, order.index(m ^ b)] for m in order], axis=2)
        return total.reshape(-1, L)

    squares = seq_sum(jnp.stack([jnp.sum(q_proj * q_proj, 1), jnp.sum(k_proj * k_proj, 1)]))
    inverse = lax.rsqrt(squares / D + EPSILON)
    q_inv, k_inv = inverse[0][:, None], inverse[1][:, None]
    gq_mine = lax.dynamic_slice(gq, (me_s * CW,), (CW,))
    gk_mine = lax.dynamic_slice(gk, (me_s * CW,), (CW,))
    positions = (slots[:, None] * R + jnp.arange(R, dtype=jnp.int32)[None]).reshape(L)
    segment_seq = to_slots(segment_all, S, me_s).reshape(L)
    tables = rope_tables(positions, HW)
    query = rope(q_proj * q_inv * gq_mine, tables, HL).astype(BF16)
    key = rope(k_proj * k_inv * gk_mine, tables, HL).astype(BF16)

    allowed = (positions[None, :] <= positions[:, None]) & (
        segment_seq[None, :] == segment_seq[:, None]
    )
    q_heads = query.reshape(L, HL, HW)
    k_heads = key.reshape(L, HL, HW)
    v_heads = value.reshape(L, HL, HW)
    scores = jnp.einsum("thd,uhd->htu", q_heads, k_heads, preferred_element_type=F32)
    scores = jnp.where(allowed[None], scores * scale, -1e30)
    row_max = jnp.max(scores, axis=-1, keepdims=True)
    terms = jnp.where(allowed[None], jnp.exp(scores - row_max), 0.0)
    probs = terms / jnp.sum(terms, axis=-1, keepdims=True)
    probs_low = probs.astype(BF16)
    attended = jnp.einsum("htu,uhd->thd", probs_low, v_heads, preferred_element_type=F32)
    attended = attended.reshape(L, CW).astype(BF16)
    o_send = attended.reshape(S, R, CW)
    o_send = from_slots(o_send, S, me_s)
    o_mine = lax.all_to_all(o_send, "seq", split_axis=0, concat_axis=0, tiled=True)
    o_mine = o_mine.transpose(1, 0, 2).reshape(R, D)
    middle = tokens.astype(F32) + times(o_mine, wo_all)
    mid_inv = inverse_rms(middle)
    mixed = (middle * mid_inv * gf).astype(BF16)
    expert_probs = jax.nn.softmax(times_transposed(mixed, router_t), axis=-1)

    chosen = routes[:, :, None] == jnp.arange(experts, dtype=jnp.int32)
    named = jnp.any(chosen, axis=1).astype(F32)
    gates = jnp.repeat((expert_probs * named).T, SPLIT, axis=0)
    gates = lax.all_to_all(gates, BOTH, split_axis=0, concat_axis=0, tiled=True).reshape(F, S, R)
    b = 1
    while b < F:
        gates = jnp.where((me_f & b) != 0, jnp.roll(gates, -b, axis=0), gates)
        b *= 2
    m_far, last = {0: mixed}, mixed
    for j in z_order:
        last = shift_in(after(mixed, last), j)
        m_far[j] = last
    chunks = [0] + z_order
    first = {j: gather_first(m_far[j], S) for j in chunks}
    mine = {j: gather_one_way(first[j], S, i % 2) for i, j in enumerate(chunks)}
    mine[0] = gather_rest(first[0], S)
    both = {j: [mine[j], other_core(mine[j], S)] for j in chunks}
    last_chunk = chunks[-1]
    top_level = len(link_bits(S))
    calls = [(j, side) for j in chunks for side in ((1, 0) if j == last_chunk else (0, 1))]
    tick = {call: t for t, call in enumerate(calls)}
    before = {t: [] for t in range(len(calls) + 4)}
    for i, j in enumerate(chunks):
        early = 2 + (j == last_chunk)
        t = 2 * i
        before[max(t - 2 - early, 0)].append(m_far[j])
        before[max(t - 1 - early, 0)] += flat(first[j])
        before[max(t - early, 0)] += flat(mine[j])
        before[max(t + 1 - early, 0)] += flat(both[j][1])
    c_rows = (me_f + jnp.arange(F, dtype=jnp.int32)) % F * S
    c_rows = (c_rows[:, None] + slots[None]).reshape(F, 2, S // 2) * R
    finished, kept, dots = {}, [], {}
    gate_up_grad, down_grad = None, None

    def flush(kept, gate_up_grad, down_grad):
        ms, cs, hids, dgus = [list(a) for a in zip(*kept)]
        down_grad = down_weights(hids, cs, down_grad)
        first = gate_up_weights(ms, dgus, gate_up_grad)
        return gate_up_weights(ms, dgus, gate_up_grad, first), down_grad

    def last_flush(at, level):
        ms, cs, hids, dgus = [list(a) for a in zip(*kept)]
        if level == 1:
            hids[0] = after(hids[0], *before[at])
            done["down"] = down_weights(hids, cs, down_grad)
            return [done["down"]]
        ms[0] = after(ms[0], *before[at + 1], *before[at + 2], *before[at + 3])
        done["gate_up"] = gate_up_weights(ms, dgus, gate_up_grad)
        return [done["gate_up"]]

    done = {}
    mix_sides, dmx_sides, mix_got, mix_done = {}, {}, {}, {}
    gate_rows = jnp.stack([to_slots(gates[j], S, me_s) for j in range(F)]).reshape(F * L, 1)
    for t, (j, side) in enumerate(calls):
        m_parts = [(a, 0, a.shape[0]) for m in order for a in both[j][side][m]]
        m_parts[0] = (after(m_parts[0][0], *before[t]), *m_parts[0][1:])
        row = j * L + side * (L // 2)
        mix, dmx, dot, *saved = expert_rows(
            m_parts, c_all, c_rows[j, side], gate_rows, row, gu_low, down_low
        )
        mix_sides[j, side], dmx_sides[j, side] = mix, dmx
        dots[j, side] = dot.reshape(-1)
        kept.append(saved)
        if F > 4 and len(kept) == 8 and t + 2 < len(calls):
            gate_up_grad, down_grad = flush(kept, gate_up_grad, down_grad)
            before[t + 2] += [gate_up_grad, down_grad]
            kept = []
        if side:
            mix_got[j] = exchange(mix, 1, S)
            before[t + 3].append(mix_got[j])
        if (j, 1 - side) in dmx_sides:
            given = tick[j, 1]

            def hold(level, sums):
                before[min(given + 2 + top_level - level, len(calls) + 3)].extend(sums)
                return sums

            ties = None
            if j == last_chunk:
                ties = {n: lambda n=n: last_flush(len(calls), n) for n in (0, 1)}

            group = (dmx_sides[j, 0], exchange(dmx_sides[j, 1], 1, S), 1, 0, chunks.index(j) % 2)
            [total] = scatter_sum([group], S, R, [BF16 if j else F32], hold, ties)
            finished[j] = shift_back(total, j) if j else total
            last_sum = total
            if F > 4:
                group = (mix_sides.pop((j, 0)), mix_got.pop(j), 1, 0, chunks.index(j) % 2)
                [mix_done[j]] = scatter_sum([group], S, R, [BF16])
                before[min(t + 4, len(calls) + 3)].append(mix_done[j])
    dots = {j: jnp.concatenate([dots[j, 0], dots[j, 1]]).reshape(S, R) for j in chunks}
    if F <= 4:
        mix_groups = [(mix_sides[j, 0], mix_got[j], 1, 0, i % 2) for i, j in enumerate(chunks)]
    dots = [dots[j] for j in range(F)]
    finished = [finished[j] for j in range(F)]
    dmx_total = finished[0]
    for t in finished[1:]:
        dmx_total = dmx_total + t.astype(F32)
    ms, _, _, dgus = [list(a) for a in zip(*kept)]
    ms[0] = after(ms[0], last_sum)
    gate_up_grad = gate_up_weights(ms, dgus, gate_up_grad, done["gate_up"])
    down_grad = done["down"]
    dmx_total = after(dmx_total, gate_up_grad)
    expert_gate_up_grad, expert_down_grad = gate_up_grad[None], down_grad[None]
    dots = jnp.stack([from_slots(d, S, me_s) for d in dots])
    b = 1
    while b < F:
        dots = jnp.where((me_f & b) != 0, jnp.roll(dots, b, axis=0), dots)
        b *= 2
    dots = dots.reshape(N, R)
    dots = lax.all_to_all(dots, BOTH, split_axis=0, concat_axis=0, tiled=True)
    grad_probs = jnp.sum(dots.reshape(experts, SPLIT, R), axis=1).T * named
    grad_logits = expert_probs * (
        grad_probs - jnp.sum(expert_probs * grad_probs, axis=-1, keepdims=True)
    )
    grad_logits = grad_logits.astype(BF16)
    router_part = rows_by_rows(grad_logits, mixed)
    grad_mixed = dmx_total + times(grad_logits, router_t)

    grad_output = out_grad.astype(F32)
    scaled = grad_mixed * gf
    grad_middle = (
        grad_output
        + mid_inv * scaled
        - middle * mid_inv**3 * jnp.mean(scaled * middle, axis=-1, keepdims=True)
    )
    ffn_part = jnp.sum(grad_mixed * middle * mid_inv, axis=0)
    early = jnp.concatenate([router_part, ffn_part[None]]).reshape(experts + 1, N, RW)
    early = lax.all_to_all(early.transpose(1, 0, 2), BOTH, split_axis=0, concat_axis=0, tiled=True)
    early = jnp.sum(early, axis=0)
    router_grad = early[:experts].T
    ffn_grad = early[experts]

    proj_low = grad_middle.astype(BF16)
    grad_proj = sequence_rows(proj_low)
    out_part = rows_by_rows(attended, grad_proj).astype(BF16).reshape(F, RW, D)
    out_grad_total = None
    for d in range(F):
        chunk = lax.dynamic_index_in_dim(out_part, (me_f + d) % F, 0, keepdims=False)
        pairs = [(f * S + s, F * s + (f + d) % F) for f in range(F) for s in range(S)]
        got = lax.ppermute(chunk, BOTH, pairs).astype(F32)
        out_grad_total = got if d == 0 else out_grad_total + got
    def hold_mix(level, sums):
        return [after(a, grad_proj) for a in sums] if level == 1 else sums

    output = middle
    if F <= 4:
        mix_done = dict(zip(chunks, scatter_sum(mix_groups, S, R, [BF16] * F, hold_mix)))
    for j in chunks:
        output = output + (shift_back(mix_done[j], j) if j else mix_done[j]).astype(F32)
    output = output.astype(BF16)

    wo_rows = lax.dynamic_slice(wo_all, (me_s * CW, 0), (CW, D))
    grad_heads = times_transposed(after(grad_proj, out_part), wo_rows).astype(BF16).reshape(L, HL, HW)
    grad_p = jnp.einsum("thd,uhd->htu", grad_heads, v_heads, preferred_element_type=F32)
    delta = jnp.sum(probs * grad_p, axis=-1, keepdims=True)
    grad_s = (probs * (grad_p - delta)).astype(BF16)
    dq = jnp.einsum("htu,uhd->thd", grad_s, k_heads, preferred_element_type=F32)
    dk = jnp.einsum("htu,thd->uhd", grad_s, q_heads, preferred_element_type=F32)
    dv = jnp.einsum("htu,thd->uhd", probs_low, grad_heads, preferred_element_type=F32)
    dq = rope_back(dq.reshape(L, CW) * scale, tables, HL)
    dk = rope_back(dk.reshape(L, CW) * scale, tables, HL)
    q_part = jnp.sum(dq * q_proj * q_inv, axis=0)
    k_part = jnp.sum(dk * k_proj * k_inv, axis=0)
    dq = dq * gq_mine
    dk = dk * gk_mine
    means = jnp.stack([jnp.sum(dq * q_proj, 1), jnp.sum(dk * k_proj, 1)])
    means = seq_sum(after(means, out_grad_total)) / D
    dqp = q_inv * dq - q_proj * q_inv**3 * means[0][:, None]
    dkp = k_inv * dk - k_proj * k_inv**3 * means[1][:, None]
    dv_low = dv.reshape(L, CW).astype(BF16)
    dqk = jnp.concatenate([dqp.astype(BF16), dkp.astype(BF16)], axis=1)
    dqk = after(dqk, *mix_done.values())
    dqkv = jnp.concatenate([dqk, dv_low], axis=1)
    x_scaled = x_seq * x_inverse
    da_keep = times_transposed(dqkv[: L // 2], w_cols)
    da_give = times_transposed(dqkv[L // 2 :], w_cols)
    attn_part = jnp.sum(da_keep * x_scaled[: L // 2], axis=0) + jnp.sum(
        da_give * x_scaled[L // 2 :], axis=0
    )
    da_keep = da_keep.astype(BF16)
    da_got = exchange(da_give.astype(BF16), 1, S)
    da_mine = jnp.concatenate(
        scatter_sum([(da_keep, da_got, 2, h, h) for h in range(2)], S, unit, [F32] * 2)
    )
    w_sums = []
    for part, n in ((dv_low, 1), (dqk, 2)):
        w_part = rows_by_rows(a_seq, part).astype(BF16).reshape(N, RW, n * CW)
        w_got = lax.all_to_all(w_part, BOTH, split_axis=0, concat_axis=0, tiled=True)
        w_sum = jnp.sum(w_got.reshape(F, S, RW, n, CW).astype(F32), axis=0)
        w_sums.append(w_sum.transpose(2, 1, 0, 3).reshape(n, RW, D))
    w_sum = [w_sums[1][0], w_sums[1][1], w_sums[0][0]]
    late = jnp.stack(
        [
            attn_part,
            lax.dynamic_update_slice(jnp.zeros((D,), F32), q_part, (me_s * CW,)),
            lax.dynamic_update_slice(jnp.zeros((D,), F32), k_part, (me_s * CW,)),
        ]
    )
    late = late.reshape(3, N, RW).transpose(1, 0, 2)
    late = lax.all_to_all(late, BOTH, split_axis=0, concat_axis=0, tiled=True)
    late = jnp.sum(late, axis=0)

    x = tokens.astype(F32)
    x_inv = inverse_rms(x)
    scaled = da_mine * ga
    grad_in = (
        grad_middle
        + x_inv * scaled
        - x * x_inv**3 * jnp.mean(scaled * x, axis=-1, keepdims=True)
    )
    return (
        output,
        grad_in.astype(BF16),
        w_sum[0],
        w_sum[1],
        w_sum[2],
        out_grad_total,
        router_grad,
        late[0],
        late[1],
        late[2],
        ffn_grad,
        expert_gate_up_grad,
        expert_down_grad,
    )


def solution(mesh):
    one, two = P(BOTH), P(BOTH, None)
    three, four = P(BOTH, None, None), P(BOTH, None, None, None)
    return jax.shard_map(
        per_device,
        mesh=mesh,
        in_specs=(two, one, two, two, two, two, two, two, two, one, one, one, one, four, three),
        out_specs=(two, two, two, two, two, two, two, one, one, one, one, four, three),
        check_vma=False,
    )
```

time: 2740 us -> 970 us (0.35)
  waiting for transfers between devices: 1770 us -> 358 us
  blocking collectives: 335 us -> 19.4 us
  Pallas kernels: 0 us -> 200 us
  matrix products: 208 us -> 58.8 us
  local copies, waits for them, and re-layouts: 215 us -> 78.8 us
  starting transfers between devices: 59.3 us -> 147 us
  other arithmetic: 124 us -> 72.8 us
    reduce_scatter x4 -> x0, waiting for transfers between devices: 683 us -> none  [the longest x1 187 us: per_device(): lax.psum_scatter(query_weight_part, ('fsdp', 'seq'), scatter_dimension=0,...]
    all_to_all x4 -> x8, waiting for transfers between devices: 686 us -> 41.4 us  [the longest x1 15 us: per_device(): lax.all_to_all(o_send, 'seq', split_axis=0, concat_axis=0, tiled=True)]
    ppermute x0 -> x102, waiting for transfers between devices: none -> 317 us  [the longest x83 146 us: exchange(): return lax.ppermute(x, 'seq', [(i, i ^ mask) for i in range(size)])]
    all_gather x6 -> x2, waiting for transfers between devices: 292 us -> 0.02 us  [the longest x1 0.02 us: per_device(): wo_all = lax.all_gather(w_out.astype(BF16), BOTH, axis=0, tiled=True)]
    all_gather x2 -> x0, blocking collectives: 251 us -> none  [the longest x1 242 us: gather_dense(): lax.all_gather(router.astype(jnp.bfloat16), ('fsdp', 'seq'), axis=0, tile...]
    pallas_call x0 -> x29, Pallas kernels: none -> 200 us  [the longest x8 117 us: expert_rows(): pl.pallas_call(kernel, out_shape=[sds((rows, width), BF16), sds((rows, wi...]
    dot_general x20 -> x12, matrix products: 165 us -> 36.5 us  [the longest x4 14.6 us: rows_by_rows(): lax.dot_general(left, right, (((0,), (0,)), ((), ())), preferred_element_...]
    ppermute x0 -> x102, starting transfers between devices: none -> 112 us  [the longest x83 66.7 us: exchange(): return lax.ppermute(x, 'seq', [(i, i ^ mask) for i in range(size)])]
  transfers between devices with their start and end apart: 17 -> 112, of which waited for: 17 -> 39; matrix products, arithmetic and copies ran while one was open for 14% -> 19% of each run, Pallas kernels for 0% -> 18%
where the time goes in v1:
time: 970 us; the launch traced here: 951 us
  waiting for transfers between devices  358 us (37%)
  Pallas kernels  200 us (21%)
  starting transfers between devices  147 us (15%)
  local copies, waits for them, and re-layouts  78.8 us (8%)
  other arithmetic  72.8 us (8%)
  matrix products  58.8 us (6%)
  blocking collectives  19.4 us (2%)
  between operations  16.6 us (2%)
    ppermute x83, waiting for transfers between devices, exchange(): return lax.ppermute(x, 'seq', [(i, i ^ mask) for i in range(size)])  146 us
    pallas_call x8, Pallas kernels, expert_rows(): pl.pallas_call(kernel, out_shape=[sds((rows, width), BF16), sds((rows, wi...  117 us
    ppermute x83, starting transfers between devices, exchange(): return lax.ppermute(x, 'seq', [(i, i ^ mask) for i in range(size)])  66.7 us
    ppermute x6, waiting for transfers between devices, shift_back(): return lax.ppermute(x, 'fsdp', [(i, (i + j) % F) for i in range(F)])  56.7 us
    unnamed x221, local copies, waits for them, and re-layouts  46 us
    ppermute x3, waiting for transfers between devices, shift_in(): return lax.ppermute(x, 'fsdp', [((i + j) % F, i) for i in range(F)])  42.7 us
    ppermute x3, waiting for transfers between devices, per_device(): up = lax.ppermute(up, 'fsdp', [(i, i + 1) for i in range(F - 1)])  37 us
    pallas_call x18, Pallas kernels, add_blocks(): pl.pallas_call(kernel, grid=(1,), out_shape=shapes, in_specs=specs, out_s...  36.4 us
  transfers between devices with their start and end apart: 112, of which 39 were waited for; matrix products, arithmetic and copies ran while one was open for 19% of the time, Pallas kernels for 18%

profile of v1, /device:TPU:0, one launch (start us, length us, event | category | flops | bytes accessed | tf_op | source)
XLA Modules:
  0.0 951.3 jit_solution(9719301898654034534)
XLA Ops:
  15.6 19.4 %all_to_all.50 = bf16[8,64,768]{2,1,0:T(8,128)(2,1)S(1)} all-to-all(bf16[8,64,768]{2,1,0:T(8,128)(2,1)S(1)} %reshape.642), channel_id=1, replica_groups=mesh['fsdp'=4,'seq'=8] {'seq'}, dimensions={0} | all-to-all | bytes 1572864 | tf_op jit(solution)/shard_map/all_to_all | solution.py:520
  63.6 12.9 %all-to-all-done.1 = bf16[32,11,128]{2,1,0:T(8,128)(2,1)S(1)} async-done(((bf16[32,11,128]{2,1,0:T(8,128)(2,1)}), bf16[32,11,128]{2,1,0:T(8,128)(2,1)S(1)}, u32[]{:S(2)}, u32[]{:S(2)}) %all-to-all-start.1) | async-done | bytes 90144 | tf_op jit(solution)/shard_map/all_to_all | solution.py:529
  95.6 19.5 %collective-permute-done.4 = bf16[512,768]{1,0:T(8,128)(2,1)} collective-permute-done((bf16[512,768]{1,0:T(8,128)(2,1)}, bf16[512,768]{1,0:T(8,128)(2,1)}, u32[]{:S(2)}, u32[]{:S(2)}) %collective-permute-start.4) | collective-permute-done | bytes 786464 | tf_op jit(solution)/shard_map/ppermute | solution.py:553
  130.2 17.5 %collective-permute-done.13 = bf16[512,768]{1,0:T(8,128)(2,1)S(1)} collective-permute-done((bf16[512,768]{1,0:T(8,128)(2,1)}, bf16[512,768]{1,0:T(8,128)(2,1)S(1)}, u32[]{:S(2)}, u32[]{:S(2)}) %collective-permute-start.13) | collective-permute-done | bytes 786464 | tf_op jit(solution)/shard_map/ppermute | solution.py:553
  180.9 10.0 %fusion.73 = (f32[2,1024]{1,0:T(2,128)S(1)}, f32[2,1024,1024]{1,2,0:T(8,128)}) fusion(pred[1024,1024]{0,1:T(8,128)(4,1)} %compare_and_fusion, bf16[1024,2,64]{2,0,1:T(8,128)(2,1)S(1)} %get-tuple-element.294, bf16[1024,2,64]{2,0,1:T(8,128)(2,1)} %get-tuple-element.295, bf16[1024,2,64]{2,0,1:T(8,128)(2,1)} %get-tuple-element.277, ...), kind=kOutput, calls=%fused_computation.266 | convolution fusion | flops 549454848 | bytes 10493952 | tf_op jit(solution)/shard_map/sub | solution.py:615
  204.1 15.0 %all-to-all-done.2 = bf16[8,128,256]{2,1,0:T(8,128)(2,1)S(1)} async-done(((bf16[8,128,256]{2,1,0:T(8,128)(2,1)}), bf16[8,128,256]{2,1,0:T(8,128)(2,1)S(1)}, u32[]{:S(2)}, u32[]{:S(2)}) %all-to-all-start.2) | async-done | bytes 524320 | tf_op jit(solution)/shard_map/all_to_all | solution.py:622
  236.9 33.3 %collective-permute-done.27.refs_0_ = bf16[128,2048]{1,0:T(8,128)(2,1)} collective-permute-done((bf16[128,2048]{1,0:T(8,128)(2,1)S(1)}, bf16[128,2048]{1,0:T(8,128)(2,1)}, u32[]{:S(2)}, u32[]{:S(2)}) %collective-permute-start.27) | collective-permute-done | bytes 524320 | tf_op jit(solution)/shard_map/ppermute | solution.py:506
  274.7 9.4 collective-permute-done.31.refs_0_
  305.5 10.6 %collective-permute-done.37.refs_2_ = bf16[128,2048]{1,0:T(8,128)(2,1)S(1)} collective-permute-done((bf16[128,2048]{1,0:T(8,128)(2,1)S(1)}, bf16[128,2048]{1,0:T(8,128)(2,1)S(1)}, u32[]{:S(2)}, u32[]{:S(2)}) %collective-permute-start.37) | collective-permute-done | bytes 524320 | tf_op jit(solution)/shard_map/ppermute | solution.py:56
  316.6 9.0 collective-permute-done.30.refs_3_
  328.6 14.6 %shard_map.247 = (bf16[512,2048]{1,0:T(8,128)(2,1)}, bf16[512,2048]{1,0:T(8,128)(2,1)}, f32[512,1]{1,0:T(8,128)}, bf16[512,2048]{1,0:T(8,128)(2,1)}, bf16[512,20...) custom-call(bf16[128,2048]{1,0:T(8,128)(2,1)} %copy-done.50, ...), custom_call_target="tpu_custom_call" | custom-call | flops 6442450944 | bytes 25165824 | tf_op jit(solution)/shard_map/pallas_call | solution.py:347
  348.6 10.2 %collective-permute-done.41.refs_1_ = bf16[128,2048]{1,0:T(8,128)(2,1)S(1)} collective-permute-done((bf16[128,2048]{1,0:T(8,128)(2,1)}, bf16[128,2048]{1,0:T(8,128)(2,1)S(1)}, u32[]{:S(2)}, u32[]{:S(2)}) %collective-permute-start.41) | collective-permute-done | bytes 524320 | tf_op jit(solution)/shard_map/ppermute | solution.py:56
  358.8 10.5 %collective-permute-done.40.refs_3_ = bf16[128,2048]{1,0:T(8,128)(2,1)} collective-permute-done((bf16[128,2048]{1,0:T(8,128)(2,1)}, bf16[128,2048]{1,0:T(8,128)(2,1)}, u32[]{:S(2)}, u32[]{:S(2)}) %collective-permute-start.40) | collective-permute-done | bytes 524320 | tf_op jit(solution)/shard_map/ppermute | solution.py:56
  370.6 14.8 %shard_map.246 = (bf16[512,2048]{1,0:T(8,128)(2,1)}, bf16[512,2048]{1,0:T(8,128)(2,1)}, f32[512,1]{1,0:T(8,128)}, bf16[512,2048]{1,0:T(8,128)(2,1)}, bf16[512,20...) custom-call(bf16[128,2048]{1,0:T(8,128)(2,1)} %copy-done.22, bf16[128,2048]{1,0:T(8,128)(2,1)} %copy-done.42, ...), custom_call_target="tpu_custom_call" | custom-call | flops 6442450944 | bytes 25165824 | tf_op jit(solution)/shard_map/pallas_call | solution.py:347
  387.2 14.7 %shard_map.250 = (bf16[512,2048]{1,0:T(8,128)(2,1)}, bf16[512,2048]{1,0:T(8,128)(2,1)}, f32[512,1]{1,0:T(8,128)}, bf16[512,2048]{1,0:T(8,128)(2,1)}, bf16[512,20...) custom-call(bf16[128,2048]{1,0:T(8,128)(2,1)} %collective-permute-done.32.refs_0_, ...), custom_call_target="tpu_custom_call" | custom-call | flops 6442450944 | bytes 25165824 | tf_op jit(solution)/shard_map/pallas_call | solution.py:347
  403.3 14.7 %shard_map.248 = (bf16[512,2048]{1,0:T(8,128)(2,1)}, bf16[512,2048]{1,0:T(8,128)(2,1)}, f32[512,1]{1,0:T(8,128)}, bf16[512,2048]{1,0:T(8,128)(2,1)}, bf16[512,20...) custom-call(bf16[128,2048]{1,0:T(8,128)(2,1)} %collective-permute-done.27.refs_0_, ...), custom_call_target="tpu_custom_call" | custom-call | flops 6442450944 | bytes 25165824 | tf_op jit(solution)/shard_map/pallas_call | solution.py:347
  419.9 12.2 %collective-permute-done.54.refs_4_ = bf16[128,2048]{1,0:T(8,128)(2,1)S(1)} collective-permute-done((bf16[128,2048]{1,0:T(8,128)(2,1)S(1)}, bf16[128,2048]{1,0:T(8,128)(2,1)S(1)}, u32[]{:S(2)}, u32[]{:S(2)}) %collective-permute-start.54) | collective-permute-done | bytes 524320 | tf_op jit(solution)/shard_map/ppermute | solution.py:56
  436.6 11.2 %collective-permute-done.55.refs_2_ = bf16[128,2048]{1,0:T(8,128)(2,1)S(1)} collective-permute-done((bf16[128,2048]{1,0:T(8,128)(2,1)S(1)}, bf16[128,2048]{1,0:T(8,128)(2,1)S(1)}, u32[]{:S(2)}, u32[]{:S(2)}) %collective-permute-start.55) | collective-permute-done | bytes 524320 | tf_op jit(solution)/shard_map/ppermute | solution.py:56
  455.5 14.6 %shard_map.255 = (bf16[512,2048]{1,0:T(8,128)(2,1)}, bf16[512,2048]{1,0:T(8,128)(2,1)}, f32[512,1]{1,0:T(8,128)}, bf16[512,2048]{1,0:T(8,128)(2,1)}, bf16[512,20...) custom-call(bf16[128,2048]{1,0:T(8,128)(2,1)} %copy-done.48, ...), custom_call_target="tpu_custom_call" | custom-call | flops 6442450944 | bytes 25165824 | tf_op jit(solution)/shard_map/pallas_call | solution.py:347
  470.6 14.7 %shard_map.252 = (bf16[512,2048]{1,0:T(8,128)(2,1)}, bf16[512,2048]{1,0:T(8,128)(2,1)}, f32[512,1]{1,0:T(8,128)}, bf16[512,2048]{1,0:T(8,128)(2,1)}, bf16[512,20...) custom-call(bf16[128,2048]{1,0:T(8,128)(2,1)} %copy-done.43, bf16[128,2048]{1,0:T(8,128)(2,1)} %copy-done.45, ...), custom_call_target="tpu_custom_call" | custom-call | flops 6442450944 | bytes 25165824 | tf_op jit(solution)/shard_map/pallas_call | solution.py:347
  488.2 12.2 %collective-permute-done.59.refs_2_ = bf16[128,2048]{1,0:T(8,128)(2,1)S(1)} collective-permute-done((bf16[128,2048]{1,0:T(8,128)(2,1)S(1)}, bf16[128,2048]{1,0:T(8,128)(2,1)S(1)}, u32[]{:S(2)}, u32[]{:S(2)}) %collective-permute-start.59) | collective-permute-done | bytes 524320 | tf_op jit(solution)/shard_map/ppermute | solution.py:56
  506.6 14.5 %shard_map.260 = (bf16[512,2048]{1,0:T(8,128)(2,1)}, bf16[512,2048]{1,0:T(8,128)(2,1)}, f32[512,1]{1,0:T(8,128)}, bf16[512,2048]{1,0:T(8,128)(2,1)}, bf16[512,20...) custom-call(bf16[128,2048]{1,0:T(8,128)(2,1)} %collective-permute-done.50.refs_0_, ...), custom_call_target="tpu_custom_call" | custom-call | flops 6442450944 | bytes 25165824 | tf_op jit(solution)/shard_map/pallas_call | solution.py:347
  527.1 14.5 %shard_map.259 = (bf16[512,2048]{1,0:T(8,128)(2,1)}, bf16[512,2048]{1,0:T(8,128)(2,1)}, f32[512,1]{1,0:T(8,128)}, bf16[512,2048]{1,0:T(8,128)(2,1)}, bf16[512,20...) custom-call(bf16[128,2048]{1,0:T(8,128)(2,1)} %collective-permute-done.38.refs_0_, ...), custom_call_target="tpu_custom_call" | custom-call | flops 6442450944 | bytes 25165824 | tf_op jit(solution)/shard_map/pallas_call | solution.py:347
  568.1 14.6 %shard_map.266 = f32[512,2048]{1,0:T(8,128)} custom-call(bf16[512,512]{1,0:T(8,128)(2,1)} %get-tuple-element.186.refs_0_, bf16[512,512]{1,0:T(8,128)(2,1)} %get-tuple-element.187.refs_1_, bf16[512,512]{1,0:T(8,128)(2,1)} %get-tuple-element.188.refs_2_, bf16[512,512]{1,0:T(8,128)(2,1)} %get-tuple-element.189.refs_3_, ...), custom_call_target="tpu_custom_call" | custom-call | flops 8589934592 | bytes 25165824 | tf_op jit(solution)/shard_map/pallas_call | solution.py:435
  592.3 15.9 %shard_map.268.refs_16_ = f32[2048,2,512]{2,1,0:T(2,128)} custom-call(bf16[512,2048]{1,0:T(8,128)(2,1)} %get-tuple-element.223.refs_0_, bf16[512,2048]{1,0:T(8,128)(2,1)} %get-tuple-element.207.refs_1_, bf16[512,2048]{1,0:T(8,128)(2,1)} %get-tuple-element.208.refs_2_, bf16[512,2048]{1,0:T(8,128)(2,1)} %get-tuple-element.209.refs_3_, ...), custom_call_target="tpu_custom_call" | custom-call | flops 8589934592 | bytes 16777216 | tf_op jit(solution)/shard_map/pallas_call | solution.py:405
  608.3 10.2 %collective-permute-done.74.refs_3_ = bf16[128,2048]{1,0:T(8,128)(2,1)} collective-permute-done((bf16[128,2048]{1,0:T(8,128)(2,1)}, bf16[128,2048]{1,0:T(8,128)(2,1)}, u32[]{:S(2)}, u32[]{:S(2)}) %collective-permute-start.74) | collective-permute-done | bytes 524320 | tf_op jit(solution)/shard_map/ppermute | solution.py:56
  624.7 16.0 %shard_map.270 = f32[2048,2,512]{2,1,0:T(2,128)} custom-call(bf16[512,2048]{1,0:T(8,128)(2,1)} %get-tuple-element.223.refs_0_, bf16[512,2048]{1,0:T(8,128)(2,1)} %get-tuple-element.207.refs_1_, bf16[512,2048]{1,0:T(8,128)(2,1)} %get-tuple-element.208.refs_2_, bf16[512,2048]{1,0:T(8,128)(2,1)} %get-tuple-element.209.refs_3_, ...), custom_call_target="tpu_custom_call", output_to_operand_aliasing={{}: (16, {})} | custom-call | flops 8589934592 | bytes 16777216 | tf_op jit(solution)/shard_map/pallas_call | solution.py:405
  726.9 30.5 %collective-permute-done.93 = bf16[64,2048]{1,0:T(8,128)(2,1)} collective-permute-done((bf16[64,2048]{1,0:T(8,128)(2,1)}, bf16[64,2048]{1,0:T(8,128)(2,1)}, u32[]{:S(2)}, u32[]{:S(2)}) %collective-permute-start.93) | collective-permute-done | bytes 262176 | tf_op jit(solution)/shard_map/ppermute | solution.py:768
  765.0 12.9 %collective-permute-start.95 = (f32[2,2,4,128]{3,2,1,0:T(4,128)S(1)}, f32[2,2,4,128]{3,2,1,0:T(4,128)S(1)}, u32[]{:S(2)}, u32[]{:S(2)}) collective-permute-start(f32[2,2,4,128]{3,2,1,0:T(4,128)S(1)} %reverse_add_fusion), channel_id=1, source_target_pairs={{0,2},{1,3},{2,0},{3,1},{4,6},{5,7},{6,4},{7,5},{8,10},{9,11},{10,... | collective-permute-start | bytes 24584 | tf_op jit(solution)/shard_map/ppermute | solution.py:56
  777.9 13.3 %collective-permute-done.95 = f32[2,2,4,128]{3,2,1,0:T(4,128)S(1)} collective-permute-done((f32[2,2,4,128]{3,2,1,0:T(4,128)S(1)}, f32[2,2,4,128]{3,2,1,0:T(4,128)S(1)}, u32[]{:S(2)}, u32[]{:S(2)}) %collective-permute-start.95) | collective-permute-done | bytes 8224 | tf_op jit(solution)/shard_map/ppermute | solution.py:56
  859.6 9.8 %collective-permute-done.98.refs_4_ = bf16[64,2048]{1,0:T(8,128)(2,1)S(1)} collective-permute-done((bf16[64,2048]{1,0:T(8,128)(2,1)}, bf16[64,2048]{1,0:T(8,128)(2,1)S(1)}, u32[]{:S(2)}, u32[]{:S(2)}) %collective-permute-start.98) | collective-permute-done | bytes 262176 | tf_op jit(solution)/shard_map/ppermute | solution.py:56
  872.1 52.9 %collective-permute-done.87 = bf16[128,2048]{1,0:T(8,128)(2,1)} collective-permute-done((bf16[128,2048]{1,0:T(8,128)(2,1)}, bf16[128,2048]{1,0:T(8,128)(2,1)}, u32[]{:S(2)}, u32[]{:S(2)}) %collective-permute-start.87) | collective-permute-done | bytes 524320 | tf_op jit(solution)/shard_map/ppermute | solution.py:509
  (672 shorter events, 428.6 us)
Async XLA Ops:
  7.2 212.3 %all-gather.3.cloned.1.call-start = ((), (), s32[]{:S(2)}) async-start(), calls=%async_computation.9 | async-start | bytes 8650752 | tf_op jit(solution)/shard_map/all_gather | solution.py:539
  9.1 319.5 %all-gather.5.cloned.1.call-start = ((), (), s32[]{:S(2)}) async-start(), calls=%async_computation.10 | async-start | bytes 17301504 | tf_op jit(solution)/shard_map/all_gather | solution.py:540
  38.7 37.9 %collective-permute-start.3 = (bf16[128,2048]{1,0:T(8,128)(2,1)S(1)}, bf16[128,2048]{1,0:T(8,128)(2,1)S(1)}, u32[]{:S(2)}, u32[]{:S(2)}) collective-permute-start(bf16[128,2048]{1,0:T(8,128)(2,1)S(1)} %copy-done.24), channel_id=1, source_target_pairs={{0,4},{1,5},{2,6},{3,7},{4,0},{5,1},{6,2},{7,3},{8,12},{9,13},{10,... | collective-permute-start | bytes 1572872 | tf_op jit(solution)/shard_map/ppermute | solution.py:56
  39.2 37.4 %collective-permute-start.2 = (bf16[128,2048]{1,0:T(8,128)(2,1)S(1)}, bf16[128,2048]{1,0:T(8,128)(2,1)S(1)}, u32[]{:S(2)}, u32[]{:S(2)}) collective-permute-start(bf16[128,2048]{1,0:T(8,128)(2,1)S(1)} %copy-done.24), channel_id=1, source_target_pairs={{0,2},{1,3},{2,0},{3,1},{4,6},{5,7},{6,4},{7,5},{8,10},{9,11},{10,... | collective-permute-start | bytes 1572872 | tf_op jit(solution)/shard_map/ppermute | solution.py:56
  39.8 36.8 %collective-permute-start.1 = (bf16[512,768]{1,0:T(8,128)(2,1)S(1)}, bf16[512,768]{1,0:T(8,128)(2,1)S(1)}, u32[]{:S(2)}, u32[]{:S(2)}) collective-permute-start(bf16[512,768]{1,0:T(8,128)(2,1)S(1)} %bitcast.288), channel_id=1, source_target_pairs={{8,0},{16,8},{24,16},{9,1},{17,9},{25,17},{10,2},{18,10},{26,18},{... | collective-permute-start | bytes 2359304 | tf_op jit(solution)/shard_map/ppermute | solution.py:554
  230.2 55.3 %collective-permute-start.22 = (bf16[128,2048]{1,0:T(8,128)(2,1)S(1)}, bf16[128,2048]{1,0:T(8,128)(2,1)S(1)}, u32[]{:S(2)}, u32[]{:S(2)}) collective-permute-start(bf16[128,2048]{1,0:T(8,128)(2,1)S(1)} %multiply_convert_fusion.2.refs_0_), channel_id=1, source_target_pairs={{0,1},{1,0},{2,3},{3,2},{4,5},{5,4},{6,7},{7,6},{8,9},{9,8},{10,11... | collective-permute-start | bytes 1572872 | tf_op jit(solution)/shard_map/ppermute | solution.py:56
  230.5 41.3 %collective-permute-start.19 = (bf16[128,2048]{1,0:T(8,128)(2,1)S(1)}, bf16[128,2048]{1,0:T(8,128)(2,1)S(1)}, u32[]{:S(2)}, u32[]{:S(2)}) collective-permute-start(bf16[128,2048]{1,0:T(8,128)(2,1)S(1)} %multiply_convert_fusion.2.refs_0_), channel_id=1, source_target_pairs={{0,4},{1,5},{2,6},{3,7},{4,0},{5,1},{6,2},{7,3},{8,12},{9,13},{10,... | collective-permute-start | bytes 1572872 | tf_op jit(solution)/shard_map/ppermute | solution.py:56
  232.2 41.0 %collective-permute-start.18 = (bf16[128,2048]{1,0:T(8,128)(2,1)S(1)}, bf16[128,2048]{1,0:T(8,128)(2,1)S(1)}, u32[]{:S(2)}, u32[]{:S(2)}) collective-permute-start(bf16[128,2048]{1,0:T(8,128)(2,1)S(1)} %multiply_convert_fusion.2.refs_0_), channel_id=1, source_target_pairs={{0,2},{1,3},{2,0},{3,1},{4,6},{5,7},{6,4},{7,5},{8,10},{9,11},{10,... | collective-permute-start | bytes 1572872 | tf_op jit(solution)/shard_map/ppermute | solution.py:56
  345.8 41.3 %collective-permute-start.42 = (bf16[128,2048]{1,0:T(8,128)(2,1)}, bf16[128,2048]{1,0:T(8,128)(2,1)S(1)}, u32[]{:S(2)}, u32[]{:S(2)}) collective-permute-start(bf16[128,2048]{1,0:T(8,128)(2,1)} %collective-permute-done.38.refs_0_), channel_id=1, source_target_pairs={{0,4},{1,5},{2,6},{3,7},{4,0},{5,1},{6,2},{7,3},{8,12},{9,13},{10,... | collective-permute-start | bytes 1572872 | tf_op jit(solution)/shard_map/ppermute | solution.py:56
  348.4 38.7 %collective-permute-start.45 = (bf16[128,2048]{1,0:T(8,128)(2,1)}, bf16[128,2048]{1,0:T(8,128)(2,1)}, u32[]{:S(2)}, u32[]{:S(2)}) collective-permute-start(bf16[128,2048]{1,0:T(8,128)(2,1)} %copy-done.44), channel_id=1, source_target_pairs={{0,1},{1,0},{2,3},{3,2},{4,5},{5,4},{6,7},{7,6},{8,9},{9,8},{10,11... | collective-permute-start | bytes 1572872 | tf_op jit(solution)/shard_map/ppermute | solution.py:56
  401.9 50.2 %collective-permute-start.57 = (bf16[512,2048]{1,0:T(8,128)(2,1)}, bf16[512,2048]{1,0:T(8,128)(2,1)}, u32[]{:S(2)}, u32[]{:S(2)}) collective-permute-start(bf16[512,2048]{1,0:T(8,128)(2,1)} %get-tuple-element.167), channel_id=1, source_target_pairs={{0,1},{1,0},{2,3},{3,2},{4,5},{5,4},{6,7},{7,6},{8,9},{9,8},{10,11... | collective-permute-start | bytes 6291464 | tf_op jit(solution)/shard_map/ppermute | solution.py:56
  402.5 52.8 %collective-permute-start.50 = (bf16[128,2048]{1,0:T(8,128)(2,1)}, bf16[128,2048]{1,0:T(8,128)(2,1)}, u32[]{:S(2)}, u32[]{:S(2)}) collective-permute-start(bf16[128,2048]{1,0:T(8,128)(2,1)} %collective-permute-done.38.refs_0_), channel_id=1, source_target_pairs={{0,1},{1,0},{2,3},{3,2},{4,5},{5,4},{6,7},{7,6},{8,9},{9,8},{10,11... | collective-permute-start | bytes 1572872 | tf_op jit(solution)/shard_map/ppermute | solution.py:56
  402.6 68.0 %collective-permute-start.39 = (bf16[512,2048]{1,0:T(8,128)(2,1)}, bf16[512,2048]{1,0:T(8,128)(2,1)}, u32[]{:S(2)}, u32[]{:S(2)}) collective-permute-start(bf16[512,2048]{1,0:T(8,128)(2,1)} %get-tuple-element.155), channel_id=1, source_target_pairs={{0,1},{1,0},{2,3},{3,2},{4,5},{5,4},{6,7},{7,6},{8,9},{9,8},{10,11... | collective-permute-start | bytes 6291464 | tf_op jit(solution)/shard_map/ppermute | solution.py:56
  455.3 51.3 %collective-permute-start.49 = (bf16[512,2048]{1,0:T(8,128)(2,1)}, bf16[512,2048]{1,0:T(8,128)(2,1)}, u32[]{:S(2)}, u32[]{:S(2)}) collective-permute-start(bf16[512,2048]{1,0:T(8,128)(2,1)} %get-tuple-element.161), channel_id=1, source_target_pairs={{0,1},{1,0},{2,3},{3,2},{4,5},{5,4},{6,7},{7,6},{8,9},{9,8},{10,11... | collective-permute-start | bytes 6291464 | tf_op jit(solution)/shard_map/ppermute | solution.py:56
  470.1 55.7 %collective-permute-start.62 = (bf16[512,2048]{1,0:T(8,128)(2,1)}, bf16[512,2048]{1,0:T(8,128)(2,1)S(1)}, u32[]{:S(2)}, u32[]{:S(2)}) collective-permute-start(bf16[512,2048]{1,0:T(8,128)(2,1)} %get-tuple-element.173), channel_id=1, source_target_pairs={{0,1},{1,0},{2,3},{3,2},{4,5},{5,4},{6,7},{7,6},{8,9},{9,8},{10,11... | collective-permute-start | bytes 6291464 | tf_op jit(solution)/shard_map/ppermute | solution.py:56
  488.1 73.7 %collective-permute-start.58 = (bf16[512,2048]{1,0:T(8,128)(2,1)}, bf16[512,2048]{1,0:T(8,128)(2,1)}, u32[]{:S(2)}, u32[]{:S(2)}) collective-permute-start(bf16[512,2048]{1,0:T(8,128)(2,1)} %get-tuple-element.169), channel_id=1, source_target_pairs={{0,1},{1,0},{2,3},{3,2},{4,5},{5,4},{6,7},{7,6},{8,9},{9,8},{10,11... | collective-permute-start | bytes 6291464 | tf_op jit(solution)/shard_map/ppermute | solution.py:56
  522.3 40.8 %collective-permute-start.63 = (bf16[512,2048]{1,0:T(8,128)(2,1)}, bf16[512,2048]{1,0:T(8,128)(2,1)}, u32[]{:S(2)}, u32[]{:S(2)}) collective-permute-start(bf16[512,2048]{1,0:T(8,128)(2,1)} %get-tuple-element.177), channel_id=1, source_target_pairs={{0,1},{1,0},{2,3},{3,2},{4,5},{5,4},{6,7},{7,6},{8,9},{9,8},{10,11... | collective-permute-start | bytes 6291464 | tf_op jit(solution)/shard_map/ppermute | solution.py:56
  549.1 91.6 %collective-permute-start.70 = (bf16[128,2048]{1,0:T(8,128)(2,1)}, bf16[128,2048]{1,0:T(8,128)(2,1)}, u32[]{:S(2)}, u32[]{:S(2)}) collective-permute-start(bf16[128,2048]{1,0:T(8,128)(2,1)} %copy-done.16), channel_id=1, source_target_pairs={{0,16},{8,24},{16,0},{24,8},{1,17},{9,25},{17,1},{25,9},{2,18},{10... | collective-permute-start | bytes 1572872 | tf_op jit(solution)/shard_map/ppermute | solution.py:509
  567.4 83.0 %collective-permute-start.64 = (bf16[256,2048]{1,0:T(8,128)(2,1)}, bf16[256,2048]{1,0:T(8,128)(2,1)S(1)}, u32[]{:S(2)}, u32[]{:S(2)}) collective-permute-start(bf16[256,2048]{1,0:T(8,128)(2,1)} %get-tuple-element.178), channel_id=1, source_target_pairs={{0,4},{1,5},{2,6},{3,7},{4,0},{5,1},{6,2},{7,3},{8,12},{9,13},{10,... | collective-permute-start | bytes 3145736 | tf_op jit(solution)/shard_map/ppermute | solution.py:56
  582.7 67.7 %collective-permute-start.65 = (bf16[256,2048]{1,0:T(8,128)(2,1)}, bf16[256,2048]{1,0:T(8,128)(2,1)}, u32[]{:S(2)}, u32[]{:S(2)}) collective-permute-start(bf16[256,2048]{1,0:T(8,128)(2,1)} %copy-done.17), channel_id=1, source_target_pairs={{0,2},{1,3},{2,0},{3,1},{4,6},{5,7},{6,4},{7,5},{8,10},{9,11},{10,... | collective-permute-start | bytes 3145736 | tf_op jit(solution)/shard_map/ppermute | solution.py:56
  657.1 136.3 %all-to-all-start.7 = ((f32[32,1,1088]{2,1,0:T(1,128)}), f32[32,1,1088]{2,1,0:T(1,128)S(1)}, u32[]{:S(2)}, u32[]{:S(2)}) async-start(f32[32,1,1088]{2,1,0:T(1,128)} %reshape.712), calls=%async_computation.7 | async-start | bytes 294912 | tf_op jit(solution)/shard_map/all_to_all | solution.py:756
  699.0 58.4 %collective-permute-start.93 = (bf16[64,2048]{1,0:T(8,128)(2,1)}, bf16[64,2048]{1,0:T(8,128)(2,1)}, u32[]{:S(2)}, u32[]{:S(2)}) collective-permute-start(bf16[64,2048]{1,0:T(8,128)(2,1)} %get-tuple-element.289), channel_id=1, source_target_pairs={{0,3},{1,7},{2,11},{3,15},{4,19},{5,23},{6,27},{7,31},{8,0},{9,4},... | collective-permute-start | bytes 786440 | tf_op jit(solution)/shard_map/ppermute | solution.py:768
  702.4 55.0 %collective-permute-start.92 = (bf16[64,2048]{1,0:T(8,128)(2,1)}, bf16[64,2048]{1,0:T(8,128)(2,1)}, u32[]{:S(2)}, u32[]{:S(2)}) collective-permute-start(bf16[64,2048]{1,0:T(8,128)(2,1)} %get-tuple-element.290), channel_id=1, source_target_pairs={{0,2},{1,6},{2,10},{3,14},{4,18},{5,22},{6,26},{7,30},{8,3},{9,7},... | collective-permute-start | bytes 786440 | tf_op jit(solution)/shard_map/ppermute | solution.py:768
  703.1 54.3 %collective-permute-start.91 = (bf16[64,2048]{1,0:T(8,128)(2,1)S(1)}, bf16[64,2048]{1,0:T(8,128)(2,1)}, u32[]{:S(2)}, u32[]{:S(2)}) collective-permute-start(bf16[64,2048]{1,0:T(8,128)(2,1)S(1)} %get-tuple-element.291), channel_id=1, source_target_pairs={{0,1},{1,5},{2,9},{3,13},{4,17},{5,21},{6,25},{7,29},{8,2},{9,6},{... | collective-permute-start | bytes 786440 | tf_op jit(solution)/shard_map/ppermute | solution.py:768
  707.5 94.9 %collective-permute-start.85 = (bf16[512,2048]{1,0:T(8,128)(2,1)S(1)}, bf16[512,2048]{1,0:T(8,128)(2,1)}, u32[]{:S(2)}, u32[]{:S(2)}) collective-permute-start(bf16[512,2048]{1,0:T(8,128)(2,1)S(1)} %get-tuple-element.233), channel_id=1, source_target_pairs={{0,2},{1,3},{2,0},{3,1},{4,6},{5,7},{6,4},{7,5},{8,10},{9,11},{10,... | collective-permute-start | bytes 6291464 | tf_op jit(solution)/shard_map/ppermute | solution.py:56
  724.2 78.1 %collective-permute-start.86 = (bf16[512,2048]{1,0:T(8,128)(2,1)}, bf16[512,2048]{1,0:T(8,128)(2,1)}, u32[]{:S(2)}, u32[]{:S(2)}) collective-permute-start(bf16[512,2048]{1,0:T(8,128)(2,1)} %get-tuple-element.235), channel_id=1, source_target_pairs={{0,4},{1,5},{2,6},{3,7},{4,0},{5,1},{6,2},{7,3},{8,12},{9,13},{10,... | collective-permute-start | bytes 6291464 | tf_op jit(solution)/shard_map/ppermute | solution.py:56
  836.9 93.6 %all-to-all-start.5 = ((bf16[32,64,512]{2,1,0:T(8,128)(2,1)}), bf16[32,64,512]{2,1,0:T(8,128)(2,1)}, u32[]{:S(2)}, u32[]{:S(2)}) async-start(bf16[32,64,512]{2,1,0:T(8,128)(2,1)} %bitcast.292), calls=%async_computation.5 | async-start | bytes 4194304 | tf_op jit(solution)/shard_map/all_to_all | solution.py:816
  844.2 80.9 %collective-permute-start.87 = (bf16[128,2048]{1,0:T(8,128)(2,1)}, bf16[128,2048]{1,0:T(8,128)(2,1)}, u32[]{:S(2)}, u32[]{:S(2)}) collective-permute-start(bf16[128,2048]{1,0:T(8,128)(2,1)} %get-tuple-element.237), channel_id=1, source_target_pairs={{0,16},{8,24},{16,0},{24,8},{1,17},{9,25},{17,1},{25,9},{2,18},{10... | collective-permute-start | bytes 1572872 | tf_op jit(solution)/shard_map/ppermute | solution.py:509
  846.8 78.3 %collective-permute-start.88 = (bf16[128,2048]{1,0:T(8,128)(2,1)}, bf16[128,2048]{1,0:T(8,128)(2,1)}, u32[]{:S(2)}, u32[]{:S(2)}) collective-permute-start(bf16[128,2048]{1,0:T(8,128)(2,1)} %get-tuple-element.238), channel_id=1, source_target_pairs={{0,8},{8,16},{16,24},{24,0},{1,9},{9,17},{17,25},{25,1},{2,10},{10... | collective-permute-start | bytes 1572872 | tf_op jit(solution)/shard_map/ppermute | solution.py:509
  848.3 76.8 %collective-permute-start.89 = (bf16[128,2048]{1,0:T(8,128)(2,1)}, bf16[128,2048]{1,0:T(8,128)(2,1)}, u32[]{:S(2)}, u32[]{:S(2)}) collective-permute-start(bf16[128,2048]{1,0:T(8,128)(2,1)} %get-tuple-element.239), channel_id=1, source_target_pairs={{0,24},{8,0},{16,8},{24,16},{1,25},{9,1},{17,9},{25,17},{2,26},{10... | collective-permute-start | bytes 1572872 | tf_op jit(solution)/shard_map/ppermute | solution.py:509
  870.9 56.7 %collective-permute-start.100 = (bf16[128,2048]{1,0:T(8,128)(2,1)S(1)}, bf16[128,2048]{1,0:T(8,128)(2,1)S(1)}, u32[]{:S(2)}, u32[]{:S(2)}) collective-permute-start(bf16[128,2048]{1,0:T(8,128)(2,1)S(1)} %get-tuple-element.245), channel_id=1, source_target_pairs={{0,2},{1,3},{2,0},{3,1},{4,6},{5,7},{6,4},{7,5},{8,10},{9,11},{10,... | collective-permute-start | bytes 1572872 | tf_op jit(solution)/shard_map/ppermute | solution.py:56
  870.9 56.7 %collective-permute-start.101 = (bf16[128,2048]{1,0:T(8,128)(2,1)S(1)}, bf16[128,2048]{1,0:T(8,128)(2,1)S(1)}, u32[]{:S(2)}, u32[]{:S(2)}) collective-permute-start(bf16[128,2048]{1,0:T(8,128)(2,1)S(1)} %get-tuple-element.246), channel_id=1, source_target_pairs={{0,4},{1,5},{2,6},{3,7},{4,0},{5,1},{6,2},{7,3},{8,12},{9,13},{10,... | collective-permute-start | bytes 1572872 | tf_op jit(solution)/shard_map/ppermute | solution.py:56
  (171 other events, 3376.7 us)
Sparse Core Ops, SparseCore 0:
  10.9 103.7 all-gather.2
  117.5 149.6 all-gather.4

commit v2 on v1

--- a/solution.py
+++ b/solution.py
@@ -470,6 +470,22 @@
     return jnp.moveaxis(y, 0, n - 1).reshape(x.shape)
 
 
+def sum_to_owners(x, planes, size, plane, place):
+    n, _, rows = x.shape
+    for axis, count, me in (("seq", size, place), ("fsdp", planes, plane)):
+        outer = planes if axis == "seq" else 1
+        b = 1
+        while b < count:
+            y = x.reshape(n, outer, -1, 2, rows)
+            high = (me & b) != 0
+            mine = jnp.where(high, y[:, :, :, 1], y[:, :, :, 0])
+            theirs = jnp.where(high, y[:, :, :, 0], y[:, :, :, 1])
+            x = mine + lax.ppermute(theirs, axis, [(i, i ^ b) for i in range(count)])
+            x = x.reshape(n, -1, rows)
+            b *= 2
+    return x[:, 0]
+
+
 def per_device(
     tokens,
     segments,
@@ -519,23 +535,6 @@
     w_send = w_low.reshape(RW, 3, S, CW).transpose(2, 0, 1, 3).reshape(S, RW, 3 * CW)
     w_mine = lax.all_to_all(w_send, "seq", split_axis=0, concat_axis=0, tiled=True)
     w_mine = w_mine.reshape(S * RW, 3 * CW)
-    gains = jnp.stack([attn_gain, q_gain, k_gain, ffn_gain])
-    small = [gains.astype(BF16), router.T.astype(BF16), segments.astype(BF16)]
-    sizes = [4 * RW, experts * RW, R]
-    pad = jnp.zeros((-sum(sizes) % 128,), BF16)
-    small = jnp.concatenate([a.reshape(-1) for a in small] + [pad]).reshape(1, -1, 128)
-    small = after(small, w_mine)
-    small = jnp.broadcast_to(small, (N,) + small.shape[1:])
-    small = lax.all_to_all(small, BOTH, split_axis=0, concat_axis=0, tiled=True).reshape(N, -1)
-    parts, at = [], 0
-    for n in sizes:
-        parts.append(small[:, at : at + n])
-        at += n
-    gains_all = parts[0].reshape(N, 4, RW).transpose(1, 0, 2).reshape(4, D).astype(F32)
-    ga, gq, gk, gf = [gains_all[i] for i in range(4)]
-    router_t = parts[1].reshape(N, experts, RW).transpose(1, 0, 2).reshape(experts, D)
-    segment_all = lax.dynamic_slice(parts[2].astype(F32), (me_f * S, 0), (S, R))
-
     wo_all = lax.all_gather(w_out.astype(BF16), BOTH, axis=0, tiled=True)
     c_all = lax.all_gather(after(out_grad, w_mine), BOTH, axis=0, tiled=True)
     expert = me // SPLIT
@@ -556,8 +555,8 @@
         downs.append(down)
         if k == 0:
             keys = list(x_first)
-            up, down, small, *got = lax.optimization_barrier(
-                (up, down, small, *[x_first[m][0] for m in keys])
+            up, down, *got = lax.optimization_barrier(
+                (up, down, *[x_first[m][0] for m in keys])
             )
             x_first = {m: [a] for m, a in zip(keys, got)}
             x_mine = gather_rest(x_first, S)
@@ -575,6 +574,23 @@
         else:
             up, down = lax.optimization_barrier((up, down))
     x_seq = jnp.concatenate(in_order(x_mine) + in_order(x_other)).astype(F32)
+    gains = jnp.stack([attn_gain, q_gain, k_gain, ffn_gain])
+    small = [gains.astype(BF16), router.T.astype(BF16), segments.astype(BF16)]
+    sizes = [4 * RW, experts * RW, R]
+    pad = jnp.zeros((-sum(sizes) % 128,), BF16)
+    small = jnp.concatenate([a.reshape(-1) for a in small] + [pad]).reshape(1, -1, 128)
+    small = after(small, ups[min(1, F - 2)])
+    small = jnp.broadcast_to(small, (N,) + small.shape[1:])
+    small = lax.all_to_all(small, BOTH, split_axis=0, concat_axis=0, tiled=True).reshape(N, -1)
+    parts, at = [], 0
+    for n in sizes:
+        parts.append(small[:, at : at + n])
+        at += n
+    gains_all = parts[0].reshape(N, 4, RW).transpose(1, 0, 2).reshape(4, D).astype(F32)
+    ga, gq, gk, gf = [gains_all[i] for i in range(4)]
+    router_t = parts[1].reshape(N, experts, RW).transpose(1, 0, 2).reshape(experts, D)
+    segment_all = lax.dynamic_slice(parts[2].astype(F32), (me_f * S, 0), (S, R))
+
     x_inverse = inverse_rms(x_seq)
     a_seq = after((x_seq * x_inverse * ga).astype(BF16), gu_low, down_low)
     cols = 3 * CW
@@ -649,7 +665,7 @@
     tick = {call: t for t, call in enumerate(calls)}
     before = {t: [] for t in range(len(calls) + 4)}
     for i, j in enumerate(chunks):
-        early = 2 + (j == last_chunk)
+        early = 1 if j == last_chunk else 0
         t = 2 * i
         before[max(t - 2 - early, 0)].append(m_far[j])
         before[max(t - 1 - early, 0)] += flat(first[j])
@@ -707,17 +723,15 @@
             if j == last_chunk:
                 ties = {n: lambda n=n: last_flush(len(calls), n) for n in (0, 1)}
 
-            group = (dmx_sides[j, 0], exchange(dmx_sides[j, 1], 1, S), 1, 0, chunks.index(j) % 2)
-            [total] = scatter_sum([group], S, R, [BF16 if j else F32], hold, ties)
+            way = chunks.index(j) % 2
+            both_sums = [(dmx_sides[j, 0], exchange(dmx_sides[j, 1], 1, S), 1, 0, way)]
+            both_sums.append((mix_sides.pop((j, 0)), mix_got.pop(j), 1, 0, 1 - way))
+            total, mix = scatter_sum(both_sums, S, R, [BF16 if j else F32, BF16], hold, ties)
+            mix_done[j] = shift_back(mix, j) if j else mix
+            before[min(given + 5, len(calls) + 3)].append(mix_done[j])
             finished[j] = shift_back(total, j) if j else total
             last_sum = total
-            if F > 4:
-                group = (mix_sides.pop((j, 0)), mix_got.pop(j), 1, 0, chunks.index(j) % 2)
-                [mix_done[j]] = scatter_sum([group], S, R, [BF16])
-                before[min(t + 4, len(calls) + 3)].append(mix_done[j])
     dots = {j: jnp.concatenate([dots[j, 0], dots[j, 1]]).reshape(S, R) for j in chunks}
-    if F <= 4:
-        mix_groups = [(mix_sides[j, 0], mix_got[j], 1, 0, i % 2) for i, j in enumerate(chunks)]
     dots = [dots[j] for j in range(F)]
     finished = [finished[j] for j in range(F)]
     dmx_total = finished[0]
@@ -736,6 +750,7 @@
         b *= 2
     dots = dots.reshape(N, R)
     dots = lax.all_to_all(dots, BOTH, split_axis=0, concat_axis=0, tiled=True)
+    dots = after(dots, gate_up_grad)
     grad_probs = jnp.sum(dots.reshape(experts, SPLIT, R), axis=1).T * named
     grad_logits = expert_probs * (
         grad_probs - jnp.sum(expert_probs * grad_probs, axis=-1, keepdims=True)
@@ -753,32 +768,23 @@
     )
     ffn_part = jnp.sum(grad_mixed * middle * mid_inv, axis=0)
     early = jnp.concatenate([router_part, ffn_part[None]]).reshape(experts + 1, N, RW)
-    early = lax.all_to_all(early.transpose(1, 0, 2), BOTH, split_axis=0, concat_axis=0, tiled=True)
-    early = jnp.sum(early, axis=0)
+    early = sum_to_owners(early, F, S, me_f, me_s)
     router_grad = early[:experts].T
     ffn_grad = early[experts]
 
     proj_low = grad_middle.astype(BF16)
     grad_proj = sequence_rows(proj_low)
-    out_part = rows_by_rows(attended, grad_proj).astype(BF16).reshape(F, RW, D)
-    out_grad_total = None
-    for d in range(F):
-        chunk = lax.dynamic_index_in_dim(out_part, (me_f + d) % F, 0, keepdims=False)
-        pairs = [(f * S + s, F * s + (f + d) % F) for f in range(F) for s in range(S)]
-        got = lax.ppermute(chunk, BOTH, pairs).astype(F32)
-        out_grad_total = got if d == 0 else out_grad_total + got
-    def hold_mix(level, sums):
-        return [after(a, grad_proj) for a in sums] if level == 1 else sums
-
+    out_part = rows_by_rows(attended, grad_proj).astype(BF16)
+    out_sum = lax.psum_scatter(out_part, "fsdp", scatter_dimension=0, tiled=True)
+    pairs = [(f * S + s, F * s + f) for f in range(F) for s in range(S)]
+    out_grad_total = lax.ppermute(out_sum, BOTH, pairs).astype(F32)
     output = middle
-    if F <= 4:
-        mix_done = dict(zip(chunks, scatter_sum(mix_groups, S, R, [BF16] * F, hold_mix)))
     for j in chunks:
-        output = output + (shift_back(mix_done[j], j) if j else mix_done[j]).astype(F32)
+        output = output + mix_done[j].astype(F32)
     output = output.astype(BF16)
 
     wo_rows = lax.dynamic_slice(wo_all, (me_s * CW, 0), (CW, D))
-    grad_heads = times_transposed(after(grad_proj, out_part), wo_rows).astype(BF16).reshape(L, HL, HW)
+    grad_heads = times_transposed(after(grad_proj, out_part, early, *mix_done.values()), wo_rows).astype(BF16).reshape(L, HL, HW)
     grad_p = jnp.einsum("thd,uhd->htu", grad_heads, v_heads, preferred_element_type=F32)
     delta = jnp.sum(probs * grad_p, axis=-1, keepdims=True)
     grad_s = (probs * (grad_p - delta)).astype(BF16)
@@ -792,13 +798,27 @@
     dq = dq * gq_mine
     dk = dk * gk_mine
     means = jnp.stack([jnp.sum(dq * q_proj, 1), jnp.sum(dk * k_proj, 1)])
-    means = seq_sum(after(means, out_grad_total)) / D
+    means = seq_sum(means) / D
     dqp = q_inv * dq - q_proj * q_inv**3 * means[0][:, None]
     dkp = k_inv * dk - k_proj * k_inv**3 * means[1][:, None]
     dv_low = dv.reshape(L, CW).astype(BF16)
     dqk = jnp.concatenate([dqp.astype(BF16), dkp.astype(BF16)], axis=1)
-    dqk = after(dqk, *mix_done.values())
-    dqkv = jnp.concatenate([dqk, dv_low], axis=1)
+    v_part = rows_by_rows(a_seq, dv_low).astype(BF16)
+    v_sum = lax.psum_scatter(v_part, "fsdp", scatter_dimension=0, tiled=True)
+    qk_part = rows_by_rows(a_seq, dqk).astype(BF16).reshape(N, RW, 2 * CW)
+    qk_got = lax.all_to_all(qk_part, BOTH, split_axis=0, concat_axis=0, tiled=True)
+    qk_parts = qk_got.reshape(F, S, RW, 2 * CW)
+    qk_all = qk_parts[0].astype(F32)
+    for f in range(1, F):
+        qk_all = qk_all + qk_parts[f].astype(F32)
+    qk_sum = [
+        qk_all[:, :, i * CW : (i + 1) * CW].transpose(1, 0, 2).reshape(RW, D) for i in range(2)
+    ]
+    v_got = lax.all_to_all(
+        after(v_sum, qk_got).reshape(S, RW, CW), "seq", split_axis=0, concat_axis=0, tiled=True
+    )
+    w_sum = [qk_sum[0], qk_sum[1], v_got.transpose(1, 0, 2).reshape(RW, D).astype(F32)]
+    dqkv = jnp.concatenate([after(dqk, qk_part), dv_low], axis=1)
     x_scaled = x_seq * x_inverse
     da_keep = times_transposed(dqkv[: L // 2], w_cols)
     da_give = times_transposed(dqkv[L // 2 :], w_cols)
@@ -810,13 +830,6 @@
     da_mine = jnp.concatenate(
         scatter_sum([(da_keep, da_got, 2, h, h) for h in range(2)], S, unit, [F32] * 2)
     )
-    w_sums = []
-    for part, n in ((dv_low, 1), (dqk, 2)):
-        w_part = rows_by_rows(a_seq, part).astype(BF16).reshape(N, RW, n * CW)
-        w_got = lax.all_to_all(w_part, BOTH, split_axis=0, concat_axis=0, tiled=True)
-        w_sum = jnp.sum(w_got.reshape(F, S, RW, n, CW).astype(F32), axis=0)
-        w_sums.append(w_sum.transpose(2, 1, 0, 3).reshape(n, RW, D))
-    w_sum = [w_sums[1][0], w_sums[1][1], w_sums[0][0]]
     late = jnp.stack(
         [
             attn_part,

time: 970 us -> 884 us (0.911)
  waiting for transfers between devices: 358 us -> 273 us
  blocking collectives: 19.4 us -> 30.8 us
    ppermute x6, waiting for transfers between devices: 56.7 us -> 10 us  [shift_back(): return lax.ppermute(x, 'fsdp', [(i, (i + j) % F) for i in range(F)])]
    ppermute x83, waiting for transfers between devices: 146 us -> 125 us  [exchange(): return lax.ppermute(x, 'seq', [(i, i ^ mask) for i in range(size)])]
    ppermute x4 -> x6, waiting for transfers between devices: 30.5 us -> 44.3 us  [the longest x5 44.3 us: sum_to_owners(): x = mine + lax.ppermute(theirs, axis, [(i, i ^ b) for i in range(count)])]
    all_to_all x1, waiting for transfers between devices: 12.9 us -> 0.01 us  [per_device(): lax.all_to_all(small, BOTH, split_axis=0, concat_axis=0, tiled=True)]
    all_to_all x0 -> x1, blocking collectives: none -> 11.4 us  [per_device(): late = lax.all_to_all(late, BOTH, split_axis=0, concat_axis=0, tiled=True)]
    ppermute x3, waiting for transfers between devices: 37 us -> 25.7 us  [per_device(): up = lax.ppermute(up, 'fsdp', [(i, i + 1) for i in range(F - 1)])]
    all_to_all x4 -> x2, starting transfers between devices: 18.3 us -> 22.9 us  [the longest x1 19.4 us: per_device(): lax.all_to_all(after(v_sum, qk_got).reshape(S, RW, CW), 'seq', split_axis...]
    unnamed x221 -> x212, local copies, waits for them, and re-layouts: 46 us -> 47.7 us
  transfers between devices with their start and end apart: 112 -> 114, of which waited for: 39 -> 36; matrix products, arithmetic and copies ran while one was open for 19% -> 17% of each run, Pallas kernels for 18% -> 20%
where the time goes in v2:
time: 884 us; the launch traced here: 875 us
  waiting for transfers between devices  273 us (31%)
  Pallas kernels  202 us (23%)
  starting transfers between devices  149 us (17%)
  local copies, waits for them, and re-layouts  73.4 us (8%)
  other arithmetic  68 us (8%)
  matrix products  62.4 us (7%)
  blocking collectives  30.8 us (3%)
  between operations  16.3 us (2%)
    ppermute x83, waiting for transfers between devices, exchange(): return lax.ppermute(x, 'seq', [(i, i ^ mask) for i in range(size)])  125 us
    pallas_call x8, Pallas kernels, expert_rows(): pl.pallas_call(kernel, out_shape=[sds((rows, width), BF16), sds((rows, wi...  117 us
    ppermute x83, starting transfers between devices, exchange(): return lax.ppermute(x, 'seq', [(i, i ^ mask) for i in range(size)])  58.3 us
    unnamed x212, local copies, waits for them, and re-layouts  47.7 us
    ppermute x3, waiting for transfers between devices, shift_in(): return lax.ppermute(x, 'fsdp', [((i + j) % F, i) for i in range(F)])  44.7 us
    ppermute x5, waiting for transfers between devices, sum_to_owners(): x = mine + lax.ppermute(theirs, axis, [(i, i ^ b) for i in range(count)])  44.3 us
    pallas_call x15, Pallas kernels, add_blocks(): pl.pallas_call(kernel, grid=(1,), out_shape=shapes, in_specs=specs, out_s...  37.7 us
    pallas_call x2, Pallas kernels, gate_up_weights(): pl.pallas_call(kernel, grid=(steps,), out_shape=jax.ShapeDtypeStruct((wid...  31.6 us
  transfers between devices with their start and end apart: 114, of which 36 were waited for; matrix products, arithmetic and copies ran while one was open for 17% of the time, Pallas kernels for 20%

profile of v2, /device:TPU:0, one launch (start us, length us, event | category | flops | bytes accessed | tf_op | source)
XLA Modules:
  0.0 874.8 jit_solution(17947695824901159415)
XLA Ops:
  15.6 19.4 %all_to_all.48 = bf16[8,64,768]{2,1,0:T(8,128)(2,1)S(1)} all-to-all(bf16[8,64,768]{2,1,0:T(8,128)(2,1)S(1)} %reshape.775), channel_id=1, replica_groups=mesh['fsdp'=4,'seq'=8] {'seq'}, dimensions={0} | all-to-all | bytes 1572864 | tf_op jit(solution)/shard_map/all_to_all | solution.py:536
  46.5 11.9 %collective-permute-done.3 = bf16[128,2048]{1,0:T(8,128)(2,1)S(1)} collective-permute-done((bf16[128,2048]{1,0:T(8,128)(2,1)S(1)}, bf16[128,2048]{1,0:T(8,128)(2,1)S(1)}, u32[]{:S(2)}, u32[]{:S(2)}) %collective-permute-start.3) | collective-permute-done | bytes 524320 | tf_op jit(solution)/shard_map/ppermute | solution.py:56
  89.3 17.4 %collective-permute-done.4 = bf16[512,768]{1,0:T(8,128)(2,1)S(1)} collective-permute-done((bf16[512,768]{1,0:T(8,128)(2,1)}, bf16[512,768]{1,0:T(8,128)(2,1)S(1)}, u32[]{:S(2)}, u32[]{:S(2)}) %collective-permute-start.4) | collective-permute-done | bytes 786464 | tf_op jit(solution)/shard_map/ppermute | solution.py:552
  109.1 12.0 %all-to-all-start.1 = ((bf16[32,11,128]{2,1,0:T(8,128)(2,1)}), bf16[32,11,128]{2,1,0:T(8,128)(2,1)S(1)}, u32[]{:S(2)}, u32[]{:S(2)}) async-start(bf16[32,11,128]{2,1,0:T(8,128)(2,1)} %broadcast_in_dim.29), calls=%async_computation.1 | async-start | bytes 262144 | tf_op jit(solution)/shard_map/all_to_all | solution.py:584
  187.1 10.0 %fusion.78 = (f32[2,1024]{1,0:T(2,128)S(1)}, f32[2,1024,1024]{1,2,0:T(8,128)}) fusion(pred[1024,1024]{0,1:T(8,128)(4,1)} %compare_and_fusion, bf16[1024,2,64]{2,0,1:T(8,128)(2,1)S(1)} %get-tuple-element.305, bf16[1024,2,64]{2,0,1:T(8,128)(2,1)} %get-tuple-element.306, bf16[1024,2,64]{2,0,1:T(8,128)(2,1)} %get-tuple-element.291, ...), kind=kOutput, calls=%fused_computation.279 | convolution fusion | flops 549454848 | bytes 10493952 | tf_op jit(solution)/shard_map/sub | solution.py:631
  208.8 15.0 %all-to-all-done.2 = bf16[8,128,256]{2,1,0:T(8,128)(2,1)S(1)} async-done(((bf16[8,128,256]{2,1,0:T(8,128)(2,1)}), bf16[8,128,256]{2,1,0:T(8,128)(2,1)S(1)}, u32[]{:S(2)}, u32[]{:S(2)}) %all-to-all-start.2) | async-done | bytes 524320 | tf_op jit(solution)/shard_map/all_to_all | solution.py:638
  242.3 7.8 collective-permute-done.19.refs_2_
  251.9 19.1 %collective-permute-done.22.refs_0_ = bf16[128,2048]{1,0:T(8,128)(2,1)S(1)} collective-permute-done((bf16[128,2048]{1,0:T(8,128)(2,1)S(1)}, bf16[128,2048]{1,0:T(8,128)(2,1)S(1)}, u32[]{:S(2)}, u32[]{:S(2)}) %collective-permute-start.22) | collective-permute-done | bytes 524320 | tf_op jit(solution)/shard_map/ppermute | solution.py:522
  275.0 15.5 %collective-permute-done.20.refs_3_ = bf16[64,2048]{1,0:T(8,128)(2,1)S(1)} collective-permute-done((bf16[64,2048]{1,0:T(8,128)(2,1)S(1)}, bf16[64,2048]{1,0:T(8,128)(2,1)S(1)}, u32[]{:S(2)}, u32[]{:S(2)}) %collective-permute-start.20) | collective-permute-done | bytes 262176 | tf_op jit(solution)/shard_map/ppermute | solution.py:56
  293.0 14.7 %shard_map.247 = (bf16[512,2048]{1,0:T(8,128)(2,1)}, bf16[512,2048]{1,0:T(8,128)(2,1)}, f32[512,1]{1,0:T(8,128)}, bf16[512,2048]{1,0:T(8,128)(2,1)}, bf16[512,20...) custom-call(bf16[128,2048]{1,0:T(8,128)(2,1)} %collective-permute-done.23.refs_0_, ...), custom_call_target="tpu_custom_call" | custom-call | flops 6442450944 | bytes 25165824 | tf_op jit(solution)/shard_map/pallas_call | solution.py:347
  309.7 12.7 %collective-permute-done.37.refs_0_ = bf16[128,2048]{1,0:T(8,128)(2,1)} collective-permute-done((bf16[128,2048]{1,0:T(8,128)(2,1)S(1)}, bf16[128,2048]{1,0:T(8,128)(2,1)}, u32[]{:S(2)}, u32[]{:S(2)}) %collective-permute-start.37) | collective-permute-done | bytes 524320 | tf_op jit(solution)/shard_map/ppermute | solution.py:522
  324.4 12.9 %collective-permute-done.44.refs_0_ = bf16[128,2048]{1,0:T(8,128)(2,1)} collective-permute-done((bf16[128,2048]{1,0:T(8,128)(2,1)S(1)}, bf16[128,2048]{1,0:T(8,128)(2,1)}, u32[]{:S(2)}, u32[]{:S(2)}) %collective-permute-start.44) | collective-permute-done | bytes 524320 | tf_op jit(solution)/shard_map/ppermute | solution.py:522
  339.1 14.7 %shard_map.246 = (bf16[512,2048]{1,0:T(8,128)(2,1)}, bf16[512,2048]{1,0:T(8,128)(2,1)}, f32[512,1]{1,0:T(8,128)}, bf16[512,2048]{1,0:T(8,128)(2,1)}, bf16[512,20...) custom-call(bf16[128,2048]{1,0:T(8,128)(2,1)} %copy-done.25, bf16[128,2048]{1,0:T(8,128)(2,1)} %copy-done.45, ...), custom_call_target="tpu_custom_call" | custom-call | flops 6442450944 | bytes 25165824 | tf_op jit(solution)/shard_map/pallas_call | solution.py:347
  357.6 14.7 %shard_map.252 = (bf16[512,2048]{1,0:T(8,128)(2,1)}, bf16[512,2048]{1,0:T(8,128)(2,1)}, f32[512,1]{1,0:T(8,128)}, bf16[512,2048]{1,0:T(8,128)(2,1)}, bf16[512,20...) custom-call(bf16[128,2048]{1,0:T(8,128)(2,1)} %copy-done.51, ...), custom_call_target="tpu_custom_call" | custom-call | flops 6442450944 | bytes 25165824 | tf_op jit(solution)/shard_map/pallas_call | solution.py:347
  375.2 12.0 %collective-permute-done.32.refs_4_ = bf16[128,2048]{1,0:T(8,128)(2,1)S(1)} collective-permute-done((bf16[128,2048]{1,0:T(8,128)(2,1)S(1)}, bf16[128,2048]{1,0:T(8,128)(2,1)S(1)}, u32[]{:S(2)}, u32[]{:S(2)}) %collective-permute-start.32) | collective-permute-done | bytes 524320 | tf_op jit(solution)/shard_map/ppermute | solution.py:56
  403.2 14.7 %shard_map.251 = (bf16[512,2048]{1,0:T(8,128)(2,1)}, bf16[512,2048]{1,0:T(8,128)(2,1)}, f32[512,1]{1,0:T(8,128)}, bf16[512,2048]{1,0:T(8,128)(2,1)}, bf16[512,20...) custom-call(bf16[128,2048]{1,0:T(8,128)(2,1)} %copy-done.48, ...), custom_call_target="tpu_custom_call" | custom-call | flops 6442450944 | bytes 25165824 | tf_op jit(solution)/shard_map/pallas_call | solution.py:347
  417.9 16.8 %collective-permute-done.52.refs_3_ = bf16[128,2048]{1,0:T(8,128)(2,1)} collective-permute-done((bf16[128,2048]{1,0:T(8,128)(2,1)}, bf16[128,2048]{1,0:T(8,128)(2,1)}, u32[]{:S(2)}, u32[]{:S(2)}) %collective-permute-start.52) | collective-permute-done | bytes 524320 | tf_op jit(solution)/shard_map/ppermute | solution.py:56
  451.2 10.0 %collective-permute-done.59.refs_3_ = bf16[128,2048]{1,0:T(8,128)(2,1)} collective-permute-done((bf16[128,2048]{1,0:T(8,128)(2,1)}, bf16[128,2048]{1,0:T(8,128)(2,1)}, u32[]{:S(2)}, u32[]{:S(2)}) %collective-permute-start.59) | collective-permute-done | bytes 524320 | tf_op jit(solution)/shard_map/ppermute | solution.py:56
  461.1 14.7 %shard_map.257 = (bf16[512,2048]{1,0:T(8,128)(2,1)}, bf16[512,2048]{1,0:T(8,128)(2,1)}, f32[512,1]{1,0:T(8,128)}, bf16[512,2048]{1,0:T(8,128)(2,1)}, bf16[512,20...) custom-call(bf16[128,2048]{1,0:T(8,128)(2,1)} %collective-permute-done.55.refs_0_, ...), custom_call_target="tpu_custom_call" | custom-call | flops 6442450944 | bytes 25165824 | tf_op jit(solution)/shard_map/pallas_call | solution.py:347
  477.4 13.0 %collective-permute-done.48.refs_9_ = bf16[128,2048]{1,0:T(8,128)(2,1)S(1)} collective-permute-done((bf16[128,2048]{1,0:T(8,128)(2,1)S(1)}, bf16[128,2048]{1,0:T(8,128)(2,1)S(1)}, u32[]{:S(2)}, u32[]{:S(2)}) %collective-permute-start.48) | collective-permute-done | bytes 524320 | tf_op jit(solution)/shard_map/ppermute | solution.py:56
  496.1 14.7 %shard_map.256 = (bf16[512,2048]{1,0:T(8,128)(2,1)}, bf16[512,2048]{1,0:T(8,128)(2,1)}, f32[512,1]{1,0:T(8,128)}, bf16[512,2048]{1,0:T(8,128)(2,1)}, bf16[512,20...) custom-call(bf16[128,2048]{1,0:T(8,128)(2,1)} %collective-permute-done.37.refs_0_, ...), custom_call_target="tpu_custom_call" | custom-call | flops 6442450944 | bytes 25165824 | tf_op jit(solution)/shard_map/pallas_call | solution.py:347
  513.5 14.6 %shard_map.262 = (bf16[512,2048]{1,0:T(8,128)(2,1)}, bf16[512,2048]{1,0:T(8,128)(2,1)}, f32[512,1]{1,0:T(8,128)}, bf16[512,2048]{1,0:T(8,128)(2,1)}, bf16[512,20...) custom-call(bf16[128,2048]{1,0:T(8,128)(2,1)} %collective-permute-done.67.refs_0_, ...), custom_call_target="tpu_custom_call" | custom-call | flops 6442450944 | bytes 25165824 | tf_op jit(solution)/shard_map/pallas_call | solution.py:347
  553.9 14.6 %shard_map.261 = (bf16[512,2048]{1,0:T(8,128)(2,1)}, bf16[512,2048]{1,0:T(8,128)(2,1)}, f32[512,1]{1,0:T(8,128)}, bf16[512,2048]{1,0:T(8,128)(2,1)}, bf16[512,20...) custom-call(bf16[128,2048]{1,0:T(8,128)(2,1)} %collective-permute-done.44.refs_0_, ...), custom_call_target="tpu_custom_call" | custom-call | flops 6442450944 | bytes 25165824 | tf_op jit(solution)/shard_map/pallas_call | solution.py:347
  582.0 15.2 %shard_map.264 = f32[512,2048]{1,0:T(8,128)} custom-call(bf16[512,512]{1,0:T(8,128)(2,1)} %get-tuple-element.203.refs_0_, bf16[512,512]{1,0:T(8,128)(2,1)} %get-tuple-element.204.refs_1_, bf16[512,512]{1,0:T(8,128)(2,1)} %get-tuple-element.205.refs_2_, bf16[512,512]{1,0:T(8,128)(2,1)} %get-tuple-element.206.refs_3_, ...), custom_call_target="tpu_custom_call" | custom-call | flops 8589934592 | bytes 25165824 | tf_op jit(solution)/shard_map/pallas_call | solution.py:435
  609.7 15.8 %shard_map.266.refs_16_ = f32[2048,2,512]{2,1,0:T(2,128)} custom-call(bf16[512,2048]{1,0:T(8,128)(2,1)} %get-tuple-element.243.refs_0_, bf16[512,2048]{1,0:T(8,128)(2,1)} %get-tuple-element.225.refs_1_, bf16[512,2048]{1,0:T(8,128)(2,1)} %get-tuple-element.226.refs_2_, bf16[512,2048]{1,0:T(8,128)(2,1)} %get-tuple-element.227.refs_3_, ...), custom_call_target="tpu_custom_call" | custom-call | flops 8589934592 | bytes 16777216 | tf_op jit(solution)/shard_map/pallas_call | solution.py:405
  631.1 15.8 %shard_map.268 = f32[2048,2,512]{2,1,0:T(2,128)} custom-call(bf16[512,2048]{1,0:T(8,128)(2,1)} %get-tuple-element.243.refs_0_, bf16[512,2048]{1,0:T(8,128)(2,1)} %get-tuple-element.225.refs_1_, bf16[512,2048]{1,0:T(8,128)(2,1)} %get-tuple-element.226.refs_2_, bf16[512,2048]{1,0:T(8,128)(2,1)} %get-tuple-element.227.refs_3_, ...), custom_call_target="tpu_custom_call", output_to_operand_aliasing={{}: (16, {})} | custom-call | flops 8589934592 | bytes 16777216 | tf_op jit(solution)/shard_map/pallas_call | solution.py:405
  650.8 10.0 %collective-permute-done.77 = bf16[128,2048]{1,0:T(8,128)(2,1)} collective-permute-done((bf16[128,2048]{1,0:T(8,128)(2,1)S(1)}, bf16[128,2048]{1,0:T(8,128)(2,1)}, u32[]{:S(2)}, u32[]{:S(2)}) %collective-permute-start.77) | collective-permute-done | bytes 524320 | tf_op jit(solution)/shard_map/ppermute | solution.py:525
  669.0 8.8 %collective-permute-done.82 = bf16[128,2048]{1,0:T(8,128)(2,1)S(1)} collective-permute-done((bf16[128,2048]{1,0:T(8,128)(2,1)S(1)}, bf16[128,2048]{1,0:T(8,128)(2,1)S(1)}, u32[]{:S(2)}, u32[]{:S(2)}) %collective-permute-start.82) | collective-permute-done | bytes 524320 | tf_op jit(solution)/shard_map/ppermute | solution.py:56
  751.4 11.4 %all_to_all.49 = f32[32,1,192]{2,1,0:T(1,128)S(1)} all-to-all(f32[32,1,192]{2,1,0:T(1,128)S(1)} %reshape.844), channel_id=1, replica_groups=mesh['fsdp'=4,'seq'=8] {'fsdp','seq'}, dimensions={0} | all-to-all | bytes 49152 | tf_op jit(solution)/shard_map/all_to_all | solution.py:841
  769.2 14.2 %collective-permute-done.100 = f32[17,4,2,64]{3,2,1,0:T(2,128)S(1)} collective-permute-done((f32[17,4,2,64]{3,2,1,0:T(2,128)S(1)}, f32[17,4,2,64]{3,2,1,0:T(2,128)S(1)}, u32[]{:S(2)}, u32[]{:S(2)}) %collective-permute-start.100) | collective-permute-done | bytes 34848 | tf_op jit(solution)/shard_map/ppermute | solution.py:483
  811.3 21.1 %collective-permute-done.103 = f32[17,1,1,64]{3,1,2,0:T(1,128)S(1)} collective-permute-done((f32[17,1,1,64]{3,1,2,0:T(1,128)S(1)}, f32[17,1,1,64]{3,1,2,0:T(1,128)S(1)}, u32[]{:S(2)}, u32[]{:S(2)}) %collective-permute-start.103) | collective-permute-done | bytes 4384 | tf_op jit(solution)/shard_map/ppermute | solution.py:483
  840.8 19.4 %all-to-all-start.6 = ((bf16[8,64,256]{2,1,0:T(8,128)(2,1)}), bf16[8,64,256]{2,1,0:T(8,128)(2,1)S(1)}, u32[]{:S(2)}, u32[]{:S(2)}) async-start(bf16[8,64,256]{2,1,0:T(8,128)(2,1)} %bitcast.351), calls=%async_computation.7 | async-start | bytes 524288 | tf_op jit(solution)/shard_map/all_to_all | solution.py:817
  (671 shorter events, 404.0 us)
Async XLA Ops:
  7.2 216.9 %all-gather.3.cloned.1.call-start = ((), (), s32[]{:S(2)}) async-start(), calls=%async_computation.10 | async-start | bytes 8650752 | tf_op jit(solution)/shard_map/all_gather | solution.py:538
  9.1 283.9 %all-gather.5.cloned.1.call-start = ((), (), s32[]{:S(2)}) async-start(), calls=%async_computation.11 | async-start | bytes 17301504 | tf_op jit(solution)/shard_map/all_gather | solution.py:539
  69.7 37.0 %collective-permute-start.4 = (bf16[512,768]{1,0:T(8,128)(2,1)}, bf16[512,768]{1,0:T(8,128)(2,1)S(1)}, u32[]{:S(2)}, u32[]{:S(2)}) collective-permute-start(bf16[512,768]{1,0:T(8,128)(2,1)} %collective-permute-done), channel_id=1, source_target_pairs={{0,8},{8,16},{16,24},{1,9},{9,17},{17,25},{2,10},{10,18},{18,26},{... | collective-permute-start | bytes 2359304 | tf_op jit(solution)/shard_map/ppermute | solution.py:552
  74.2 47.0 %collective-permute-start.5 = (bf16[512,768]{1,0:T(8,128)(2,1)S(1)}, bf16[512,768]{1,0:T(8,128)(2,1)}, u32[]{:S(2)}, u32[]{:S(2)}) collective-permute-start(bf16[512,768]{1,0:T(8,128)(2,1)S(1)} %collective-permute-done.1), channel_id=1, source_target_pairs={{8,0},{16,8},{24,16},{9,1},{17,9},{25,17},{10,2},{18,10},{26,18},{... | collective-permute-start | bytes 2359304 | tf_op jit(solution)/shard_map/ppermute | solution.py:553
  88.0 33.2 %collective-permute-start.10 = (bf16[128,2048]{1,0:T(8,128)(2,1)S(1)}, bf16[128,2048]{1,0:T(8,128)(2,1)}, u32[]{:S(2)}, u32[]{:S(2)}) collective-permute-start(bf16[128,2048]{1,0:T(8,128)(2,1)S(1)} %collective-permute-done.3), channel_id=1, source_target_pairs={{0,1},{1,0},{2,3},{3,2},{4,5},{5,4},{6,7},{7,6},{8,9},{9,8},{10,11... | collective-permute-start | bytes 1572872 | tf_op jit(solution)/shard_map/ppermute | solution.py:56
  88.0 33.2 %collective-permute-start.8 = (bf16[128,2048]{1,0:T(8,128)(2,1)S(1)}, bf16[128,2048]{1,0:T(8,128)(2,1)}, u32[]{:S(2)}, u32[]{:S(2)}) collective-permute-start(bf16[128,2048]{1,0:T(8,128)(2,1)S(1)} %copy-done.27), channel_id=1, source_target_pairs={{0,1},{1,0},{2,3},{3,2},{4,5},{5,4},{6,7},{7,6},{8,9},{9,8},{10,11... | collective-permute-start | bytes 1572872 | tf_op jit(solution)/shard_map/ppermute | solution.py:56
  88.5 32.7 %collective-permute-start.9 = (bf16[128,2048]{1,0:T(8,128)(2,1)S(1)}, bf16[128,2048]{1,0:T(8,128)(2,1)}, u32[]{:S(2)}, u32[]{:S(2)}) collective-permute-start(bf16[128,2048]{1,0:T(8,128)(2,1)S(1)} %collective-permute-done.2), channel_id=1, source_target_pairs={{0,1},{1,0},{2,3},{3,2},{4,5},{5,4},{6,7},{7,6},{8,9},{9,8},{10,11... | collective-permute-start | bytes 1572872 | tf_op jit(solution)/shard_map/ppermute | solution.py:56
  126.3 32.7 %collective-permute-start.14 = (bf16[512,768]{1,0:T(8,128)(2,1)}, bf16[512,768]{1,0:T(8,128)(2,1)}, u32[]{:S(2)}, u32[]{:S(2)}) collective-permute-start(bf16[512,768]{1,0:T(8,128)(2,1)} %collective-permute-done.5), channel_id=1, source_target_pairs={{8,0},{16,8},{24,16},{9,1},{17,9},{25,17},{10,2},{18,10},{26,18},{... | collective-permute-start | bytes 2359304 | tf_op jit(solution)/shard_map/ppermute | solution.py:553
  235.5 39.0 %collective-permute-start.23 = (bf16[128,2048]{1,0:T(8,128)(2,1)S(1)}, bf16[128,2048]{1,0:T(8,128)(2,1)}, u32[]{:S(2)}, u32[]{:S(2)}) collective-permute-start(bf16[128,2048]{1,0:T(8,128)(2,1)S(1)} %multiply_convert_fusion.2.refs_0_), channel_id=1, source_target_pairs={{0,1},{1,0},{2,3},{3,2},{4,5},{5,4},{6,7},{7,6},{8,9},{9,8},{10,11... | collective-permute-start | bytes 1572872 | tf_op jit(solution)/shard_map/ppermute | solution.py:56
  237.5 34.9 %collective-permute-start.18 = (bf16[128,2048]{1,0:T(8,128)(2,1)S(1)}, bf16[128,2048]{1,0:T(8,128)(2,1)S(1)}, u32[]{:S(2)}, u32[]{:S(2)}) collective-permute-start(bf16[128,2048]{1,0:T(8,128)(2,1)S(1)} %multiply_convert_fusion.2.refs_0_), channel_id=1, source_target_pairs={{0,2},{1,3},{2,0},{3,1},{4,6},{5,7},{6,4},{7,5},{8,10},{9,11},{10,... | collective-permute-start | bytes 1572872 | tf_op jit(solution)/shard_map/ppermute | solution.py:56
  323.8 33.1 %collective-permute-start.43 = (bf16[128,2048]{1,0:T(8,128)(2,1)}, bf16[128,2048]{1,0:T(8,128)(2,1)}, u32[]{:S(2)}, u32[]{:S(2)}) collective-permute-start(bf16[128,2048]{1,0:T(8,128)(2,1)} %collective-permute-done.37.refs_0_), channel_id=1, source_target_pairs={{0,4},{1,5},{2,6},{3,7},{4,0},{5,1},{6,2},{7,3},{8,12},{9,13},{10,... | collective-permute-start | bytes 1572872 | tf_op jit(solution)/shard_map/ppermute | solution.py:56
  372.4 63.6 %collective-permute-start.45 = (bf16[512,2048]{1,0:T(8,128)(2,1)}, bf16[512,2048]{1,0:T(8,128)(2,1)S(1)}, u32[]{:S(2)}, u32[]{:S(2)}) collective-permute-start(bf16[512,2048]{1,0:T(8,128)(2,1)} %get-tuple-element.173), channel_id=1, source_target_pairs={{0,1},{1,0},{2,3},{3,2},{4,5},{5,4},{6,7},{7,6},{8,9},{9,8},{10,11... | collective-permute-start | bytes 6291464 | tf_op jit(solution)/shard_map/ppermute | solution.py:56
  372.9 64.4 %collective-permute-start.46 = (bf16[512,2048]{1,0:T(8,128)(2,1)}, bf16[512,2048]{1,0:T(8,128)(2,1)}, u32[]{:S(2)}, u32[]{:S(2)}) collective-permute-start(bf16[512,2048]{1,0:T(8,128)(2,1)} %get-tuple-element.175), channel_id=1, source_target_pairs={{0,1},{1,0},{2,3},{3,2},{4,5},{5,4},{6,7},{7,6},{8,9},{9,8},{10,11... | collective-permute-start | bytes 6291464 | tf_op jit(solution)/shard_map/ppermute | solution.py:56
  393.3 42.2 %collective-permute-start.34 = (bf16[256,2048]{1,0:T(8,128)(2,1)}, bf16[256,2048]{1,0:T(8,128)(2,1)S(1)}, u32[]{:S(2)}, u32[]{:S(2)}) collective-permute-start(bf16[256,2048]{1,0:T(8,128)(2,1)} %get-tuple-element.165), channel_id=1, source_target_pairs={{0,2},{1,3},{2,0},{3,1},{4,6},{5,7},{6,4},{7,5},{8,10},{9,11},{10,... | collective-permute-start | bytes 3145736 | tf_op jit(solution)/shard_map/ppermute | solution.py:56
  394.4 41.0 %collective-permute-start.35 = (bf16[256,2048]{1,0:T(8,128)(2,1)}, bf16[256,2048]{1,0:T(8,128)(2,1)}, u32[]{:S(2)}, u32[]{:S(2)}) collective-permute-start(bf16[256,2048]{1,0:T(8,128)(2,1)} %get-tuple-element.166), channel_id=1, source_target_pairs={{0,4},{1,5},{2,6},{3,7},{4,0},{5,1},{6,2},{7,3},{8,12},{9,13},{10,... | collective-permute-start | bytes 3145736 | tf_op jit(solution)/shard_map/ppermute | solution.py:56
  402.4 32.4 %collective-permute-start.52 = (bf16[128,2048]{1,0:T(8,128)(2,1)}, bf16[128,2048]{1,0:T(8,128)(2,1)}, u32[]{:S(2)}, u32[]{:S(2)}) collective-permute-start(bf16[128,2048]{1,0:T(8,128)(2,1)} %collective-permute-done.43.refs_2_), channel_id=1, source_target_pairs={{0,2},{1,3},{2,0},{3,1},{4,6},{5,7},{6,4},{7,5},{8,10},{9,11},{10,... | collective-permute-start | bytes 1572872 | tf_op jit(solution)/shard_map/ppermute | solution.py:56
  449.9 44.8 %collective-permute-start.67 = (bf16[128,2048]{1,0:T(8,128)(2,1)}, bf16[128,2048]{1,0:T(8,128)(2,1)}, u32[]{:S(2)}, u32[]{:S(2)}) collective-permute-start(bf16[128,2048]{1,0:T(8,128)(2,1)} %collective-permute-done.44.refs_0_), channel_id=1, source_target_pairs={{0,1},{1,0},{2,3},{3,2},{4,5},{5,4},{6,7},{7,6},{8,9},{9,8},{10,11... | collective-permute-start | bytes 1572872 | tf_op jit(solution)/shard_map/ppermute | solution.py:56
  449.9 45.3 %collective-permute-start.69 = (bf16[128,2048]{1,0:T(8,128)(2,1)}, bf16[128,2048]{1,0:T(8,128)(2,1)}, u32[]{:S(2)}, u32[]{:S(2)}) collective-permute-start(bf16[128,2048]{1,0:T(8,128)(2,1)} %collective-permute-done.54.refs_2_), channel_id=1, source_target_pairs={{0,1},{1,0},{2,3},{3,2},{4,5},{5,4},{6,7},{7,6},{8,9},{9,8},{10,11... | collective-permute-start | bytes 1572872 | tf_op jit(solution)/shard_map/ppermute | solution.py:56
  475.8 52.3 %collective-permute-start.60 = (bf16[512,2048]{1,0:T(8,128)(2,1)}, bf16[512,2048]{1,0:T(8,128)(2,1)}, u32[]{:S(2)}, u32[]{:S(2)}) collective-permute-start(bf16[512,2048]{1,0:T(8,128)(2,1)} %get-tuple-element.185), channel_id=1, source_target_pairs={{0,1},{1,0},{2,3},{3,2},{4,5},{5,4},{6,7},{7,6},{8,9},{9,8},{10,11... | collective-permute-start | bytes 6291464 | tf_op jit(solution)/shard_map/ppermute | solution.py:56
  475.9 52.8 %collective-permute-start.61 = (bf16[512,2048]{1,0:T(8,128)(2,1)}, bf16[512,2048]{1,0:T(8,128)(2,1)}, u32[]{:S(2)}, u32[]{:S(2)}) collective-permute-start(bf16[512,2048]{1,0:T(8,128)(2,1)} %get-tuple-element.187), channel_id=1, source_target_pairs={{0,1},{1,0},{2,3},{3,2},{4,5},{5,4},{6,7},{7,6},{8,9},{9,8},{10,11... | collective-permute-start | bytes 6291464 | tf_op jit(solution)/shard_map/ppermute | solution.py:56
  495.2 38.3 %collective-permute-start.49 = (bf16[256,2048]{1,0:T(8,128)(2,1)}, bf16[256,2048]{1,0:T(8,128)(2,1)S(1)}, u32[]{:S(2)}, u32[]{:S(2)}) collective-permute-start(bf16[256,2048]{1,0:T(8,128)(2,1)} %get-tuple-element.178), channel_id=1, source_target_pairs={{0,2},{1,3},{2,0},{3,1},{4,6},{5,7},{6,4},{7,5},{8,10},{9,11},{10,... | collective-permute-start | bytes 3145736 | tf_op jit(solution)/shard_map/ppermute | solution.py:56
  528.1 41.6 %collective-permute-start.71 = (bf16[512,2048]{1,0:T(8,128)(2,1)}, bf16[512,2048]{1,0:T(8,128)(2,1)}, u32[]{:S(2)}, u32[]{:S(2)}) collective-permute-start(bf16[512,2048]{1,0:T(8,128)(2,1)} %get-tuple-element.197), channel_id=1, source_target_pairs={{0,1},{1,0},{2,3},{3,2},{4,5},{5,4},{6,7},{7,6},{8,9},{9,8},{10,11... | collective-permute-start | bytes 6291464 | tf_op jit(solution)/shard_map/ppermute | solution.py:56
  528.2 44.9 %collective-permute-start.72 = (bf16[512,2048]{1,0:T(8,128)(2,1)}, bf16[512,2048]{1,0:T(8,128)(2,1)}, u32[]{:S(2)}, u32[]{:S(2)}) collective-permute-start(bf16[512,2048]{1,0:T(8,128)(2,1)} %get-tuple-element.199), channel_id=1, source_target_pairs={{0,1},{1,0},{2,3},{3,2},{4,5},{5,4},{6,7},{7,6},{8,9},{9,8},{10,11... | collective-permute-start | bytes 6291464 | tf_op jit(solution)/shard_map/ppermute | solution.py:56
  542.0 35.7 %collective-permute-start.51 = (bf16[128,2048]{1,0:T(8,128)(2,1)}, bf16[128,2048]{1,0:T(8,128)(2,1)}, u32[]{:S(2)}, u32[]{:S(2)}) collective-permute-start(bf16[128,2048]{1,0:T(8,128)(2,1)} %get-tuple-element.180), channel_id=1, source_target_pairs={{0,16},{8,24},{16,0},{24,8},{1,17},{9,25},{17,1},{25,9},{2,18},{10... | collective-permute-start | bytes 1572872 | tf_op jit(solution)/shard_map/ppermute | solution.py:525
  569.7 79.5 %collective-permute-start.79 = (bf16[128,2048]{1,0:T(8,128)(2,1)}, bf16[128,2048]{1,0:T(8,128)(2,1)}, u32[]{:S(2)}, u32[]{:S(2)}) collective-permute-start(bf16[128,2048]{1,0:T(8,128)(2,1)} %copy-done.17), channel_id=1, source_target_pairs={{0,16},{8,24},{16,0},{24,8},{1,17},{9,25},{17,1},{25,9},{2,18},{10... | collective-permute-start | bytes 1572872 | tf_op jit(solution)/shard_map/ppermute | solution.py:525
  603.7 43.3 %all-to-all-start.4 = ((f32[32,1,128]{2,1,0:T(1,128)}), f32[32,1,128]{2,1,0:T(1,128)S(1)}, u32[]{:S(2)}, u32[]{:S(2)}) async-start(f32[32,1,128]{2,1,0:T(1,128)} %bitcast.86), calls=%async_computation.4 | async-start | bytes 32768 | tf_op jit(solution)/shard_map/all_to_all | solution.py:752
  607.8 224.6 %reduce-scatter.5.cloned.1.call-start = ((), (), s32[]{:S(2)}) async-start(), calls=%async_computation.13 | async-start | bytes 1310720 | tf_op jit(solution)/shard_map/reduce_scatter | solution.py:778
  607.9 41.2 %collective-permute-start.78 = (bf16[128,2048]{1,0:T(8,128)(2,1)}, bf16[128,2048]{1,0:T(8,128)(2,1)}, u32[]{:S(2)}, u32[]{:S(2)}) collective-permute-start(bf16[128,2048]{1,0:T(8,128)(2,1)} %copy-done.18), channel_id=1, source_target_pairs={{0,8},{8,16},{16,24},{24,0},{1,9},{9,17},{17,25},{25,1},{2,10},{10... | collective-permute-start | bytes 1572872 | tf_op jit(solution)/shard_map/ppermute | solution.py:525
  727.0 39.5 %collective-permute-start.99 = (f32[17,4,4,64]{3,2,1,0:T(4,128)}, f32[17,4,4,64]{3,2,1,0:T(4,128)}, u32[]{:S(2)}, u32[]{:S(2)}) collective-permute-start(f32[17,4,4,64]{3,2,1,0:T(4,128)} %select_bitcast_fusion), channel_id=1, source_target_pairs={{0,1},{1,0},{2,3},{3,2},{4,5},{5,4},{6,7},{7,6},{8,9},{9,8},{10,11... | collective-permute-start | bytes 208904 | tf_op jit(solution)/shard_map/ppermute | solution.py:483
  750.3 42.8 %collective-permute-start.93 = (bf16[512,2048]{1,0:T(8,128)(2,1)}, bf16[512,2048]{1,0:T(8,128)(2,1)}, u32[]{:S(2)}, u32[]{:S(2)}) collective-permute-start(bf16[512,2048]{1,0:T(8,128)(2,1)} %get-tuple-element.287), channel_id=1, source_target_pairs={{0,1},{1,0},{2,3},{3,2},{4,5},{5,4},{6,7},{7,6},{8,9},{9,8},{10,11... | collective-permute-start | bytes 6291464 | tf_op jit(solution)/shard_map/ppermute | solution.py:56
  762.9 77.9 %all-to-all-start.5 = ((bf16[32,64,512]{2,1,0:T(8,128)(2,1)}), bf16[32,64,512]{2,1,0:T(8,128)(2,1)}, u32[]{:S(2)}, u32[]{:S(2)}) async-start(bf16[32,64,512]{2,1,0:T(8,128)(2,1)} %bitcast.325), calls=%async_computation.5 | async-start | bytes 4194304 | tf_op jit(solution)/shard_map/all_to_all | solution.py:809
  766.4 74.4 %reduce-scatter.3.cloned.1.call-start = ((), (), s32[]{:S(2)}) async-start(), calls=%async_computation.12 | async-start | bytes 1310720 | tf_op jit(solution)/shard_map/reduce_scatter | solution.py:807
  (170 other events, 2484.0 us)
Sparse Core Ops, SparseCore 0:
  10.9 102.1 all-gather.2
  115.9 149.9 all-gather.4
  727.1 27.3 reduce-scatter.4
  793.2 35.7 reduce-scatter.2

commit v3 on v2

--- a/solution.py
+++ b/solution.py
@@ -35,21 +35,6 @@
     frequency = THETA ** (-jnp.arange(half_width, dtype=F32) * 2.0 / head_width)
     angles = positions.astype(F32)[:, None] * frequency[None, :]
     return jnp.cos(angles)[:, None, :], jnp.sin(angles)[:, None, :]
-
-
-def rope(values, tables, heads):
-    rows, width = values.shape
-    cosine, sine = tables
-    shaped = values.reshape(rows, heads, width // heads)
-    half = width // heads // 2
-    a, b = shaped[..., :half], shaped[..., half:]
-    turned = jnp.concatenate([a * cosine - b * sine, b * cosine + a * sine], axis=-1)
-    return turned.reshape(rows, width)
-
-
-def rope_back(values, tables, heads):
-    cosine, sine = tables
-    return rope(values, (cosine, -sine), heads)
 
 
 def exchange(x, mask, size):
@@ -381,6 +366,143 @@
             flops=2 * rows * width * hidden * 6, bytes_accessed=24 << 20, transcendentals=0
         ),
     )(*m_arrays, c_all, c_rows, gates, gu, down)
+
+
+def attention_specs(length, heads, head_width, step):
+    rows = pl.BlockSpec((step, head_width), lambda h, i: (i, h))
+    whole = pl.BlockSpec((length, head_width), lambda h, i: (0, h))
+    marks = pl.BlockSpec((step, 2), lambda h, i: (i, 0))
+    marks_t = pl.BlockSpec((2, length), lambda h, i: (0, 0))
+    sums = pl.BlockSpec((1, step, 1), lambda h, i: (h, i, 0))
+    return rows, whole, marks, marks_t, sums
+
+
+def pair_scores(q, k, marks, marks_t, scale):
+    scores = times_transposed(q, k) * scale
+    allowed = (marks_t[0:1, :] <= marks[:, 0:1]) & (marks_t[1:2, :] == marks[:, 1:2])
+    return scores, allowed
+
+
+def turn(values, cosine, sine):
+    return values * cosine + pltpu.roll(values, values.shape[1] // 2, 1) * sine
+
+
+def turn_back(values, cosine, sine):
+    return values * cosine + pltpu.roll(values * sine, values.shape[1] // 2, 1)
+
+
+def attention(qkv, inverse, gains, tables, marks, heads, scale):
+    length, width = qkv.shape[0], gains.shape[1]
+    head_width, step = width // heads, 256
+
+    def kernel(q_ref, k_ref, v_ref, qi_ref, ki_ref, qg_ref, cq_ref, sq_ref, ck_ref, sk_ref,
+               marks_ref, marks_t_ref, o_ref, sum_ref, q_out, k_out):
+        @pl.when(pl.program_id(1) == 0)
+        def _():
+            scaled = k_ref[...] * ki_ref[:, 1:2] * qg_ref[1:2, :]
+            k_out[...] = turn(scaled, ck_ref[...], sk_ref[...]).astype(BF16)
+
+        scaled = q_ref[...] * qi_ref[:, 0:1] * qg_ref[0:1, :]
+        q = turn(scaled, cq_ref[...], sq_ref[...]).astype(BF16)
+        q_out[...] = q
+        scores, allowed = pair_scores(q, k_out[...], marks_ref[...], marks_t_ref[...], scale)
+        scores = jnp.where(allowed, scores, -1e30)
+        top = jnp.max(scores, axis=1, keepdims=True)
+        terms = jnp.where(allowed, jnp.exp(scores - top), 0.0)
+        total = jnp.sum(terms, axis=1, keepdims=True)
+        probs = terms * (1.0 / total)
+        o_ref[...] = times(probs.astype(BF16), v_ref[...].astype(BF16)).astype(BF16)
+        sum_ref[0] = top + jnp.log(total)
+
+    rows, whole, marks_s, marks_ts, sums = attention_specs(length, heads, head_width, step)
+    turned = pl.BlockSpec((step, head_width), lambda h, i: (i, 0))
+    turned_all = pl.BlockSpec((length, head_width), lambda h, i: (0, 0))
+    return pl.pallas_call(
+        kernel,
+        grid=(heads, length // step),
+        out_shape=[
+            jax.ShapeDtypeStruct((length, width), BF16),
+            jax.ShapeDtypeStruct((heads, length, 1), F32),
+            jax.ShapeDtypeStruct((length, width), BF16),
+            jax.ShapeDtypeStruct((length, width), BF16),
+        ],
+        in_specs=[
+            rows,
+            pl.BlockSpec((length, head_width), lambda h, i: (0, heads + h)),
+            pl.BlockSpec((length, head_width), lambda h, i: (0, 2 * heads + h)),
+            marks_s,
+            pl.BlockSpec((length, 2), lambda h, i: (0, 0)),
+            pl.BlockSpec((2, head_width), lambda h, i: (0, h)),
+            turned,
+            turned,
+            turned_all,
+            turned_all,
+            marks_s,
+            marks_ts,
+        ],
+        out_specs=[rows, sums, rows, whole],
+        compiler_params=pltpu.CompilerParams(vmem_limit_bytes=48 << 20),
+        cost_estimate=pl.CostEstimate(
+            flops=4 * length * length * width, bytes_accessed=4 << 20, transcendentals=0
+        ),
+    )(qkv, qkv, qkv, inverse, inverse, gains, *tables, *tables, marks, marks.T)
+
+
+def attention_back(query, key, qkv, grad, log_sums, tables, marks, heads, scale):
+    length, width = query.shape
+    head_width, step = width // heads, 256
+
+    def kernel(q_ref, k_ref, v_ref, do_ref, sum_ref, cq_ref, sq_ref, ck_ref, sk_ref, marks_ref,
+               marks_t_ref, dq_ref, dk_ref, dv_ref):
+        q, k, do = q_ref[...], k_ref[...], do_ref[...]
+        scores, allowed = pair_scores(q, k, marks_ref[...], marks_t_ref[...], scale)
+        probs = jnp.where(allowed, jnp.exp(scores - sum_ref[0]), 0.0)
+        grad_p = times_transposed(do, v_ref[...].astype(BF16))
+        delta = jnp.sum(probs * grad_p, axis=1, keepdims=True)
+        grad_s = (probs * (grad_p - delta)).astype(BF16)
+        dq_ref[...] = turn_back(times(grad_s, k) * scale, cq_ref[...], sq_ref[...])
+        dk = rows_by_rows(grad_s, q) * scale
+        dv = rows_by_rows(probs.astype(BF16), do)
+        first = pl.program_id(1) == 0
+
+        @pl.when(first)
+        def _():
+            dk_ref[...] = dk
+            dv_ref[...] = dv
+
+        @pl.when(jnp.logical_not(first))
+        def _():
+            dk_ref[...] += dk
+            dv_ref[...] += dv
+
+        @pl.when(pl.program_id(1) == length // step - 1)
+        def _():
+            dk_ref[...] = turn_back(dk_ref[...], ck_ref[...], sk_ref[...])
+
+    rows, whole, marks_s, marks_ts, sums = attention_specs(length, heads, head_width, step)
+    return pl.pallas_call(
+        kernel,
+        grid=(heads, length // step),
+        out_shape=[jax.ShapeDtypeStruct((length, width), F32)] * 3,
+        in_specs=[
+            rows,
+            whole,
+            pl.BlockSpec((length, head_width), lambda h, i: (0, 2 * heads + h)),
+            rows,
+            sums,
+            pl.BlockSpec((step, head_width), lambda h, i: (i, 0)),
+            pl.BlockSpec((step, head_width), lambda h, i: (i, 0)),
+            pl.BlockSpec((length, head_width), lambda h, i: (0, 0)),
+            pl.BlockSpec((length, head_width), lambda h, i: (0, 0)),
+            marks_s,
+            marks_ts,
+        ],
+        out_specs=[rows, whole, whole],
+        compiler_params=pltpu.CompilerParams(vmem_limit_bytes=48 << 20),
+        cost_estimate=pl.CostEstimate(
+            flops=10 * length * length * width, bytes_accessed=8 << 20, transcendentals=0
+        ),
+    )(query, key, qkv, grad, log_sums, *tables, *tables, marks, marks.T)
 
 
 def gate_up_weights(lefts, rights, before=None, rest=None):
@@ -598,7 +720,6 @@
     w_cols = lax.dynamic_slice(w_cols, ((F - 1 - me_f) * S * RW, 0), (D, cols))
     qkv = times(a_seq, w_cols)
     q_proj, k_proj = qkv[:, :CW], qkv[:, CW : 2 * CW]
-    value = qkv[:, 2 * CW :].astype(BF16)
 
     def seq_sum(stats):
         stats = stats.reshape(-1, 2, S // 2, R)
@@ -615,24 +736,16 @@
     gk_mine = lax.dynamic_slice(gk, (me_s * CW,), (CW,))
     positions = (slots[:, None] * R + jnp.arange(R, dtype=jnp.int32)[None]).reshape(L)
     segment_seq = to_slots(segment_all, S, me_s).reshape(L)
-    tables = rope_tables(positions, HW)
-    query = rope(q_proj * q_inv * gq_mine, tables, HL).astype(BF16)
-    key = rope(k_proj * k_inv * gk_mine, tables, HL).astype(BF16)
-
-    allowed = (positions[None, :] <= positions[:, None]) & (
-        segment_seq[None, :] == segment_seq[:, None]
-    )
-    q_heads = query.reshape(L, HL, HW)
-    k_heads = key.reshape(L, HL, HW)
-    v_heads = value.reshape(L, HL, HW)
-    scores = jnp.einsum("thd,uhd->htu", q_heads, k_heads, preferred_element_type=F32)
-    scores = jnp.where(allowed[None], scores * scale, -1e30)
-    row_max = jnp.max(scores, axis=-1, keepdims=True)
-    terms = jnp.where(allowed[None], jnp.exp(scores - row_max), 0.0)
-    probs = terms / jnp.sum(terms, axis=-1, keepdims=True)
-    probs_low = probs.astype(BF16)
-    attended = jnp.einsum("htu,uhd->thd", probs_low, v_heads, preferred_element_type=F32)
-    attended = attended.reshape(L, CW).astype(BF16)
+    cosine, sine = [t[:, 0] for t in rope_tables(positions, HW)]
+    tables = (
+        jnp.concatenate([cosine, cosine], axis=1),
+        jnp.concatenate([-sine, sine], axis=1),
+    )
+    marks = jnp.stack([positions.astype(F32), segment_seq], axis=1)
+    gains_mine = jnp.stack([gq_mine, gk_mine])
+    attended, log_sums, query, key = attention(
+        qkv, inverse.T, gains_mine, tables, marks, HL, scale
+    )
     o_send = attended.reshape(S, R, CW)
     o_send = from_slots(o_send, S, me_s)
     o_mine = lax.all_to_all(o_send, "seq", split_axis=0, concat_axis=0, tiled=True)
@@ -784,15 +897,12 @@
     output = output.astype(BF16)
 
     wo_rows = lax.dynamic_slice(wo_all, (me_s * CW, 0), (CW, D))
-    grad_heads = times_transposed(after(grad_proj, out_part, early, *mix_done.values()), wo_rows).astype(BF16).reshape(L, HL, HW)
-    grad_p = jnp.einsum("thd,uhd->htu", grad_heads, v_heads, preferred_element_type=F32)
-    delta = jnp.sum(probs * grad_p, axis=-1, keepdims=True)
-    grad_s = (probs * (grad_p - delta)).astype(BF16)
-    dq = jnp.einsum("htu,uhd->thd", grad_s, k_heads, preferred_element_type=F32)
-    dk = jnp.einsum("htu,thd->uhd", grad_s, q_heads, preferred_element_type=F32)
-    dv = jnp.einsum("htu,thd->uhd", probs_low, grad_heads, preferred_element_type=F32)
-    dq = rope_back(dq.reshape(L, CW) * scale, tables, HL)
-    dk = rope_back(dk.reshape(L, CW) * scale, tables, HL)
+    grad_heads = times_transposed(
+        after(grad_proj, out_part, early, *mix_done.values()), wo_rows
+    ).astype(BF16)
+    dq, dk, dv = attention_back(
+        query, key, qkv, grad_heads, log_sums, tables, marks, HL, scale
+    )
     q_part = jnp.sum(dq * q_proj * q_inv, axis=0)
     k_part = jnp.sum(dk * k_proj * k_inv, axis=0)
     dq = dq * gq_mine
@@ -801,11 +911,11 @@
     means = seq_sum(means) / D
     dqp = q_inv * dq - q_proj * q_inv**3 * means[0][:, None]
     dkp = k_inv * dk - k_proj * k_inv**3 * means[1][:, None]
-    dv_low = dv.reshape(L, CW).astype(BF16)
+    dv_low = dv.astype(BF16)
     dqk = jnp.concatenate([dqp.astype(BF16), dkp.astype(BF16)], axis=1)
     v_part = rows_by_rows(a_seq, dv_low).astype(BF16)
     v_sum = lax.psum_scatter(v_part, "fsdp", scatter_dimension=0, tiled=True)
-    qk_part = rows_by_rows(a_seq, dqk).astype(BF16).reshape(N, RW, 2 * CW)
+    qk_part = rows_by_rows(a_seq, after(dqk, v_part)).astype(BF16).reshape(N, RW, 2 * CW)
     qk_got = lax.all_to_all(qk_part, BOTH, split_axis=0, concat_axis=0, tiled=True)
     qk_parts = qk_got.reshape(F, S, RW, 2 * CW)
     qk_all = qk_parts[0].astype(F32)

time: 884 us -> 883 us (level)
  matrix products: 62.4 us -> 33.3 us
  Pallas kernels: 202 us -> 227 us
  waiting for transfers between devices: 273 us -> 294 us
  other arithmetic: 68 us -> 47.3 us
  starting transfers between devices: 149 us -> 167 us
  blocking collectives: 30.8 us -> 19.4 us
    pallas_call x0 -> x2, Pallas kernels: none -> 25.6 us  [the longest x1 13.7 us: attention_back(): pl.pallas_call(kernel, grid=(heads, length // step), out_shape=[jax.Shape...]
    dot_general x5 -> x0, matrix products: 18.3 us -> none  [the longest x1 5.88 us: per_device(): jnp.einsum('htu,thd->uhd', probs_low, grad_heads, preferred_element_type=...]
    all_to_all x1 -> x0, blocking collectives: 11.4 us -> none  [per_device(): late = lax.all_to_all(late, BOTH, split_axis=0, concat_axis=0, tiled=True)]
    ppermute x3, starting transfers between devices: 3.74 us -> 15.1 us  [shift_in(): return lax.ppermute(x, 'fsdp', [((i + j) % F, i) for i in range(F)])]
    sub x1 -> x0, matrix products: 9.99 us -> none  [per_device(): terms = jnp.where(allowed[None], jnp.exp(scores - row_max), 0.0)]
    unnamed x212 -> x202, local copies, waits for them, and re-layouts: 47.7 us -> 47.1 us
  transfers between devices with their start and end apart: 114 -> 115, of which waited for: 36 -> 38; matrix products, arithmetic and copies ran while one was open for 17% -> 14% of each run, Pallas kernels for 20% -> 23%
where the time goes in v3:
time: 883 us; the launch traced here: 873 us
  waiting for transfers between devices  294 us (33%)
  Pallas kernels  227 us (26%)
  starting transfers between devices  167 us (19%)
  local copies, waits for them, and re-layouts  68.2 us (8%)
  other arithmetic  47.3 us (5%)
  matrix products  33.3 us (4%)
  blocking collectives  19.4 us (2%)
  between operations  16.3 us (2%)
    ppermute x83, waiting for transfers between devices, exchange(): return lax.ppermute(x, 'seq', [(i, i ^ mask) for i in range(size)])  131 us
    pallas_call x8, Pallas kernels, expert_rows(): pl.pallas_call(kernel, out_shape=[sds((rows, width), BF16), sds((rows, wi...  117 us
    ppermute x83, starting transfers between devices, exchange(): return lax.ppermute(x, 'seq', [(i, i ^ mask) for i in range(size)])  57.5 us
    ppermute x3, waiting for transfers between devices, shift_in(): return lax.ppermute(x, 'fsdp', [((i + j) % F, i) for i in range(F)])  51.1 us
    ppermute x5, waiting for transfers between devices, sum_to_owners(): x = mine + lax.ppermute(theirs, axis, [(i, i ^ b) for i in range(count)])  49.9 us
    unnamed x202, local copies, waits for them, and re-layouts  47.1 us
    pallas_call x15, Pallas kernels, add_blocks(): pl.pallas_call(kernel, grid=(1,), out_shape=shapes, in_specs=specs, out_s...  37.6 us
    pallas_call x2, Pallas kernels, gate_up_weights(): pl.pallas_call(kernel, grid=(steps,), out_shape=jax.ShapeDtypeStruct((wid...  31.6 us
  transfers between devices with their start and end apart: 115, of which 38 were waited for; matrix products, arithmetic and copies ran while one was open for 14% of the time, Pallas kernels for 23%

profile of v3, /device:TPU:0, one launch (start us, length us, event | category | flops | bytes accessed | tf_op | source)
XLA Modules:
  0.0 872.6 jit_solution(15405094532295229051)
XLA Ops:
  15.6 19.4 %all_to_all.48 = bf16[8,64,768]{2,1,0:T(8,128)(2,1)S(1)} all-to-all(bf16[8,64,768]{2,1,0:T(8,128)(2,1)S(1)} %reshape.600), channel_id=1, replica_groups=mesh['fsdp'=4,'seq'=8] {'seq'}, dimensions={0} | all-to-all | bytes 1572864 | tf_op jit(solution)/shard_map/all_to_all | solution.py:658
  45.7 12.7 %collective-permute-done.3 = bf16[128,2048]{1,0:T(8,128)(2,1)} collective-permute-done((bf16[128,2048]{1,0:T(8,128)(2,1)S(1)}, bf16[128,2048]{1,0:T(8,128)(2,1)}, u32[]{:S(2)}, u32[]{:S(2)}) %collective-permute-start.3) | collective-permute-done | bytes 524320 | tf_op jit(solution)/shard_map/ppermute | solution.py:41
  90.5 16.8 %collective-permute-done.4 = bf16[512,768]{1,0:T(8,128)(2,1)} collective-permute-done((bf16[512,768]{1,0:T(8,128)(2,1)}, bf16[512,768]{1,0:T(8,128)(2,1)}, u32[]{:S(2)}, u32[]{:S(2)}) %collective-permute-start.4) | collective-permute-done | bytes 786464 | tf_op jit(solution)/shard_map/ppermute | solution.py:674
  111.8 13.1 %all-to-all-start.1 = ((bf16[32,11,128]{2,1,0:T(8,128)(2,1)}), bf16[32,11,128]{2,1,0:T(8,128)(2,1)S(1)}, u32[]{:S(2)}, u32[]{:S(2)}) async-start(bf16[32,11,128]{2,1,0:T(8,128)(2,1)} %broadcast_in_dim.11), calls=%async_computation.1 | async-start | bytes 262144 | tf_op jit(solution)/shard_map/all_to_all | solution.py:706
  178.5 11.9 %shard_map.246 = (bf16[1024,256]{1,0:T(8,128)(2,1)S(1)}, f32[2,1024,1]{2,1,0:T(8,128)S(1)}, bf16[1024,256]{1,0:T(8,128)(2,1)S(1)}, bf16[1024,256]{1,0:T(8,128)(2,1)S(1)}) custom-call(f32[1024,768]{1,0:T(8,128)} %copy-done.36, f32[1024,768]{1,0:T(8,128)} %copy-done.36, f32[1024,768]{1,0:T(8,128)} %copy-done.36, f32[1024,2]{1,0:T(8,128)S(1)} %bitcast.265, ...), custom_call_target="tpu_custom_call" | custom-call | flops 1073741824 | bytes 4194304 | tf_op jit(solution)/shard_map/pallas_call | solution.py:420
  197.2 15.0 %all-to-all-done.2 = bf16[8,128,256]{2,1,0:T(8,128)(2,1)S(1)} async-done(((bf16[8,128,256]{2,1,0:T(8,128)(2,1)}), bf16[8,128,256]{2,1,0:T(8,128)(2,1)S(1)}, u32[]{:S(2)}, u32[]{:S(2)}) %all-to-all-start.2) | async-done | bytes 524320 | tf_op jit(solution)/shard_map/all_to_all | solution.py:751
  231.6 9.8 %collective-permute-done.19.refs_2_ = bf16[128,2048]{1,0:T(8,128)(2,1)S(1)} collective-permute-done((bf16[128,2048]{1,0:T(8,128)(2,1)S(1)}, bf16[128,2048]{1,0:T(8,128)(2,1)S(1)}, u32[]{:S(2)}, u32[]{:S(2)}) %collective-permute-start.19) | collective-permute-done | bytes 524320 | tf_op jit(solution)/shard_map/ppermute | solution.py:41
  243.0 26.0 %collective-permute-done.22.refs_0_ = bf16[128,2048]{1,0:T(8,128)(2,1)S(1)} collective-permute-done((bf16[128,2048]{1,0:T(8,128)(2,1)S(1)}, bf16[128,2048]{1,0:T(8,128)(2,1)S(1)}, u32[]{:S(2)}, u32[]{:S(2)}) %collective-permute-start.22) | collective-permute-done | bytes 524320 | tf_op jit(solution)/shard_map/ppermute | solution.py:644
  272.3 15.2 %collective-permute-done.20.refs_3_ = bf16[64,2048]{1,0:T(8,128)(2,1)S(1)} collective-permute-done((bf16[64,2048]{1,0:T(8,128)(2,1)S(1)}, bf16[64,2048]{1,0:T(8,128)(2,1)S(1)}, u32[]{:S(2)}, u32[]{:S(2)}) %collective-permute-start.20) | collective-permute-done | bytes 262176 | tf_op jit(solution)/shard_map/ppermute | solution.py:41
  290.1 14.7 %shard_map.248 = (bf16[512,2048]{1,0:T(8,128)(2,1)}, bf16[512,2048]{1,0:T(8,128)(2,1)}, f32[512,1]{1,0:T(8,128)}, bf16[512,2048]{1,0:T(8,128)(2,1)}, bf16[512,20...) custom-call(bf16[128,2048]{1,0:T(8,128)(2,1)} %collective-permute-done.23.refs_0_, ...), custom_call_target="tpu_custom_call" | custom-call | flops 6442450944 | bytes 25165824 | tf_op jit(solution)/shard_map/pallas_call | solution.py:332
  309.7 11.4 %collective-permute-done.37.refs_0_ = bf16[128,2048]{1,0:T(8,128)(2,1)} collective-permute-done((bf16[128,2048]{1,0:T(8,128)(2,1)S(1)}, bf16[128,2048]{1,0:T(8,128)(2,1)}, u32[]{:S(2)}, u32[]{:S(2)}) %collective-permute-start.37) | collective-permute-done | bytes 524320 | tf_op jit(solution)/shard_map/ppermute | solution.py:644
  331.7 13.7 %collective-permute-done.44.refs_0_ = bf16[128,2048]{1,0:T(8,128)(2,1)} collective-permute-done((bf16[128,2048]{1,0:T(8,128)(2,1)S(1)}, bf16[128,2048]{1,0:T(8,128)(2,1)}, u32[]{:S(2)}, u32[]{:S(2)}) %collective-permute-start.44) | collective-permute-done | bytes 524320 | tf_op jit(solution)/shard_map/ppermute | solution.py:644
  346.6 14.7 %shard_map.247 = (bf16[512,2048]{1,0:T(8,128)(2,1)}, bf16[512,2048]{1,0:T(8,128)(2,1)}, f32[512,1]{1,0:T(8,128)}, bf16[512,2048]{1,0:T(8,128)(2,1)}, bf16[512,20...) custom-call(bf16[128,2048]{1,0:T(8,128)(2,1)} %copy-done.40, bf16[128,2048]{1,0:T(8,128)(2,1)} %copy-done.54, ...), custom_call_target="tpu_custom_call" | custom-call | flops 6442450944 | bytes 25165824 | tf_op jit(solution)/shard_map/pallas_call | solution.py:332
  365.2 14.7 %shard_map.253 = (bf16[512,2048]{1,0:T(8,128)(2,1)}, bf16[512,2048]{1,0:T(8,128)(2,1)}, f32[512,1]{1,0:T(8,128)}, bf16[512,2048]{1,0:T(8,128)(2,1)}, bf16[512,20...) custom-call(bf16[128,2048]{1,0:T(8,128)(2,1)} %copy-done.58, ...), custom_call_target="tpu_custom_call" | custom-call | flops 6442450944 | bytes 25165824 | tf_op jit(solution)/shard_map/pallas_call | solution.py:332
  382.5 12.3 %collective-permute-done.32.refs_4_ = bf16[128,2048]{1,0:T(8,128)(2,1)S(1)} collective-permute-done((bf16[128,2048]{1,0:T(8,128)(2,1)S(1)}, bf16[128,2048]{1,0:T(8,128)(2,1)S(1)}, u32[]{:S(2)}, u32[]{:S(2)}) %collective-permute-start.32) | collective-permute-done | bytes 524320 | tf_op jit(solution)/shard_map/ppermute | solution.py:41
  411.4 14.7 %shard_map.252 = (bf16[512,2048]{1,0:T(8,128)(2,1)}, bf16[512,2048]{1,0:T(8,128)(2,1)}, f32[512,1]{1,0:T(8,128)}, bf16[512,2048]{1,0:T(8,128)(2,1)}, bf16[512,20...) custom-call(bf16[128,2048]{1,0:T(8,128)(2,1)} %copy-done.56, ...), custom_call_target="tpu_custom_call" | custom-call | flops 6442450944 | bytes 25165824 | tf_op jit(solution)/shard_map/pallas_call | solution.py:332
  426.0 16.2 %collective-permute-done.52.refs_3_ = bf16[128,2048]{1,0:T(8,128)(2,1)} collective-permute-done((bf16[128,2048]{1,0:T(8,128)(2,1)}, bf16[128,2048]{1,0:T(8,128)(2,1)}, u32[]{:S(2)}, u32[]{:S(2)}) %collective-permute-start.52) | collective-permute-done | bytes 524320 | tf_op jit(solution)/shard_map/ppermute | solution.py:41
  458.5 10.2 %collective-permute-done.59.refs_3_ = bf16[128,2048]{1,0:T(8,128)(2,1)} collective-permute-done((bf16[128,2048]{1,0:T(8,128)(2,1)}, bf16[128,2048]{1,0:T(8,128)(2,1)}, u32[]{:S(2)}, u32[]{:S(2)}) %collective-permute-start.59) | collective-permute-done | bytes 524320 | tf_op jit(solution)/shard_map/ppermute | solution.py:41
  468.7 14.7 %shard_map.258 = (bf16[512,2048]{1,0:T(8,128)(2,1)}, bf16[512,2048]{1,0:T(8,128)(2,1)}, f32[512,1]{1,0:T(8,128)}, bf16[512,2048]{1,0:T(8,128)(2,1)}, bf16[512,20...) custom-call(bf16[128,2048]{1,0:T(8,128)(2,1)} %collective-permute-done.55.refs_0_, ...), custom_call_target="tpu_custom_call" | custom-call | flops 6442450944 | bytes 25165824 | tf_op jit(solution)/shard_map/pallas_call | solution.py:332
  485.5 12.4 %collective-permute-done.48.refs_9_ = bf16[128,2048]{1,0:T(8,128)(2,1)S(1)} collective-permute-done((bf16[128,2048]{1,0:T(8,128)(2,1)S(1)}, bf16[128,2048]{1,0:T(8,128)(2,1)S(1)}, u32[]{:S(2)}, u32[]{:S(2)}) %collective-permute-start.48) | collective-permute-done | bytes 524320 | tf_op jit(solution)/shard_map/ppermute | solution.py:41
  504.1 14.7 %shard_map.257 = (bf16[512,2048]{1,0:T(8,128)(2,1)}, bf16[512,2048]{1,0:T(8,128)(2,1)}, f32[512,1]{1,0:T(8,128)}, bf16[512,2048]{1,0:T(8,128)(2,1)}, bf16[512,20...) custom-call(bf16[128,2048]{1,0:T(8,128)(2,1)} %collective-permute-done.37.refs_0_, ...), custom_call_target="tpu_custom_call" | custom-call | flops 6442450944 | bytes 25165824 | tf_op jit(solution)/shard_map/pallas_call | solution.py:332
  520.7 14.5 %shard_map.263 = (bf16[512,2048]{1,0:T(8,128)(2,1)}, bf16[512,2048]{1,0:T(8,128)(2,1)}, f32[512,1]{1,0:T(8,128)}, bf16[512,2048]{1,0:T(8,128)(2,1)}, bf16[512,20...) custom-call(bf16[128,2048]{1,0:T(8,128)(2,1)} %collective-permute-done.67.refs_0_, ...), custom_call_target="tpu_custom_call" | custom-call | flops 6442450944 | bytes 25165824 | tf_op jit(solution)/shard_map/pallas_call | solution.py:332
  561.2 14.6 %shard_map.262 = (bf16[512,2048]{1,0:T(8,128)(2,1)}, bf16[512,2048]{1,0:T(8,128)(2,1)}, f32[512,1]{1,0:T(8,128)}, bf16[512,2048]{1,0:T(8,128)(2,1)}, bf16[512,20...) custom-call(bf16[128,2048]{1,0:T(8,128)(2,1)} %collective-permute-done.44.refs_0_, ...), custom_call_target="tpu_custom_call" | custom-call | flops 6442450944 | bytes 25165824 | tf_op jit(solution)/shard_map/pallas_call | solution.py:332
  589.3 15.0 %shard_map.265 = f32[512,2048]{1,0:T(8,128)} custom-call(bf16[512,512]{1,0:T(8,128)(2,1)} %get-tuple-element.212.refs_0_, bf16[512,512]{1,0:T(8,128)(2,1)} %get-tuple-element.213.refs_1_, bf16[512,512]{1,0:T(8,128)(2,1)} %get-tuple-element.214.refs_2_, bf16[512,512]{1,0:T(8,128)(2,1)} %get-tuple-element.215.refs_3_, ...), custom_call_target="tpu_custom_call" | custom-call | flops 8589934592 | bytes 25165824 | tf_op jit(solution)/shard_map/pallas_call | solution.py:557
  617.2 15.8 %shard_map.267.refs_16_ = f32[2048,2,512]{2,1,0:T(2,128)} custom-call(bf16[512,2048]{1,0:T(8,128)(2,1)} %get-tuple-element.252.refs_0_, bf16[512,2048]{1,0:T(8,128)(2,1)} %get-tuple-element.234.refs_1_, bf16[512,2048]{1,0:T(8,128)(2,1)} %get-tuple-element.235.refs_2_, bf16[512,2048]{1,0:T(8,128)(2,1)} %get-tuple-element.236.refs_3_, ...), custom_call_target="tpu_custom_call" | custom-call | flops 8589934592 | bytes 16777216 | tf_op jit(solution)/shard_map/pallas_call | solution.py:527
  638.9 15.8 %shard_map.269 = f32[2048,2,512]{2,1,0:T(2,128)} custom-call(bf16[512,2048]{1,0:T(8,128)(2,1)} %get-tuple-element.252.refs_0_, bf16[512,2048]{1,0:T(8,128)(2,1)} %get-tuple-element.234.refs_1_, bf16[512,2048]{1,0:T(8,128)(2,1)} %get-tuple-element.235.refs_2_, bf16[512,2048]{1,0:T(8,128)(2,1)} %get-tuple-element.236.refs_3_, ...), custom_call_target="tpu_custom_call", output_to_operand_aliasing={{}: (16, {})} | custom-call | flops 8589934592 | bytes 16777216 | tf_op jit(solution)/shard_map/pallas_call | solution.py:527
  658.2 10.0 %collective-permute-done.77 = bf16[128,2048]{1,0:T(8,128)(2,1)} collective-permute-done((bf16[128,2048]{1,0:T(8,128)(2,1)S(1)}, bf16[128,2048]{1,0:T(8,128)(2,1)}, u32[]{:S(2)}, u32[]{:S(2)}) %collective-permute-start.77) | collective-permute-done | bytes 524320 | tf_op jit(solution)/shard_map/ppermute | solution.py:647
  708.0 13.7 %shard_map.270 = (f32[1024,256]{1,0:T(8,128)S(1)}, f32[1024,256]{1,0:T(8,128)S(1)}, f32[1024,256]{1,0:T(8,128)}) custom-call(bf16[1024,256]{1,0:T(8,128)(2,1)S(1)} %copy-done.29, bf16[1024,256]{1,0:T(8,128)(2,1)S(1)} %copy-done.31, f32[1024,768]{1,0:T(8,128)} %copy-done.36, bf16[1024,256]{1,0:T(8,128)(2,1)S(1)} %convolution_convert_fusion.3.do_ref, ...), custom_call_target="tpu_custom_call" | custom-call | flops 2684354560 | bytes 8388608 | tf_op jit(solution)/shard_map/pallas_call | solution.py:483
  767.4 13.7 %collective-permute-done.100 = f32[17,4,2,64]{3,2,1,0:T(2,128)S(1)} collective-permute-done((f32[17,4,2,64]{3,2,1,0:T(2,128)S(1)}, f32[17,4,2,64]{3,2,1,0:T(2,128)S(1)}, u32[]{:S(2)}, u32[]{:S(2)}) %collective-permute-start.100) | collective-permute-done | bytes 34848 | tf_op jit(solution)/shard_map/ppermute | solution.py:605
  789.6 13.8 %collective-permute-done.102 = f32[17,1,2,64]{3,2,0,1:T(2,128)S(1)} collective-permute-done((f32[17,1,2,64]{3,2,0,1:T(2,128)S(1)}, f32[17,1,2,64]{3,2,0,1:T(2,128)S(1)}, u32[]{:S(2)}, u32[]{:S(2)}) %collective-permute-start.102) | collective-permute-done | bytes 8736 | tf_op jit(solution)/shard_map/ppermute | solution.py:605
  812.9 17.2 %collective-permute-done.103 = f32[17,1,1,64]{3,1,2,0:T(1,128)S(1)} collective-permute-done((f32[17,1,1,64]{3,1,2,0:T(1,128)S(1)}, f32[17,1,1,64]{3,1,2,0:T(1,128)S(1)}, u32[]{:S(2)}, u32[]{:S(2)}) %collective-permute-start.103) | collective-permute-done | bytes 4384 | tf_op jit(solution)/shard_map/ppermute | solution.py:605
  838.5 19.4 %all-to-all-start.6 = ((bf16[8,64,256]{2,1,0:T(8,128)(2,1)}), bf16[8,64,256]{2,1,0:T(8,128)(2,1)S(1)}, u32[]{:S(2)}, u32[]{:S(2)}) async-start(bf16[8,64,256]{2,1,0:T(8,128)(2,1)} %bitcast.305), calls=%async_computation.7 | async-start | bytes 524288 | tf_op jit(solution)/shard_map/all_to_all | solution.py:927
  (650 shorter events, 388.6 us)
Async XLA Ops:
  7.2 205.3 %all-gather.3.cloned.1.call-start = ((), (), s32[]{:S(2)}) async-start(), calls=%async_computation.10 | async-start | bytes 8650752 | tf_op jit(solution)/shard_map/all_gather | solution.py:660
  9.1 281.0 %all-gather.5.cloned.1.call-start = ((), (), s32[]{:S(2)}) async-start(), calls=%async_computation.11 | async-start | bytes 17301504 | tf_op jit(solution)/shard_map/all_gather | solution.py:661
  70.4 36.8 %collective-permute-start.4 = (bf16[512,768]{1,0:T(8,128)(2,1)}, bf16[512,768]{1,0:T(8,128)(2,1)}, u32[]{:S(2)}, u32[]{:S(2)}) collective-permute-start(bf16[512,768]{1,0:T(8,128)(2,1)} %collective-permute-done), channel_id=1, source_target_pairs={{0,8},{8,16},{16,24},{1,9},{9,17},{17,25},{2,10},{10,18},{18,26},{... | collective-permute-start | bytes 2359304 | tf_op jit(solution)/shard_map/ppermute | solution.py:674
  75.8 49.1 %collective-permute-start.5 = (bf16[512,768]{1,0:T(8,128)(2,1)}, bf16[512,768]{1,0:T(8,128)(2,1)S(1)}, u32[]{:S(2)}, u32[]{:S(2)}) collective-permute-start(bf16[512,768]{1,0:T(8,128)(2,1)} %collective-permute-done.1), channel_id=1, source_target_pairs={{8,0},{16,8},{24,16},{9,1},{17,9},{25,17},{10,2},{18,10},{26,18},{... | collective-permute-start | bytes 2359304 | tf_op jit(solution)/shard_map/ppermute | solution.py:675
  87.4 37.6 %collective-permute-start.10 = (bf16[128,2048]{1,0:T(8,128)(2,1)}, bf16[128,2048]{1,0:T(8,128)(2,1)}, u32[]{:S(2)}, u32[]{:S(2)}) collective-permute-start(bf16[128,2048]{1,0:T(8,128)(2,1)} %collective-permute-done.3), channel_id=1, source_target_pairs={{0,1},{1,0},{2,3},{3,2},{4,5},{5,4},{6,7},{7,6},{8,9},{9,8},{10,11... | collective-permute-start | bytes 1572872 | tf_op jit(solution)/shard_map/ppermute | solution.py:41
  87.4 37.6 %collective-permute-start.8 = (bf16[128,2048]{1,0:T(8,128)(2,1)S(1)}, bf16[128,2048]{1,0:T(8,128)(2,1)}, u32[]{:S(2)}, u32[]{:S(2)}) collective-permute-start(bf16[128,2048]{1,0:T(8,128)(2,1)S(1)} %copy-done.42), channel_id=1, source_target_pairs={{0,1},{1,0},{2,3},{3,2},{4,5},{5,4},{6,7},{7,6},{8,9},{9,8},{10,11... | collective-permute-start | bytes 1572872 | tf_op jit(solution)/shard_map/ppermute | solution.py:41
  87.9 37.1 %collective-permute-start.9 = (bf16[128,2048]{1,0:T(8,128)(2,1)}, bf16[128,2048]{1,0:T(8,128)(2,1)}, u32[]{:S(2)}, u32[]{:S(2)}) collective-permute-start(bf16[128,2048]{1,0:T(8,128)(2,1)} %collective-permute-done.2), channel_id=1, source_target_pairs={{0,1},{1,0},{2,3},{3,2},{4,5},{5,4},{6,7},{7,6},{8,9},{9,8},{10,11... | collective-permute-start | bytes 1572872 | tf_op jit(solution)/shard_map/ppermute | solution.py:41
  224.8 46.9 %collective-permute-start.23 = (bf16[128,2048]{1,0:T(8,128)(2,1)S(1)}, bf16[128,2048]{1,0:T(8,128)(2,1)}, u32[]{:S(2)}, u32[]{:S(2)}) collective-permute-start(bf16[128,2048]{1,0:T(8,128)(2,1)S(1)} %multiply_convert_fusion.1.refs_0_), channel_id=1, source_target_pairs={{0,1},{1,0},{2,3},{3,2},{4,5},{5,4},{6,7},{7,6},{8,9},{9,8},{10,11... | collective-permute-start | bytes 1572872 | tf_op jit(solution)/shard_map/ppermute | solution.py:41
  226.8 42.8 %collective-permute-start.18 = (bf16[128,2048]{1,0:T(8,128)(2,1)S(1)}, bf16[128,2048]{1,0:T(8,128)(2,1)S(1)}, u32[]{:S(2)}, u32[]{:S(2)}) collective-permute-start(bf16[128,2048]{1,0:T(8,128)(2,1)S(1)} %multiply_convert_fusion.1.refs_0_), channel_id=1, source_target_pairs={{0,2},{1,3},{2,0},{3,1},{4,6},{5,7},{6,4},{7,5},{8,10},{9,11},{10,... | collective-permute-start | bytes 1572872 | tf_op jit(solution)/shard_map/ppermute | solution.py:41
  228.2 40.8 %collective-permute-start.22 = (bf16[128,2048]{1,0:T(8,128)(2,1)S(1)}, bf16[128,2048]{1,0:T(8,128)(2,1)S(1)}, u32[]{:S(2)}, u32[]{:S(2)}) collective-permute-start(bf16[128,2048]{1,0:T(8,128)(2,1)S(1)} %multiply_convert_fusion.1.refs_0_), channel_id=1, source_target_pairs={{16,0},{24,8},{0,16},{8,24},{17,1},{25,9},{1,17},{9,25},{18,2},{26... | collective-permute-start | bytes 1572872 | tf_op jit(solution)/shard_map/ppermute | solution.py:644
  304.9 41.1 %collective-permute-start.30 = (bf16[512,2048]{1,0:T(8,128)(2,1)}, bf16[512,2048]{1,0:T(8,128)(2,1)S(1)}, u32[]{:S(2)}, u32[]{:S(2)}) collective-permute-start(bf16[512,2048]{1,0:T(8,128)(2,1)} %get-tuple-element.169), channel_id=1, source_target_pairs={{0,1},{1,0},{2,3},{3,2},{4,5},{5,4},{6,7},{7,6},{8,9},{9,8},{10,11... | collective-permute-start | bytes 6291464 | tf_op jit(solution)/shard_map/ppermute | solution.py:41
  305.0 41.5 %collective-permute-start.31 = (bf16[512,2048]{1,0:T(8,128)(2,1)}, bf16[512,2048]{1,0:T(8,128)(2,1)}, u32[]{:S(2)}, u32[]{:S(2)}) collective-permute-start(bf16[512,2048]{1,0:T(8,128)(2,1)} %get-tuple-element.171), channel_id=1, source_target_pairs={{0,1},{1,0},{2,3},{3,2},{4,5},{5,4},{6,7},{7,6},{8,9},{9,8},{10,11... | collective-permute-start | bytes 6291464 | tf_op jit(solution)/shard_map/ppermute | solution.py:41
  330.2 34.1 %collective-permute-start.43 = (bf16[128,2048]{1,0:T(8,128)(2,1)}, bf16[128,2048]{1,0:T(8,128)(2,1)}, u32[]{:S(2)}, u32[]{:S(2)}) collective-permute-start(bf16[128,2048]{1,0:T(8,128)(2,1)} %collective-permute-done.37.refs_0_), channel_id=1, source_target_pairs={{0,4},{1,5},{2,6},{3,7},{4,0},{5,1},{6,2},{7,3},{8,12},{9,13},{10,... | collective-permute-start | bytes 1572872 | tf_op jit(solution)/shard_map/ppermute | solution.py:41
  379.9 63.4 %collective-permute-start.45 = (bf16[512,2048]{1,0:T(8,128)(2,1)}, bf16[512,2048]{1,0:T(8,128)(2,1)S(1)}, u32[]{:S(2)}, u32[]{:S(2)}) collective-permute-start(bf16[512,2048]{1,0:T(8,128)(2,1)} %get-tuple-element.182), channel_id=1, source_target_pairs={{0,1},{1,0},{2,3},{3,2},{4,5},{5,4},{6,7},{7,6},{8,9},{9,8},{10,11... | collective-permute-start | bytes 6291464 | tf_op jit(solution)/shard_map/ppermute | solution.py:41
  380.4 64.4 %collective-permute-start.46 = (bf16[512,2048]{1,0:T(8,128)(2,1)}, bf16[512,2048]{1,0:T(8,128)(2,1)}, u32[]{:S(2)}, u32[]{:S(2)}) collective-permute-start(bf16[512,2048]{1,0:T(8,128)(2,1)} %get-tuple-element.184), channel_id=1, source_target_pairs={{0,1},{1,0},{2,3},{3,2},{4,5},{5,4},{6,7},{7,6},{8,9},{9,8},{10,11... | collective-permute-start | bytes 6291464 | tf_op jit(solution)/shard_map/ppermute | solution.py:41
  401.4 41.4 %collective-permute-start.34 = (bf16[256,2048]{1,0:T(8,128)(2,1)}, bf16[256,2048]{1,0:T(8,128)(2,1)S(1)}, u32[]{:S(2)}, u32[]{:S(2)}) collective-permute-start(bf16[256,2048]{1,0:T(8,128)(2,1)} %get-tuple-element.174), channel_id=1, source_target_pairs={{0,2},{1,3},{2,0},{3,1},{4,6},{5,7},{6,4},{7,5},{8,10},{9,11},{10,... | collective-permute-start | bytes 3145736 | tf_op jit(solution)/shard_map/ppermute | solution.py:41
  402.0 40.8 %collective-permute-start.35 = (bf16[256,2048]{1,0:T(8,128)(2,1)}, bf16[256,2048]{1,0:T(8,128)(2,1)}, u32[]{:S(2)}, u32[]{:S(2)}) collective-permute-start(bf16[256,2048]{1,0:T(8,128)(2,1)} %get-tuple-element.175), channel_id=1, source_target_pairs={{0,4},{1,5},{2,6},{3,7},{4,0},{5,1},{6,2},{7,3},{8,12},{9,13},{10,... | collective-permute-start | bytes 3145736 | tf_op jit(solution)/shard_map/ppermute | solution.py:41
  457.4 44.7 %collective-permute-start.67 = (bf16[128,2048]{1,0:T(8,128)(2,1)}, bf16[128,2048]{1,0:T(8,128)(2,1)}, u32[]{:S(2)}, u32[]{:S(2)}) collective-permute-start(bf16[128,2048]{1,0:T(8,128)(2,1)} %collective-permute-done.44.refs_0_), channel_id=1, source_target_pairs={{0,1},{1,0},{2,3},{3,2},{4,5},{5,4},{6,7},{7,6},{8,9},{9,8},{10,11... | collective-permute-start | bytes 1572872 | tf_op jit(solution)/shard_map/ppermute | solution.py:41
  457.4 45.2 %collective-permute-start.69 = (bf16[128,2048]{1,0:T(8,128)(2,1)}, bf16[128,2048]{1,0:T(8,128)(2,1)}, u32[]{:S(2)}, u32[]{:S(2)}) collective-permute-start(bf16[128,2048]{1,0:T(8,128)(2,1)} %collective-permute-done.54.refs_2_), channel_id=1, source_target_pairs={{0,1},{1,0},{2,3},{3,2},{4,5},{5,4},{6,7},{7,6},{8,9},{9,8},{10,11... | collective-permute-start | bytes 1572872 | tf_op jit(solution)/shard_map/ppermute | solution.py:41
  483.3 52.0 %collective-permute-start.60 = (bf16[512,2048]{1,0:T(8,128)(2,1)}, bf16[512,2048]{1,0:T(8,128)(2,1)}, u32[]{:S(2)}, u32[]{:S(2)}) collective-permute-start(bf16[512,2048]{1,0:T(8,128)(2,1)} %get-tuple-element.194), channel_id=1, source_target_pairs={{0,1},{1,0},{2,3},{3,2},{4,5},{5,4},{6,7},{7,6},{8,9},{9,8},{10,11... | collective-permute-start | bytes 6291464 | tf_op jit(solution)/shard_map/ppermute | solution.py:41
  483.4 52.5 %collective-permute-start.61 = (bf16[512,2048]{1,0:T(8,128)(2,1)}, bf16[512,2048]{1,0:T(8,128)(2,1)}, u32[]{:S(2)}, u32[]{:S(2)}) collective-permute-start(bf16[512,2048]{1,0:T(8,128)(2,1)} %get-tuple-element.196), channel_id=1, source_target_pairs={{0,1},{1,0},{2,3},{3,2},{4,5},{5,4},{6,7},{7,6},{8,9},{9,8},{10,11... | collective-permute-start | bytes 6291464 | tf_op jit(solution)/shard_map/ppermute | solution.py:41
  502.6 38.8 %collective-permute-start.49 = (bf16[256,2048]{1,0:T(8,128)(2,1)}, bf16[256,2048]{1,0:T(8,128)(2,1)S(1)}, u32[]{:S(2)}, u32[]{:S(2)}) collective-permute-start(bf16[256,2048]{1,0:T(8,128)(2,1)} %get-tuple-element.187), channel_id=1, source_target_pairs={{0,2},{1,3},{2,0},{3,1},{4,6},{5,7},{6,4},{7,5},{8,10},{9,11},{10,... | collective-permute-start | bytes 3145736 | tf_op jit(solution)/shard_map/ppermute | solution.py:41
  535.3 41.7 %collective-permute-start.71 = (bf16[512,2048]{1,0:T(8,128)(2,1)}, bf16[512,2048]{1,0:T(8,128)(2,1)}, u32[]{:S(2)}, u32[]{:S(2)}) collective-permute-start(bf16[512,2048]{1,0:T(8,128)(2,1)} %get-tuple-element.206), channel_id=1, source_target_pairs={{0,1},{1,0},{2,3},{3,2},{4,5},{5,4},{6,7},{7,6},{8,9},{9,8},{10,11... | collective-permute-start | bytes 6291464 | tf_op jit(solution)/shard_map/ppermute | solution.py:41
  535.4 45.4 %collective-permute-start.72 = (bf16[512,2048]{1,0:T(8,128)(2,1)}, bf16[512,2048]{1,0:T(8,128)(2,1)}, u32[]{:S(2)}, u32[]{:S(2)}) collective-permute-start(bf16[512,2048]{1,0:T(8,128)(2,1)} %get-tuple-element.208), channel_id=1, source_target_pairs={{0,1},{1,0},{2,3},{3,2},{4,5},{5,4},{6,7},{7,6},{8,9},{9,8},{10,11... | collective-permute-start | bytes 6291464 | tf_op jit(solution)/shard_map/ppermute | solution.py:41
  550.1 36.2 %collective-permute-start.51 = (bf16[128,2048]{1,0:T(8,128)(2,1)}, bf16[128,2048]{1,0:T(8,128)(2,1)}, u32[]{:S(2)}, u32[]{:S(2)}) collective-permute-start(bf16[128,2048]{1,0:T(8,128)(2,1)} %get-tuple-element.189), channel_id=1, source_target_pairs={{0,16},{8,24},{16,0},{24,8},{1,17},{9,25},{17,1},{25,9},{2,18},{10... | collective-permute-start | bytes 1572872 | tf_op jit(solution)/shard_map/ppermute | solution.py:647
  576.9 79.5 %collective-permute-start.79 = (bf16[128,2048]{1,0:T(8,128)(2,1)}, bf16[128,2048]{1,0:T(8,128)(2,1)}, u32[]{:S(2)}, u32[]{:S(2)}) collective-permute-start(bf16[128,2048]{1,0:T(8,128)(2,1)} %copy-done.32), channel_id=1, source_target_pairs={{0,16},{8,24},{16,0},{24,8},{1,17},{9,25},{17,1},{25,9},{2,18},{10... | collective-permute-start | bytes 1572872 | tf_op jit(solution)/shard_map/ppermute | solution.py:647
  610.4 44.3 %all-to-all-start.4 = ((f32[32,1,128]{2,1,0:T(1,128)}), f32[32,1,128]{2,1,0:T(1,128)S(1)}, u32[]{:S(2)}, u32[]{:S(2)}) async-start(f32[32,1,128]{2,1,0:T(1,128)} %bitcast.83), calls=%async_computation.4 | async-start | bytes 32768 | tf_op jit(solution)/shard_map/all_to_all | solution.py:865
  615.4 214.8 %reduce-scatter.5.cloned.1.call-start = ((), (), s32[]{:S(2)}) async-start(), calls=%async_computation.13 | async-start | bytes 1310720 | tf_op jit(solution)/shard_map/reduce_scatter | solution.py:891
  615.4 41.1 %collective-permute-start.78 = (bf16[128,2048]{1,0:T(8,128)(2,1)}, bf16[128,2048]{1,0:T(8,128)(2,1)}, u32[]{:S(2)}, u32[]{:S(2)}) collective-permute-start(bf16[128,2048]{1,0:T(8,128)(2,1)} %copy-done.33), channel_id=1, source_target_pairs={{0,8},{8,16},{16,24},{24,0},{1,9},{9,17},{17,25},{25,1},{2,10},{10... | collective-permute-start | bytes 1572872 | tf_op jit(solution)/shard_map/ppermute | solution.py:647
  753.3 32.9 %collective-permute-start.93 = (bf16[512,2048]{1,0:T(8,128)(2,1)}, bf16[512,2048]{1,0:T(8,128)(2,1)}, u32[]{:S(2)}, u32[]{:S(2)}) collective-permute-start(bf16[512,2048]{1,0:T(8,128)(2,1)} %get-tuple-element.303), channel_id=1, source_target_pairs={{0,1},{1,0},{2,3},{3,2},{4,5},{5,4},{6,7},{7,6},{8,9},{9,8},{10,11... | collective-permute-start | bytes 6291464 | tf_op jit(solution)/shard_map/ppermute | solution.py:41
  760.5 78.0 %all-to-all-start.5 = ((bf16[32,64,512]{2,1,0:T(8,128)(2,1)}), bf16[32,64,512]{2,1,0:T(8,128)(2,1)}, u32[]{:S(2)}, u32[]{:S(2)}) async-start(bf16[32,64,512]{2,1,0:T(8,128)(2,1)} %bitcast.286), calls=%async_computation.5 | async-start | bytes 4194304 | tf_op jit(solution)/shard_map/all_to_all | solution.py:919
  764.0 74.5 %reduce-scatter.3.cloned.1.call-start = ((), (), s32[]{:S(2)}) async-start(), calls=%async_computation.12 | async-start | bytes 1310720 | tf_op jit(solution)/shard_map/reduce_scatter | solution.py:917
  (168 other events, 2845.2 us)
Sparse Core Ops, SparseCore 0:
  11.5 100.4 all-gather.2
  114.8 154.0 all-gather.4
  704.1 27.0 reduce-scatter.4
  786.3 39.5 reduce-scatter.2
